TPU v7x, 256 devices: a whole 4x4x8 slice. The times are simulated.
256 devices in a mesh: row: 16 (over y, x_hi, core), col: 16 (over z, x_lo).
Axes of the slice: x: 4 (x_hi: 2, x_lo: 2; x = x_hi * 2 + x_lo), y: 4, z: 8, core: 2. Of those that a mesh axis runs over, the one named last changes fastest.
Arguments:
- pair: bfloat16 [1024, 4096, 128], P('row', 'col'), may hold values from -6 to 6
- single_q: bfloat16 [1024, 384], P('row'), may hold values from -6 to 6
- single_k: bfloat16 [4096, 384], P('col'), may hold values from -6 to 6
- w_query: bfloat16 [384, 192], replicated, may hold values from -0.3125 to 0.3125
- w_key: bfloat16 [384, 192], replicated, may hold values from -0.3125 to 0.3125
- w_value: bfloat16 [384, 192], replicated, may hold values from -0.3125 to 0.3125
- w_qpoint: bfloat16 [384, 288], replicated, may hold values from -0.3125 to 0.3125
- w_kpoint: bfloat16 [384, 288], replicated, may hold values from -0.3125 to 0.3125
- w_vpoint: bfloat16 [384, 288], replicated, may hold values from -0.3125 to 0.3125
- w_bias: bfloat16 [128, 12], replicated, may hold values from -0.5 to 0.5
- w_out: bfloat16 [2112, 384], replicated, may hold values from -0.125 to 0.125
- head_gamma: float32 [12], replicated, may hold values from 0.05 to 1
- chain_bias: float32 [12], replicated, may hold values from -1.5 to 1.5
- rot_q: float32 [9, 1024], P(None, 'row'), may hold values from -1 to 1, as said below
- trans_q: float32 [3, 1024], P(None, 'row'), may hold values from -6 to 26
- rot_k: float32 [9, 4096], P(None, 'col'), may hold values from -1 to 1, as said below
- trans_k: float32 [3, 4096], P(None, 'col'), may hold values from -6 to 6
- chain_q: int32 [1024], P('row'), may hold values from 0 to 4
- chain_k: int32 [4096], P('col'), may hold values from 0 to 4
- key_mask: int32 [4096], P('col'), may hold values 0 or 1
- cotangent: bfloat16 [1024, 384], P('row'), may hold values from -96 to 96
Outputs:
- pair_grad: bfloat16 [1024, 4096, 128], P('row', 'col')
- single_q_grad: bfloat16 [1024, 384], P('row')
- trans_q_grad: float32 [3, 1024], P(None, 'row')
- single_k_grad: bfloat16 [4096, 384], P('col')
- trans_k_grad: float32 [3, 4096], P(None, 'col')
Inputs may be any that keep to these rules, and one draw needn't show every extreme that they name: `rot_q`: each column holds a rotation matrix. `rot_k`: each column holds a rotation matrix.
All inputs are finite; a program needn't handle non-finite values. No bound on the sum of `key_mask` on one device may be relied on, other than what follows from the above.
Results may differ from a plain program's by a relative error of at most 0.02.
The roundings to bfloat16 on the way count: a program that leaves them out, or rounds other values in their place, can miss the bound.
Values sent between devices are 32-bit elements; how exact they have to be, the bound alone decides.
No kernel may reach another device: no remote copies, remote signals or barrier semaphores. Data moves between devices by JAX's collectives and lax.ppermute only.
A program may use at most 128 MiB of HBM per device.

v0:
```python
import math

import jax
import jax.numpy as jnp
from jax import lax
from jax.sharding import PartitionSpec as P

HIGH = lax.Precision.HIGHEST


def joined(value, axis, combine):
    everything = jax.tree.map(lambda part: lax.all_gather(part, axis), value)
    leading = jax.tree.map(lambda part: part[0], everything)

    def turn(k, so_far):
        return combine(so_far, jax.tree.map(lambda part: part[k], everything))

    return lax.fori_loop(1, lax.axis_size(axis), turn, leading)


def points(single, weight, rotation, shift, heads):
    count = single.shape[0]
    local = jnp.dot(single, weight, preferred_element_type=jnp.float32).reshape(count, 3, -1)
    rotm = rotation.reshape(3, 3, count)
    glob = jnp.einsum("abn,nbk->ank", rotm, local, precision=HIGH) + shift[:, :, None]
    return glob.reshape(3, count, heads, -1)


def finish(pairs, pts, sums, coords, rotation, coef, wpoint):
    count = pts.shape[1]
    grad_pts = coef[None, None, :, None] * (pts - coords * sums.T[None, :, :, None])
    local = jnp.einsum(
        "abn,anhp->nbhp", rotation.reshape(3, 3, count), grad_pts, precision=HIGH
    ).reshape(count, -1)
    single = jnp.dot(local, wpoint.astype(jnp.float32).T, precision=HIGH)
    for grad, weight in pairs:
        single = single + jnp.dot(
            grad.reshape(count, -1), weight.astype(jnp.float32).T, precision=HIGH
        )
    return (single, jnp.sum(grad_pts, axis=(2, 3)))


def value_part(vpts, rotation, wvpoint):
    count = vpts.shape[1]
    local = jnp.einsum(
        "abn,anhp->nbhp", rotation.reshape(3, 3, count), vpts, precision=HIGH
    ).reshape(count, -1)
    single = jnp.dot(local, wvpoint.astype(jnp.float32).T, precision=HIGH)
    return (single, jnp.sum(vpts, axis=(2, 3)))


def point_back(opt, rotation, shift, d_ol, d_on):
    count = opt.shape[1]
    rotm = rotation.reshape(3, 3, count)
    oloc = jnp.einsum("abi,aihp->ibhp", rotm, opt - shift[:, :, None, None], precision=HIGH)
    onorm = jnp.sqrt(1.0 + jnp.sum(oloc * oloc, axis=1))
    d_loc = d_ol + (d_on / onorm)[:, None, :, :] * oloc
    return jnp.einsum("abi,ibhp->aihp", rotm, d_loc, precision=HIGH)


def combine_stats(first, second):
    top = jnp.maximum(first[0], second[0])
    return (top, first[1] * jnp.exp(first[0] - top) + second[1] * jnp.exp(second[0] - top))


def body(
    pair,
    single_q,
    single_k,
    w_query,
    w_key,
    w_value,
    w_qpoint,
    w_kpoint,
    w_vpoint,
    w_bias,
    w_out,
    head_gamma,
    chain_bias,
    rot_q,
    trans_q,
    rot_k,
    trans_k,
    chain_q,
    chain_k,
    key_mask,
    cotangent,
):
    rows, keys, depth = pair.shape
    heads = w_bias.shape[1]
    width = w_query.shape[1] // heads
    npoint = w_qpoint.shape[1] // (3 * heads)
    w_logit = math.sqrt(1.0 / 3.0)
    w_point = math.sqrt(2.0 / (9.0 * npoint))
    scale = w_logit / math.sqrt(width)
    query = (
        jnp.dot(single_q, w_query, preferred_element_type=jnp.float32)
        .astype(jnp.bfloat16)
        .reshape(rows, heads, width)
    )
    keyed = (
        jnp.dot(single_k, w_key, preferred_element_type=jnp.float32)
        .astype(jnp.bfloat16)
        .reshape(keys, heads, width)
    )
    valued = (
        jnp.dot(single_k, w_value, preferred_element_type=jnp.float32)
        .astype(jnp.bfloat16)
        .reshape(keys, heads, width)
    )
    gq = points(single_q, w_qpoint, rot_q, trans_q, heads)
    gk = points(single_k, w_kpoint, rot_k, trans_k, heads)
    gv = points(single_k, w_vpoint, rot_k, trans_k, heads)
    coef = w_logit * w_point * head_gamma
    sq_q = jnp.sum(gq * gq, axis=(0, 3))
    sq_k = jnp.sum(gk * gk, axis=(0, 3))
    cross = jnp.einsum("cihp,cjhp->hij", gq, gk, precision=HIGH)
    dist = sq_q.T[:, :, None] + sq_k.T[:, None, :] - 2.0 * cross
    same = (chain_q[:, None] == chain_k[None, :]).astype(jnp.float32)
    logit = (
        w_logit
        * (
            jnp.einsum("ihc,jhc->hij", query, keyed, preferred_element_type=jnp.float32)
            / math.sqrt(width)
            + jnp.einsum("ijz,zh->hij", pair, w_bias, preferred_element_type=jnp.float32)
            + chain_bias[:, None, None] * same[None]
        )
        - 0.5 * coef[:, None, None] * dist
    )
    valid = (key_mask == 1)[None, None, :]
    masked = jnp.where(valid, logit, -1e30)
    local_max = jnp.max(masked, axis=2)
    local_sum = jnp.sum(jnp.where(valid, jnp.exp(masked - local_max[:, :, None]), 0.0), axis=2)
    top, total = joined((local_max, local_sum), "col", combine_stats)
    attn = jnp.where(valid, jnp.exp(masked - top[:, :, None]), 0.0) / total[:, :, None]
    attn_b = attn.astype(jnp.bfloat16)
    attn_f = attn_b.astype(jnp.float32)
    d_cat = lax.dot_general(
        cotangent, w_out, (((1,), (1,)), ((), ())), preferred_element_type=jnp.float32
    ).astype(jnp.bfloat16)
    first = heads * width + heads * depth
    d_os = d_cat[:, : heads * width].reshape(rows, heads, width)
    d_oz = d_cat[:, heads * width : first].reshape(rows, heads, depth)
    d_ol = (
        d_cat[:, first : first + 3 * heads * npoint]
        .astype(jnp.float32)
        .reshape(rows, 3, heads, npoint)
    )
    d_on = d_cat[:, first + 3 * heads * npoint :].astype(jnp.float32).reshape(rows, heads, npoint)
    part_pts = jnp.einsum("hij,ajhp->aihp", attn_f, gv, precision=HIGH)
    d_attn = jnp.einsum(
        "ihc,jhc->hij", d_os, valued, preferred_element_type=jnp.float32
    ) + jnp.einsum("ihz,ijz->hij", d_oz, pair, preferred_element_type=jnp.float32)
    out_s = jnp.einsum("hij,jhc->ihc", attn_b, valued, preferred_element_type=jnp.float32)
    out_z = jnp.einsum("hij,ijz->ihz", attn_b, pair, preferred_element_type=jnp.float32)
    out_s, out_z, opt = lax.psum((out_s, out_z, part_pts), "col")
    d_glob = point_back(opt, rot_q, trans_q, d_ol, d_on)
    d_attn = d_attn + jnp.einsum("aihp,ajhp->hij", d_glob, gv, precision=HIGH)
    delta = (
        jnp.einsum("ihc,ihc->hi", d_os.astype(jnp.float32), out_s, precision=HIGH)
        + jnp.einsum("ihz,ihz->hi", d_oz.astype(jnp.float32), out_z, precision=HIGH)
        + jnp.einsum("aihp,aihp->hi", d_glob, opt, precision=HIGH)
    )
    d_logit = attn * (d_attn - delta[:, :, None])
    d_logit_b = d_logit.astype(jnp.bfloat16)
    pair_grad = (
        w_logit * jnp.einsum("hij,zh->ijz", d_logit_b, w_bias, preferred_element_type=jnp.float32)
        + jnp.einsum("hij,ihz->ijz", attn_b, d_oz, preferred_element_type=jnp.float32)
    ).astype(jnp.bfloat16)
    grad_dq = scale * jnp.einsum(
        "hij,jhc->ihc", d_logit_b, keyed, preferred_element_type=jnp.float32
    )
    q_pts = jnp.einsum("hij,cjhp->cihp", d_logit, gk, precision=HIGH)
    q_sums = jnp.sum(d_logit, axis=2)
    grad_dk = scale * jnp.einsum(
        "hij,ihc->jhc", d_logit_b, query, preferred_element_type=jnp.float32
    )
    grad_dv = jnp.einsum("hij,ihc->jhc", attn_b, d_os, preferred_element_type=jnp.float32)
    k_pts = jnp.einsum("hij,cihp->cjhp", d_logit, gq, precision=HIGH)
    k_sums = jnp.sum(d_logit, axis=1)
    v_pts = jnp.einsum("hij,aihp->ajhp", attn, d_glob, precision=HIGH)
    back_q = jnp.sum(d_glob, axis=(2, 3))
    grad_dq, q_pts, q_sums = lax.psum((grad_dq, q_pts, q_sums), "col")
    grad_q, shift_q = finish([(grad_dq, w_query)], q_pts, q_sums, gq, rot_q, coef, w_qpoint)
    shift_q = shift_q - back_q
    grad_dk, grad_dv, k_pts, k_sums, v_pts = lax.psum(
        (grad_dk, grad_dv, k_pts, k_sums, v_pts), "row"
    )
    grad_k, shift_k = finish(
        [(grad_dk, w_key), (grad_dv, w_value)], k_pts, k_sums, gk, rot_k, coef, w_kpoint
    )
    more_k, more_shift = value_part(v_pts, rot_k, w_vpoint)
    grad_k = grad_k + more_k
    shift_k = shift_k + more_shift
    return (pair_grad, grad_q.astype(jnp.bfloat16), shift_q, grad_k.astype(jnp.bfloat16), shift_k)


def solution(mesh):
    placed = (
        P("row", "col", None),
        P("row", None),
        P("col", None),
        P(),
        P(),
        P(),
        P(),
        P(),
        P(),
        P(),
        P(),
        P(),
        P(),
        P(None, "row"),
        P(None, "row"),
        P(None, "col"),
        P(None, "col"),
        P("row"),
        P("col"),
        P("col"),
        P("row", None),
    )
    return jax.shard_map(
        body,
        mesh=mesh,
        in_specs=placed,
        out_specs=(
            P("row", "col", None),
            P("row", None),
            P(None, "row"),
            P("col", None),
            P(None, "col"),
        ),
        check_vma=False,
    )
```

profile of v0, /device:TPU:1, one launch (start us, length us, event | category | flops | bytes accessed | tf_op | source)
XLA Modules:
  0.0 615.9 jit_solution(7034678303483813803)
XLA Ops:
  21.6 3.9 fusion.13
  25.5 3.9 multiply_reduce_fusion.1
  29.4 1.9 copy.209
  32.8 3.4 fusion.38
  38.4 30.7 %all-gather.3 = f32[16,12,64]{2,1,0:T(8,128)S(1)} all-gather(f32[1,12,64]{2,1,0:T(8,128)S(1)} %bitcast.247), channel_id=3, replica_groups=mesh['row'=16,'col'=16] {'col'}, dimensions={0}, use_global_device_ids=true | all-gather | bytes 52224 | tf_op jit(solution)/shard_map/all_gather | solution.py:12
  69.1 23.5 %all-gather.2 = f32[16,12,64]{2,1,0:T(8,128)S(1)} all-gather(f32[1,12,64]{2,1,0:T(8,128)S(1)} %bitcast.244), channel_id=2, replica_groups=mesh['row'=16,'col'=16] {'col'}, dimensions={0}, use_global_device_ids=true | all-gather | bytes 52224 | tf_op jit(solution)/shard_map/all_gather | solution.py:12
  94.2 3.8 fusion.25
  98.0 2.0 convolution_bitcast_fusion.10
  109.5 50.6 %psum.78 = f32[64,12,16]{0,2,1:T(8,128)S(1)} all-reduce(f32[64,12,16]{0,2,1:T(8,128)S(1)} %convolution_bitcast_fusion.12), channel_id=1, replica_groups=mesh['row'=16,'col'=16] {'col'}, use_global_device_ids=true, to_apply=%region_10.11 | all-reduce | flops 12288 | bytes 98304 | tf_op jit(solution)/shard_map/psum | solution.py:156
  161.6 4.4 fusion.49
  166.0 74.1 %all-reduce.9.cloned.1.call-done = (f32[3,64,12,8]{1,3,0,2:T(8,128)}, f32[64,12,128]{2,1,0:T(8,128)}) async-done(((f32[3,64,12,8]{1,3,0,2:T(8,128)}, f32[64,12,128]{2,1,0:T(8,128)}), (f32[3,64,12,8]{1,3,0,2:T(8,128)}, f32[64,12,128]{2,1,0:T(8,128)})) %all-reduce.9.cloned.1.call-update) | async-done | bytes 466960 | tf_op jit(solution)/shard_map/psum | solution.py:156
  241.6 2.1 copy.211
  243.7 5.2 multiply_reduce_fusion
  251.7 4.5 bitcast_reduce_fusion.2
  257.4 2.8 convolution_bitcast_fusion.7
  260.2 2.8 convolution_bitcast_fusion.3
  268.2 2.8 fusion.43
  273.3 2.4 convolution_bitcast_fusion.8
  276.5 4.8 fusion.28
  281.4 7.3 %add_convert_fusion = bf16[64,256,128]{2,1,0:T(8,128)(2,1)} fusion(f32[64,256,128]{2,1,0:T(8,128)} %fusion.28, bf16[64,12,128]{2,1,0:T(8,128)(2,1)S(1)} %copy-done.5, bf16[12,64,256]{2,1,0:T(8,128)(2,1)S(1)} %fusion.42), kind=kOutput, calls=%fused_computation.5 | convolution fusion | flops 56623104 | bytes 13172736 | tf_op jit(solution)/shard_map/hij,ihz->ijz/dot_general | solution.py:168
  289.0 49.9 %all-reduce = (f32[64,12]{0,1:T(8,128)S(1)}, f32[64,192]{0,1:T(8,128)}) all-reduce(f32[64,12]{0,1:T(8,128)S(1)} %bitcast.249, f32[64,192]{0,1:T(8,128)S(1)} %bitcast.240), channel_id=1, replica_groups=mesh['row'=16,'col'=16] {'col'}, use_global_device_ids=true, to_apply=%region_14.15 | all-reduce | flops 13056 | bytes 104448 | tf_op jit(solution)/shard_map/psum | solution.py:183
  338.9 83.1 %psum.84 = f32[256,12]{0,1:T(8,128)S(1)} all-reduce(f32[256,12]{0,1:T(8,128)S(1)} %bitcast.248), channel_id=1, replica_groups=mesh['row'=16,'col'=16] {'row'}, use_global_device_ids=true, to_apply=%region_20.21 | all-reduce | flops 3072 | bytes 24576 | tf_op jit(solution)/shard_map/psum | solution.py:186
  423.1 1.8 copy.224
  424.9 4.2 convolution_bitcast_fusion.2
  431.8 1.8 fusion.18
  433.6 133.0 %all-reduce.11.cloned.1.call-done = (f32[3,256,12,8]{1,3,0,2:T(8,128)}, f32[3,256,12,8]{1,3,0,2:T(8,128)}, f32[256,192]{0,1:T(8,128)}, f32[256,192]{0,1:T(8,128)}) async-done(((f32[3,256,12,8]{1,3,0,2:T(8,128)}, f32[3,256,12,8]{1,3,0,2:T(8,128)}, f32[256,192]{0,1:T(8,128)}, f32[256,192]{0,1:T(8,128)}), (f32[3,256,12,8]{1,3,0,2:T(8,128)}, f32[3,256,12,8]{1,3,0,2:T(8,128)}, f32[256,192]{0,1:T(8,128)}, ...) | async-done | bytes 983056 | tf_op jit(solution)/shard_map/psum | solution.py:186
  566.6 5.4 copy.234
  572.0 10.5 %convolution_bitcast_fusion = f32[256,3,12,8]{2,1,3,0:T(4,128)} fusion(f32[3,256,12,8]{2,0,3,1:T(4,128)} %copy.234, f32[3,3,256,1]{0,1,3,2:T(4,128)S(1)} %copy-done.2), kind=kOutput, calls=%fused_computation.7 | convolution fusion | flops 2654208 | bytes 599040 | tf_op jit(solution)/shard_map/abn,anhp->nbhp/dot_general | solution.py:45
  582.5 3.3 copy.236
  587.5 4.4 copy.230
  592.0 10.8 %convolution_bitcast_fusion.1 = f32[256,3,12,8]{2,1,3,0:T(4,128)} fusion(f32[3,256,12,8]{2,0,3,1:T(4,128)} %copy.230, f32[3,3,256,1]{0,1,3,2:T(4,128)S(1)} %copy-done.2), kind=kOutput, calls=%fused_computation.8 | convolution fusion | flops 2654208 | bytes 599040 | tf_op jit(solution)/shard_map/abn,anhp->nbhp/dot_general | solution.py:32
  602.8 3.4 copy.232
  (178 shorter events, 53.0 us)
Async XLA Ops:
  7.2 94.5 %copy-start = (bf16[2112,384]{1,0:T(8,128)(2,1)S(1)}, bf16[2112,384]{1,0:T(8,128)(2,1)}, u32[]{:S(2)}) copy-start(bf16[2112,384]{1,0:T(8,128)(2,1)} %param.33) | copy-start | bytes 4866052
  7.2 12.1 %copy-start.7 = (bf16[256,384]{1,0:T(8,128)(2,1)S(1)}, bf16[256,384]{1,0:T(8,128)(2,1)}, u32[]{:S(2)}) copy-start(bf16[256,384]{1,0:T(8,128)(2,1)} %param.25) | copy-start | bytes 589828
  7.2 12.1 %copy-start.12 = (bf16[384,288]{0,1:T(8,128)(2,1)S(1)}, bf16[384,288]{0,1:T(8,128)(2,1)}, u32[]{:S(2)}) copy-start(bf16[384,288]{0,1:T(8,128)(2,1)} %param.31) | copy-start | bytes 663556
  7.2 232.8 %all-reduce.9.cloned.1.call-start = ((), (), s32[]{:S(2)}) async-start(), calls=%async_computation.1 | async-start | bytes 1343488 | tf_op jit(solution)/shard_map/psum | solution.py:156
  11.3 18.2 %copy-start.27 = (f32[3,3,256]{2,1,0:T(4,128)}, f32[3,3,256]{2,1,0:T(4,128)S(1)}, u32[]{:S(2)}) copy-start(f32[3,3,256]{2,1,0:T(4,128)S(1)} %reshape.144) | copy-start | bytes 27652
  12.5 24.6 %copy-start.19 = (bf16[64,192]{0,1:T(8,128)(2,1)}, bf16[64,192]{0,1:T(8,128)(2,1)S(1)}, u32[]{:S(2)}) copy-start(bf16[64,192]{0,1:T(8,128)(2,1)S(1)} %copy.192) | copy-start | bytes 73732
  17.7 19.5 %copy-start.10 = (bf16[256,192]{0,1:T(8,128)(2,1)}, bf16[256,192]{0,1:T(8,128)(2,1)S(1)}, u32[]{:S(2)}) copy-start(bf16[256,192]{0,1:T(8,128)(2,1)S(1)} %convolution_convert_fusion.2) | copy-start | bytes 294916
  19.3 13.4 %copy-start.38 = (s32[256]{0:T(256)S(1)}, s32[256]{0:T(256)}, u32[]{:S(2)}) copy-start(s32[256]{0:T(256)} %param.41) | copy-start | bytes 3076
  19.3 13.4 %copy-start.39 = (s32[64]{0:T(128)S(1)}, s32[64]{0:T(128)}, u32[]{:S(2)}) copy-start(s32[64]{0:T(128)} %param.40) | copy-start | bytes 772
  19.3 13.5 %copy-start.33 = (bf16[128,12]{0,1:T(8,128)(2,1)S(1)}, bf16[128,12]{0,1:T(8,128)(2,1)}, u32[]{:S(2)}) copy-start(bf16[128,12]{0,1:T(8,128)(2,1)} %param.32) | copy-start | bytes 9220
  29.4 7.7 %copy-start.36 = (pred[256]{0:T(512)(128)(4,1)S(1)}, pred[256]{0:T(512)(128)(4,1)}, u32[]{:S(2)}) copy-start(pred[256]{0:T(512)(128)(4,1)} %broadcast_compare_fusion) | copy-start | bytes 772
  29.4 7.7 %copy-start.40 = (f32[12]{0:T(128)S(1)}, f32[12]{0:T(128)}, u32[]{:S(2)}) copy-start(f32[12]{0:T(128)} %param.35) | copy-start | bytes 148
  38.0 62.0 %copy-start.1 = (f32[12,64,256]{2,1,0:T(8,128)}, f32[12,64,256]{2,1,0:T(8,128)S(1)}, u32[]{:S(2)}) copy-start(f32[12,64,256]{2,1,0:T(8,128)S(1)} %get-tuple-element.179) | copy-start | bytes 2359300
  92.5 7.6 %copy-start.30 = (f32[3,3,64]{2,1,0:T(4,128)S(1)}, f32[3,3,64]{2,1,0:T(4,128)}, u32[]{:S(2)}) copy-start(f32[3,3,64]{2,1,0:T(4,128)} %copy-done.29) | copy-start | bytes 6916
  93.2 9.1 %copy-start.21 = (f32[12,64]{1,0:T(8,128)}, f32[12,64]{1,0:T(8,128)S(1)}, u32[]{:S(2)}) copy-start(f32[12,64]{1,0:T(8,128)S(1)} %get-tuple-element.139) | copy-start | bytes 9220
  93.2 9.1 %copy-start.22 = (f32[12,64]{1,0:T(8,128)}, f32[12,64]{1,0:T(8,128)S(1)}, u32[]{:S(2)}) copy-start(f32[12,64]{1,0:T(8,128)S(1)} %get-tuple-element.138) | copy-start | bytes 9220
  93.2 8.5 %copy-start.32 = (bf16[64,384]{1,0:T(8,128)(2,1)S(1)}, bf16[64,384]{1,0:T(8,128)(2,1)}, u32[]{:S(2)}) copy-start(bf16[64,384]{1,0:T(8,128)(2,1)} %param.43) | copy-start | bytes 147460
  94.2 12.2 %copy-start.28 = (f32[3,3,256]{2,1,0:T(4,128)S(1)}, f32[3,3,256]{2,1,0:T(4,128)}, u32[]{:S(2)}) copy-start(f32[3,3,256]{2,1,0:T(4,128)} %copy-done.27) | copy-start | bytes 27652
  100.0 322.0 %all-reduce.7.cloned.1.call-start = ((), (), s32[]{:S(2)}) async-start(), calls=%async_computation | async-start | bytes 294912 | tf_op jit(solution)/shard_map/psum | solution.py:183
  104.4 61.6 %copy-start.23 = (bf16[256,192]{0,1:T(8,128)(2,1)}, bf16[256,192]{0,1:T(8,128)(2,1)S(1)}, u32[]{:S(2)}) copy-start(bf16[256,192]{0,1:T(8,128)(2,1)S(1)} %convolution_convert_fusion.1) | copy-start | bytes 294916
  106.4 59.6 %copy-start.3 = (bf16[64,12,128]{2,1,0:T(8,128)(2,1)}, bf16[64,12,128]{2,1,0:T(8,128)(2,1)S(1)}, u32[]{:S(2)}) copy-start(bf16[64,12,128]{2,1,0:T(8,128)(2,1)S(1)} %reshape.149) | copy-start | bytes 589828
  107.5 132.6 %copy-start.35 = (f32[3,64]{1,0:T(4,128)S(1)}, f32[3,64]{1,0:T(4,128)}, u32[]{:S(2)}) copy-start(f32[3,64]{1,0:T(4,128)} %param.37) | copy-start | bytes 2308
  266.5 9.2 %copy-start.20 = (bf16[64,192]{0,1:T(8,128)(2,1)S(1)}, bf16[64,192]{0,1:T(8,128)(2,1)}, u32[]{:S(2)}) copy-start(bf16[64,192]{0,1:T(8,128)(2,1)} %copy-done.19) | copy-start | bytes 73732
  266.5 10.1 %copy-start.34 = (bf16[128,12]{0,1:T(8,128)(2,1)S(1)}, bf16[128,12]{0,1:T(8,128)(2,1)}, u32[]{:S(2)}) copy-start(bf16[128,12]{0,1:T(8,128)(2,1)} %param.32) | copy-start | bytes 9220
  281.3 7.4 %copy-start.11 = (bf16[256,192]{0,1:T(8,128)(2,1)S(1)}, bf16[256,192]{0,1:T(8,128)(2,1)}, u32[]{:S(2)}) copy-start(bf16[256,192]{0,1:T(8,128)(2,1)} %copy-done.10) | copy-start | bytes 294916
  281.3 7.6 %copy-start.26 = (f32[3,64]{0,1:T(8,128)S(1)}, f32[3,64]{0,1:T(8,128)}, u32[]{:S(2)}) copy-start(f32[3,64]{0,1:T(8,128)} %get-tuple-element.183) | copy-start | bytes 2308
  281.3 140.7 %copy-start.37 = (f32[12]{0:T(128)S(1)}, f32[12]{0:T(128)}, u32[]{:S(2)}) copy-start(f32[12]{0:T(128)} %get-tuple-element.172) | copy-start | bytes 148
  281.3 143.6 %copy-start.9 = (f32[3,3,64,1]{0,1,3,2:T(4,128)S(1)}, f32[3,3,64,1]{0,1,3,2:T(4,128)}, u32[]{:S(2)}) copy-start(f32[3,3,64,1]{0,1,3,2:T(4,128)} %copy.238) | copy-start | bytes 6916
  281.4 285.2 %all-reduce.11.cloned.1.call-start = ((), (), s32[]{:S(2)}) async-start(), calls=%async_computation.2 | async-start | bytes 1966080 | tf_op jit(solution)/shard_map/psum | solution.py:186
  288.7 142.7 %copy-start.15 = (bf16[384,288]{0,1:T(8,128)(2,1)S(1)}, bf16[384,288]{0,1:T(8,128)(2,1)}, u32[]{:S(2)}) copy-start(bf16[384,288]{0,1:T(8,128)(2,1)} %param.29) | copy-start | bytes 663556
  338.9 92.9 %copy-start.31 = (f32[64,192]{0,1:T(8,128)S(1)}, f32[64,192]{0,1:T(8,128)}, u32[]{:S(2)}) copy-start(f32[64,192]{0,1:T(8,128)} %get-tuple-element.158) | copy-start | bytes 147460
  424.9 147.1 %copy-start.2 = (f32[3,3,256,1]{0,1,3,2:T(4,128)S(1)}, f32[3,3,256,1]{0,1,3,2:T(4,128)}, u32[]{:S(2)}) copy-start(f32[3,3,256,1]{0,1,3,2:T(4,128)} %copy.262) | copy-start | bytes 27652
  (12 other events, 54.1 us)
Sparse Core Ops, SparseCore 0:
  100.2 139.8 all-reduce.8
  281.4 130.8 all-reduce.6
  422.1 144.3 all-reduce.10
where the time goes:
time: 628 us; the launch traced here: 616 us
  blocking collectives  238 us (38%)
  waiting for transfers between devices  207 us (33%)
  matrix products  97 us (15%)
  local copies, waits for them, and re-layouts  44.6 us (7%)
  between operations  14.9 us (2%)
  other arithmetic  14 us (2%)
    psum x1, waiting for transfers between devices, body(): lax.psum((grad_dk, grad_dv, k_pts, k_sums, v_pts), 'row')  133 us
    psum x1, blocking collectives, body(): lax.psum((grad_dk, grad_dv, k_pts, k_sums, v_pts), 'row')  83.1 us
    psum x1, waiting for transfers between devices, body(): out_s, out_z, opt = lax.psum((out_s, out_z, part_pts), 'col')  74.1 us
    all_gather x2, blocking collectives, joined(): everything = jax.tree.map(lambda part: lax.all_gather(part, axis), value)  54.2 us
    psum x1, blocking collectives, body(): out_s, out_z, opt = lax.psum((out_s, out_z, part_pts), 'col')  50.6 us
    psum x1, blocking collectives, body(): grad_dq, q_pts, q_sums = lax.psum((grad_dq, q_pts, q_sums), 'col')  49.9 us
    dot_general x2, matrix products, finish(): jnp.einsum('abn,anhp->nbhp', rotation.reshape(3, 3, count), grad_pts, pre...  15 us
  transfers between devices with their start and end apart: 3, of which 2 were waited for; matrix products, arithmetic and copies ran while one was open for 6% of the time, Pallas kernels for 0%

commit v1 on v0

v1 whole, which is shorter than its diff:
```python
import functools
import math

import jax
import jax.numpy as jnp
from jax import lax
from jax.experimental import pallas as pl
from jax.experimental.pallas import tpu as pltpu
from jax.sharding import PartitionSpec as P

HIGH = lax.Precision.HIGHEST
F32 = jnp.float32
BF = jnp.bfloat16
HP = 16
LANE = 128
NEG = -1e30
LIMIT = 56 * 1024 * 1024


def nn(a, b, precision=None):
    return lax.dot_general(
        a, b, (((1,), (0,)), ((), ())), preferred_element_type=F32, precision=precision
    )


def nt(a, b, precision=None):
    return lax.dot_general(
        a, b, (((1,), (1,)), ((), ())), preferred_element_type=F32, precision=precision
    )


def tn(a, b, precision=None):
    return lax.dot_general(
        a, b, (((0,), (0,)), ((), ())), preferred_element_type=F32, precision=precision
    )


def split(x):
    hi = x.astype(BF)
    return hi, (x - hi.astype(F32)).astype(BF)


def iota(shape, axis):
    return lax.broadcasted_iota(jnp.int32, shape, axis)


def head_mask(heads, npoint, width):
    lane = iota((HP, width), 1) % LANE
    row = iota((HP, width), 0)
    return (lane // npoint == row) & (lane < heads * npoint)


def channel_mask(heads, channels):
    lane = iota((HP, heads * channels), 1)
    return lane // channels == iota((HP, heads * channels), 0)


def spread(x, mask):
    n, w = x.shape
    wide = jnp.broadcast_to(x[:, None, :], (n, HP, w))
    return jnp.where(mask[None], wide, jnp.zeros((), x.dtype)).reshape(n * HP, w)


def gather_heads(x, mask):
    w = x.shape[1]
    full = jnp.where(mask[None], x.reshape(-1, HP, w), 0.0)
    return jnp.sum(full, axis=1)


def to_lanes(col, offset=0):
    n = col.shape[0] // HP
    mask = iota((HP, LANE), 1) == iota((HP, LANE), 0) + offset
    wide = jnp.broadcast_to(col, (n * HP, LANE)).reshape(n, HP, LANE)
    return jnp.sum(jnp.where(mask[None], wide, 0.0), axis=1)


def to_col(x, offset=0):
    n = x.shape[0]
    mask = iota((HP, LANE), 1) == iota((HP, LANE), 0) + offset
    wide = jnp.broadcast_to(x[:, None, :], (n, HP, LANE))
    return jnp.sum(jnp.where(mask[None], wide, 0.0), axis=2, keepdims=True).reshape(n * HP, 1)


def pad_lanes(x, width=LANE):
    n, w = x.shape
    return jnp.concatenate([x, jnp.zeros((n, width - w), x.dtype)], axis=1)


def rotate_points(local, cols, hp):
    parts = [local[:, b * hp : (b + 1) * hp] for b in range(3)]
    out = []
    for a in range(3):
        g = cols[:, 9 + a : 10 + a]
        g = g + sum(cols[:, 3 * a + b : 3 * a + b + 1] * parts[b] for b in range(3))
        out.append(pad_lanes(g))
    return jnp.concatenate(out, axis=1)


def back_rotate(x, cols):
    parts = [x[:, a * LANE : (a + 1) * LANE] for a in range(3)]
    return [sum(cols[:, 3 * a + b : 3 * a + b + 1] * parts[a] for a in range(3)) for b in range(3)]


def logits_kernel(
    heads,
    channels,
    npoint,
    pair_hbm,
    sq_ref,
    sk_ref,
    wq_ref,
    wk_ref,
    wv_ref,
    wqp_ref,
    wkp_ref,
    wvp_ref,
    wb_ref,
    wout_ref,
    gamma_ref,
    chainb_ref,
    rotq_ref,
    trq_ref,
    rotk_ref,
    trk_ref,
    cq_ref,
    ck_ref,
    km_ref,
    cot_ref,
    masked_ref,
    base_ref,
    stats_ref,
    query_ref,
    key_ref,
    value_ref,
    gq_ref,
    gk_ref,
    gv_ref,
    dos_ref,
    dpt_ref,
    rhs_ref,
    qcol_ref,
    kcol_ref,
    pair_ref,
    lhs_ref,
    tq_ref,
    tk_ref,
    sems,
):
    rows, keys, depth = pair_hbm.shape
    hp = heads * npoint
    nchunk = sems.shape[0]
    step = rows // nchunk
    copies = [
        pltpu.make_async_copy(
            pair_hbm.at[pl.ds(c * step, step)], pair_ref.at[pl.ds(c * step, step)], sems.at[c]
        )
        for c in range(nchunk)
    ]
    for copy in copies:
        copy.start()

    w_logit = math.sqrt(1.0 / 3.0)
    w_point = math.sqrt(2.0 / (9.0 * npoint))
    tq_ref[...] = jnp.zeros_like(tq_ref)
    tq_ref[0:9, 0:rows] = rotq_ref[...]
    tq_ref[9:12, 0:rows] = trq_ref[...]
    tq_ref[12:13, 0:rows] = cq_ref[...].astype(F32)
    tq_ref[13:14, 0:heads] = gamma_ref[...]
    tq_ref[14:15, 0:heads] = chainb_ref[...]
    qcols_all = tq_ref[...].T
    qcols = qcols_all[:rows]
    head_cols = qcols_all[:HP]
    qcol_ref[...] = qcols_all
    tk_ref[...] = jnp.zeros_like(tk_ref)
    tk_ref[0:9, :] = rotk_ref[...]
    tk_ref[9:12, :] = trk_ref[...]
    kcols = tk_ref[...].T
    kcol_ref[...] = kcols

    sq = sq_ref[...]
    sk = sk_ref[...]
    cot = cot_ref[...]
    query = nt(sq, wq_ref[...]).astype(BF)
    key = nt(sk, wk_ref[...]).astype(BF)
    query_ref[...] = query
    key_ref[...] = key
    value_ref[...] = nt(sk, wv_ref[...]).astype(BF)
    gq = rotate_points(nt(sq, wqp_ref[...]), qcols, hp)
    gk = rotate_points(nt(sk, wkp_ref[...]), kcols, hp)
    gq_ref[...] = gq
    gk_ref[...] = gk
    gv_ref[...] = rotate_points(nt(sk, wvp_ref[...]), kcols, hp)

    nos = heads * channels
    first = nos + heads * depth
    dos_ref[...] = nt(cot, wout_ref[0:nos, :]).astype(BF)
    for b in range(4):
        d = nt(cot, wout_ref[first + b * hp : first + (b + 1) * hp, :]).astype(BF).astype(F32)
        dpt_ref[:, b * LANE : (b + 1) * LANE] = pad_lanes(d)
    doz = nt(cot, wout_ref[nos:first, :]).astype(BF).astype(F32)
    wbt = jnp.concatenate(
        [wb_ref[...].astype(F32), jnp.zeros((HP - heads, depth), F32)], axis=0
    )
    wb_wide = jnp.broadcast_to(wbt[None], (rows, HP, depth))
    lhs_ref[...] = jnp.zeros_like(lhs_ref)
    for h in range(heads):
        lhs_ref[pl.ds(HP + h, rows, stride=2 * HP), :] = doz[:, h * depth : (h + 1) * depth]
    lhs3 = lhs_ref[...].reshape(rows, 2 * HP, depth)
    doz_b = lhs3[:, HP:, :]
    whi, wlo = split(w_logit * wb_wide)
    rhs_ref[:, 0:HP, :] = whi
    rhs_ref[:, HP : 2 * HP, :] = wlo
    rhs_ref[:, 2 * HP : 3 * HP, :] = doz_b.astype(BF)
    lhs_ref[...] = jnp.concatenate([wb_wide, doz_b], axis=1).reshape(rows * 2 * HP, depth)

    for c in range(nchunk):
        copies[c].wait()

        def one(i, carry):
            r = pl.multiple_of(i * 2 * HP, 2 * HP)
            g = nt(lhs_ref[pl.ds(r, 2 * HP), :].astype(BF), pair_ref[i])
            r = pl.multiple_of(i * HP, HP)
            masked_ref[pl.ds(r, HP), :] = g[:HP]
            base_ref[pl.ds(r, HP), :] = g[HP:]
            return carry

        lax.fori_loop(c * step, (c + 1) * step, one, 0, unroll=8)

    pmask = head_mask(heads, npoint, 3 * LANE)
    cmask = channel_mask(heads, channels)
    gqm = spread(gq, pmask)
    cross = nt(gqm, gk, HIGH)
    sqq = jnp.sum(gqm * gqm, axis=1, keepdims=True)
    sqk = nt(pmask.astype(F32), gk * gk, HIGH)
    qk = nt(spread(query.astype(F32), cmask).astype(BF), key)
    coef = (w_logit * w_point) * head_cols[:, 13:14]
    same = (qcols[:, 12:13] == ck_ref[...].astype(F32)).astype(F32)
    shape = (rows, HP, keys)
    dist = (sqq.reshape(rows, HP, 1) + sqk[None]) - 2.0 * cross.reshape(shape)
    inner = (
        qk.reshape(shape) * (1.0 / math.sqrt(channels))
        + masked_ref[...].reshape(shape)
        + head_cols[:, 14:15][None] * jnp.broadcast_to(same[:, None, :], shape)
    )
    logit = w_logit * inner - (0.5 * coef)[None] * dist
    valid = (km_ref[...] == 1)[None]
    masked = jnp.where(valid, logit, NEG)
    top = jnp.max(masked, axis=2, keepdims=True)
    total = jnp.sum(jnp.where(valid, jnp.exp(masked - top), 0.0), axis=2, keepdims=True)
    masked_ref[...] = masked.reshape(rows * HP, keys)
    packed = to_lanes(top.reshape(rows * HP, 1)) + to_lanes(total.reshape(rows * HP, 1), HP)
    stats_ref[...] = packed.T[: 2 * HP]
    dosm = spread(dos_ref[...].astype(F32), cmask).astype(BF)
    base_ref[...] += nt(dosm, value_ref[...])


def attend_kernel(heads, npoint, masked_ref, base_ref, km_ref, stats_ref, gv_ref, attn_ref, out_ref):
    rows = stats_ref.shape[1]
    keys = masked_ref.shape[1]
    stats = jnp.concatenate(
        [stats_ref[...], jnp.zeros((LANE - stats_ref.shape[0], rows), F32)], axis=0
    ).T
    top = to_col(stats)
    total = to_col(stats, HP)
    valid = km_ref[...] == 1
    attn = jnp.where(valid, jnp.exp(masked_ref[...] - top), 0.0) / total
    attn_ref[...] = attn
    attn_b = attn.astype(BF)
    attn_f = attn_b.astype(F32)
    ghi, glo = split(gv_ref[...])
    opt = nn(attn_b, ghi) + nn(attn_b, glo)
    pmask = head_mask(heads, npoint, 3 * LANE)
    delta = jnp.sum(attn_f * base_ref[...], axis=1, keepdims=True)
    out_ref[...] = gather_heads(opt, pmask)
    out_ref[:, 0:LANE] += to_lanes(delta, heads * npoint)


def frames_of(heads, npoint, qcol_ref, rows):
    pmask = head_mask(heads, npoint, 3 * LANE)
    qall = qcol_ref[...]
    w_logit = math.sqrt(1.0 / 3.0)
    w_point = math.sqrt(2.0 / (9.0 * npoint))
    coef = (w_logit * w_point) * qall[:HP, 13:14]
    coef_lane = jnp.sum(jnp.where(pmask, coef, 0.0), axis=0, keepdims=True)
    return pmask, qall[:rows], coef_lane


def project(parts, width):
    single = jnp.zeros((parts[0][0].shape[0], width), F32)
    for part, weight in parts:
        phi, plo = split(part)
        single = single + (nn(phi, weight) + nn(plo, weight))
    return single


def component_sums(x):
    n = x.shape[0]
    cols = [jnp.sum(x[:, a * LANE : (a + 1) * LANE], axis=1, keepdims=True) for a in range(3)]
    return jnp.concatenate(cols + [jnp.zeros((n, LANE - 3), F32)], axis=1).T


def query_kernel(
    heads,
    channels,
    npoint,
    place_ref,
    attn_ref,
    base_ref,
    psum0_ref,
    psum1_ref,
    psum2_ref,
    psum3_ref,
    key_ref,
    gq_ref,
    gk_ref,
    gv_ref,
    dpt_ref,
    qcol_ref,
    wq_ref,
    wqp_ref,
    qout_ref,
    both_ref,
    dlo_ref,
    alo_ref,
    dglob_ref,
):
    rows, keys = gq_ref.shape[0], gk_ref.shape[0]
    hp = heads * npoint
    scale = math.sqrt(1.0 / 3.0) / math.sqrt(channels)
    cmask = channel_mask(heads, channels)
    pmask, qcols, coef_lane = frames_of(heads, npoint, qcol_ref, rows)
    inside = iota((1, LANE), 1) < hp

    psum = (psum0_ref[...] + psum1_ref[...]) + (psum2_ref[...] + psum3_ref[...])
    delta0 = to_col(psum[:, :LANE], hp)
    opt = [jnp.where(inside, psum[:, a * LANE : (a + 1) * LANE], 0.0) for a in range(3)]
    moved = [jnp.where(inside, opt[a] - qcols[:, 9 + a : 10 + a], 0.0) for a in range(3)]
    oloc = back_rotate(jnp.concatenate(moved, axis=1), qcols)
    onorm = jnp.sqrt(1.0 + (oloc[0] * oloc[0] + oloc[1] * oloc[1] + oloc[2] * oloc[2]))
    ratio = dpt_ref[:, 3 * LANE : 4 * LANE] / onorm
    dloc = [dpt_ref[:, b * LANE : (b + 1) * LANE] + ratio * oloc[b] for b in range(3)]
    dglob = jnp.concatenate(
        [
            sum(qcols[:, 3 * a + b : 3 * a + b + 1] * dloc[b] for b in range(3))
            for a in range(3)
        ],
        axis=1,
    )
    dglob_ref[...] = dglob
    dghi, dglo = split(spread(dglob, pmask))
    opt_row = jnp.concatenate(opt, axis=1)
    delta = delta0 + jnp.sum(spread(opt_row * dglob, pmask), axis=1, keepdims=True)
    gvhi, gvlo = split(gv_ref[...])
    dattn = base_ref[...] + nt(dghi, gvhi) + (nt(dghi, gvlo) + nt(dglo, gvhi))
    attn = attn_ref[...]
    dlogit = attn * (dattn - delta)
    dhi, dlo = split(dlogit)
    ahi, alo = split(attn)
    both_ref[:, 0:HP, :] = dhi.reshape(rows, HP, keys)
    both_ref[:, HP : 2 * HP, :] = ahi.reshape(rows, HP, keys)
    dlo_ref[...] = dlo
    alo_ref[...] = alo

    gkhi, gklo = split(gk_ref[...])
    dq = scale * gather_heads(nn(dhi, key_ref[...]), cmask)
    qpts = gather_heads(nn(dhi, gkhi) + (nn(dhi, gklo) + nn(dlo, gkhi)), pmask)
    qsum = jnp.sum(dlogit, axis=1, keepdims=True)
    qsum_lane = gather_heads(jnp.broadcast_to(qsum, (rows * HP, 3 * LANE)), pmask)
    dgq = coef_lane * (qpts - gq_ref[...] * qsum_lane)
    mq = back_rotate(dgq, qcols)
    width = qout_ref.shape[1]
    qout_ref[0:rows, :] = project(
        [(dq, wq_ref[...])]
        + [(mq[b][:, :hp], wqp_ref[b * hp : (b + 1) * hp, :]) for b in range(3)],
        width,
    )
    shift = jnp.where(place_ref[0] == 0, dgq - dglob, dgq)
    qout_ref[rows:, :] = jnp.zeros((qout_ref.shape[0] - rows, width), F32)
    qout_ref[rows : rows + 8, 0:rows] = component_sums(shift)[:8, :rows]


def key_kernel(
    heads,
    channels,
    npoint,
    place_ref,
    both_ref,
    dlo_ref,
    alo_ref,
    dglob_ref,
    query_ref,
    gq_ref,
    gk_ref,
    dos_ref,
    qcol_ref,
    kcol_ref,
    wk_ref,
    wv_ref,
    wkp_ref,
    wvp_ref,
    mine_ref,
    other_ref,
):
    rows, keys = gq_ref.shape[0], gk_ref.shape[0]
    hp = heads * npoint
    scale = math.sqrt(1.0 / 3.0) / math.sqrt(channels)
    cmask = channel_mask(heads, channels)
    pmask, qcols, coef_lane = frames_of(heads, npoint, qcol_ref, rows)
    kcols = kcol_ref[...]
    dhi = both_ref[:, 0:HP, :].reshape(rows * HP, keys)
    ahi = both_ref[:, HP : 2 * HP, :].reshape(rows * HP, keys)
    dlo, alo = dlo_ref[...], alo_ref[...]
    dghi, dglo = split(spread(dglob_ref[...], pmask))
    gqhi, gqlo = split(spread(gq_ref[...], pmask))
    ones = jnp.broadcast_to(pmask[None], (rows, HP, 3 * LANE)).astype(F32).reshape(
        rows * HP, 3 * LANE
    )
    ones = ones.astype(BF)
    qm = spread(query_ref[...].astype(F32), cmask).astype(BF)
    dosm = spread(dos_ref[...].astype(F32), cmask).astype(BF)
    dk = scale * tn(dhi, qm)
    dv = tn(ahi, dosm)
    kpts = tn(dhi, gqhi) + (tn(dhi, gqlo) + tn(dlo, gqhi))
    ksum = tn(dhi, ones) + tn(dlo, ones)
    vpts = tn(ahi, dghi) + (tn(ahi, dglo) + tn(alo, dghi))
    dgk = coef_lane * (kpts - gk_ref[...] * ksum)
    mk = back_rotate(dgk, kcols)
    mv = back_rotate(vpts, kcols)
    width = mine_ref.shape[1]
    single = project(
        [(dk, wk_ref[...]), (dv, wv_ref[...])]
        + [(mk[b][:, :hp], wkp_ref[b * hp : (b + 1) * hp, :]) for b in range(3)]
        + [(mv[b][:, :hp], wvp_ref[b * hp : (b + 1) * hp, :]) for b in range(3)],
        width,
    )
    cols = component_sums(dgk + vpts)
    piece = keys // 8
    core, quarter = place_ref[1], place_ref[2]

    def put(ref, half):
        for n in range(4):
            k = half * 4 + n
            r = pl.multiple_of((n ^ quarter) * (piece + 8), 8)
            ref[pl.ds(r, piece), :] = single[k * piece : (k + 1) * piece]
            r = pl.multiple_of((n ^ quarter) * (piece + 8) + piece, 8)
            ref[pl.ds(r, 8), :] = jnp.concatenate(
                [cols[:8, k * piece : (k + 1) * piece], jnp.zeros((8, width - piece), F32)], axis=1
            )

    @pl.when(core == 0)
    def _():
        put(mine_ref, 0)
        put(other_ref, 1)

    @pl.when(core != 0)
    def _():
        put(mine_ref, 1)
        put(other_ref, 0)


def finish_kernel(
    place_ref,
    q0_ref,
    q1_ref,
    q2_ref,
    q3_ref,
    mine_ref,
    other_ref,
    gradq_ref,
    shiftq_ref,
    gradk_ref,
    shiftk_ref,
    shift_ref,
):
    rows = gradq_ref.shape[0]
    keys = gradk_ref.shape[0]
    piece = keys // 8
    total = (q0_ref[...] + q1_ref[...]) + (q2_ref[...] + q3_ref[...])
    gradq_ref[...] = total[:rows].astype(BF)
    shiftq_ref[...] = total[rows : rows + 3, :rows]
    core, quarter = place_ref[1], place_ref[2]

    def put(ref, half):
        parts = []
        for n in range(4):
            k = half * 4 + n
            r = pl.multiple_of((n ^ quarter) * (piece + 8), 8)
            gradk_ref[k * piece : (k + 1) * piece, :] = ref[pl.ds(r, piece), :].astype(BF)
            r = pl.multiple_of((n ^ quarter) * (piece + 8) + piece, 8)
            parts.append(ref[pl.ds(r, 8), 0:piece])
        shift_ref[:, half * 4 * piece : (half + 1) * 4 * piece] = jnp.concatenate(parts, axis=1)

    @pl.when(core == 0)
    def _():
        put(mine_ref, 0)
        put(other_ref, 1)

    @pl.when(core != 0)
    def _():
        put(mine_ref, 1)
        put(other_ref, 0)

    shiftk_ref[...] = shift_ref[0:3, :]


def pair_kernel(both_ref, rhs_ref, out_ref):
    rows = both_ref.shape[0]

    def one(i, carry):
        both = both_ref[i]
        left = jnp.concatenate([both[:HP], both[:HP], both[HP:]], axis=0)
        out_ref[i] = tn(left, rhs_ref[i]).astype(BF)
        return carry

    lax.fori_loop(0, rows, one, 0, unroll=True)


def permuted(x, axis, flip):
    size = lax.axis_size(axis)
    return lax.ppermute(x, axis, [(i, i ^ flip) for i in range(size)])


def around(x, hops):
    size = lax.axis_size("col")
    ring = size // 2
    sign = -1 if hops == 2 else 1
    moves = []
    for i in range(size):
        z, low = i // 2, i % 2
        source = (z + (hops if z % 2 else -hops) * sign) % ring
        moves.append((source * 2 + low, i))
    return lax.ppermute(x, "col", moves)


def merged(parts):
    top = functools.reduce(jnp.maximum, [p[:HP] for p in parts])
    total = sum(p[HP:] * jnp.exp(p[:HP] - top) for p in parts)
    return jnp.concatenate([top, total], axis=0)


def body(
    pair,
    single_q,
    single_k,
    w_query,
    w_key,
    w_value,
    w_qpoint,
    w_kpoint,
    w_vpoint,
    w_bias,
    w_out,
    head_gamma,
    chain_bias,
    rot_q,
    trans_q,
    rot_k,
    trans_k,
    chain_q,
    chain_k,
    key_mask,
    cotangent,
):
    rows, keys, depth = pair.shape
    heads = w_bias.shape[1]
    channels = w_query.shape[1] // heads
    npoint = w_qpoint.shape[1] // (3 * heads)
    chans = single_q.shape[1]
    hc = heads * channels
    n = rows * HP
    sds = jax.ShapeDtypeStruct
    params = pltpu.CompilerParams(vmem_limit_bytes=LIMIT)
    vmem = pl.BlockSpec(memory_space=pltpu.VMEM)
    wide = 3 * LANE
    km = key_mask.reshape(1, keys)
    w_query, w_key, w_value = w_query.T, w_key.T, w_value.T
    w_qpoint, w_kpoint, w_vpoint = w_qpoint.T, w_kpoint.T, w_vpoint.T
    w_bias = w_bias.T
    (
        masked,
        base,
        stats,
        query,
        key,
        value,
        gq,
        gk,
        gv,
        d_os,
        d_pt,
        rhs,
        qcol,
        kcol,
    ) = pl.pallas_call(
        functools.partial(logits_kernel, heads, channels, npoint),
        out_shape=[
            sds((n, keys), F32),
            sds((n, keys), F32),
            sds((2 * HP, rows), F32),
            sds((rows, hc), BF),
            sds((keys, hc), BF),
            sds((keys, hc), BF),
            sds((rows, wide), F32),
            sds((keys, wide), F32),
            sds((keys, wide), F32),
            sds((rows, hc), BF),
            sds((rows, 4 * LANE), F32),
            sds((rows, 3 * HP, depth), BF),
            sds((LANE, LANE), F32),
            sds((keys, LANE), F32),
        ],
        in_specs=[pl.BlockSpec(memory_space=pl.ANY)] + [vmem] * 20,
        out_specs=[vmem] * 14,
        scratch_shapes=[
            pltpu.VMEM((rows, keys, depth), BF),
            pltpu.VMEM((rows * 2 * HP, depth), F32),
            pltpu.VMEM((LANE, LANE), F32),
            pltpu.VMEM((LANE, keys), F32),
            pltpu.SemaphoreType.DMA((4,)),
        ],
        compiler_params=params,
        name="logits",
    )(
        pair,
        single_q,
        single_k,
        w_query,
        w_key,
        w_value,
        w_qpoint,
        w_kpoint,
        w_vpoint,
        w_bias,
        w_out,
        head_gamma.reshape(1, heads),
        chain_bias.reshape(1, heads),
        rot_q,
        trans_q,
        rot_k,
        trans_k,
        chain_q.reshape(1, rows),
        chain_k.reshape(1, keys),
        km,
        cotangent,
    )

    parts = [stats] + [permuted(stats, "col", f) for f in (1, 2, 3)]
    stats = merged(parts)
    stats = merged([stats] + [around(stats, f) for f in (3, 2, 1)])

    attn, points = pl.pallas_call(
        functools.partial(attend_kernel, heads, npoint),
        out_shape=[sds((n, keys), F32), sds((rows, wide), F32)],
        in_specs=[vmem] * 5,
        out_specs=[vmem] * 2,
        compiler_params=params,
        name="attend",
    )(masked, base, km, stats, gv)
    points = points + sum(permuted(points, "col", f) for f in (1, 2, 3))
    parts = [points] + [around(points, f) for f in (3, 2, 1)]

    me = lax.axis_index("row")
    place = jnp.stack([lax.axis_index("col"), me % 2, me // 4]).astype(jnp.int32)
    smem = pl.BlockSpec(memory_space=pltpu.SMEM)
    qpart, both, dlo, alo, dglob = pl.pallas_call(
        functools.partial(query_kernel, heads, channels, npoint),
        out_shape=[
            sds((rows + 8, chans), F32),
            sds((rows, 2 * HP, keys), BF),
            sds((n, keys), BF),
            sds((n, keys), BF),
            sds((rows, wide), F32),
        ],
        in_specs=[smem] + [vmem] * 14,
        out_specs=[vmem] * 5,
        compiler_params=params,
        name="query_grads",
    )(place, attn, base, *parts, key, gq, gk, gv, d_pt, qcol, w_query, w_qpoint)

    first = [qpart] + [permuted(qpart, "col", f) for f in (1, 2, 3)]
    half = sds((keys // 2 + 32, chans), F32)
    mine, other = pl.pallas_call(
        functools.partial(key_kernel, heads, channels, npoint),
        out_shape=[half, half],
        in_specs=[smem] + [vmem] * 14,
        out_specs=[vmem] * 2,
        compiler_params=params,
        name="key_grads",
        cost_estimate=pl.CostEstimate(
            flops=2 * n * keys * 12 * wide, bytes_accessed=4 * n * keys, transcendentals=0
        ),
    )(
        place,
        both,
        dlo,
        alo,
        dglob,
        query,
        gq,
        gk,
        d_os,
        qcol,
        kcol,
        w_key,
        w_value,
        w_kpoint,
        w_vpoint,
    )
    first[0], mine, other = lax.optimization_barrier((first[0], mine, other))

    mine = mine + permuted(other, "row", 1)
    mine = mine.reshape(4, -1, chans)
    held = mine[0] + sum(permuted(mine[f], "row", 4 * f) for f in (1, 2, 3))

    pair_grad = pl.pallas_call(
        pair_kernel,
        out_shape=sds((rows, keys, depth), BF),
        in_specs=[vmem] * 2,
        out_specs=vmem,
        compiler_params=params,
        name="pair_grad",
        cost_estimate=pl.CostEstimate(
            flops=2 * rows * keys * depth * 3 * HP,
            bytes_accessed=2 * rows * keys * depth,
            transcendentals=0,
        ),
    )(both, rhs)
    held, pair_grad = lax.optimization_barrier((held, pair_grad))
    qpart = (first[0] + first[1]) + (first[2] + first[3])
    second = [qpart] + [around(qpart, f) for f in (3, 2, 1)]
    held = held + permuted(held, "row", 2)
    mine = jnp.concatenate([held] + [permuted(held, "row", 4 * f) for f in (1, 2, 3)], axis=0)
    other = permuted(mine, "row", 1)
    grad_q, shift_q, grad_k, shift_k = pl.pallas_call(
        finish_kernel,
        out_shape=[
            sds((rows, chans), BF),
            sds((3, rows), F32),
            sds((keys, chans), BF),
            sds((3, keys), F32),
        ],
        in_specs=[smem] + [vmem] * 6,
        out_specs=[vmem] * 4,
        scratch_shapes=[pltpu.VMEM((8, keys), F32)],
        compiler_params=params,
        name="finish",
    )(place, *second, mine, other)
    return pair_grad, grad_q, shift_q, grad_k, shift_k


def solution(mesh):
    placed = (
        P("row", "col", None),
        P("row", None),
        P("col", None),
        P(),
        P(),
        P(),
        P(),
        P(),
        P(),
        P(),
        P(),
        P(),
        P(),
        P(None, "row"),
        P(None, "row"),
        P(None, "col"),
        P(None, "col"),
        P("row"),
        P("col"),
        P("col"),
        P("row", None),
    )
    return jax.shard_map(
        body,
        mesh=mesh,
        in_specs=placed,
        out_specs=(
            P("row", "col", None),
            P("row", None),
            P(None, "row"),
            P("col", None),
            P(None, "col"),
        ),
        check_vma=False,
    )
```

time: 628 us -> 116 us (0.18)
  the two profiles are of different devices: /device:TPU:1 before, /device:TPU:48 now
where the time goes in v1:
time: 116 us
  starting transfers between devices  40.8 us (35%)
  Pallas kernels  34.3 us (30%)
  waiting for transfers between devices  33.9 us (29%)
  other arithmetic  3.99 us (3%)
  local copies, waits for them, and re-layouts  1.98 us (2%)
    ppermute x18, starting transfers between devices, permuted(): return lax.ppermute(x, axis, [(i, i ^ flip) for i in range(size)])  22.8 us
    ppermute x9, waiting for transfers between devices, around(): return lax.ppermute(x, 'col', moves)  18.7 us
    ppermute x9, starting transfers between devices, around(): return lax.ppermute(x, 'col', moves)  18 us
    ppermute x18, waiting for transfers between devices, permuted(): return lax.ppermute(x, axis, [(i, i ^ flip) for i in range(size)])  15.3 us
    pallas_call x1, Pallas kernels, body(): pl.pallas_call(functools.partial(logits_kernel, heads, channels, npoint),...  10.8 us
    pallas_call x1, Pallas kernels, body(): pl.pallas_call(functools.partial(query_kernel, heads, channels, npoint),...  7.1 us
    pallas_call x1, Pallas kernels, body(): pl.pallas_call(functools.partial(key_kernel, heads, channels, npoint), ou...  6.39 us
    pallas_call x1, Pallas kernels, body(): pl.pallas_call(pair_kernel, out_shape=sds((rows, keys, depth), BF), in_sp...  4.77 us
  transfers between devices with their start and end apart: 27, of which 18 were waited for; matrix products, arithmetic and copies ran while one was open for 1% of the time, Pallas kernels for 4%

profile of v1, /device:TPU:48, one launch (start us, length us, event | category | flops | bytes accessed | tf_op | source)
XLA Modules:
  0.0 115.8 jit_solution(15719475557133372049)
XLA Ops:
  0.6 10.8 %logits.1 = (f32[1024,256]{1,0:T(8,128)}, f32[1024,256]{1,0:T(8,128)}, f32[32,64]{1,0:T(8,128)}, bf16[64,192]{1,0:T(8,128)(2,1)}, bf16[256,192]{1,0:T(8,128)(2,1...) custom-call(bf16[64,256,128]{2,1,0:T(8,128)(2,1)} %pair_hbm.1, ...), custom_call_target="tpu_custom_call" | custom-call | tf_op jit(solution)/shard_map/logits/pallas_call | solution.py:594
  12.6 1.9 %collective-permute-start.1 = (f32[32,64]{1,0:T(8,128)}, f32[32,64]{1,0:T(8,128)S(1)}, u32[]{:S(2)}, u32[]{:S(2)}) collective-permute-start(f32[32,64]{1,0:T(8,128)} %get-tuple-element.38), channel_id=1, source_target_pairs={{0,2},{1,3},{2,0},{3,1},{4,6},{5,7},{6,4},{7,5},{8,10},{9,11},{10,... | collective-permute-start | bytes 24584 | tf_op jit(solution)/shard_map/ppermute | solution.py:520
  15.0 1.4 %collective-permute-done.2 = f32[32,64]{1,0:T(8,128)S(1)} collective-permute-done((f32[32,64]{1,0:T(8,128)}, f32[32,64]{1,0:T(8,128)S(1)}, u32[]{:S(2)}, u32[]{:S(2)}) %collective-permute-start.2) | collective-permute-done | bytes 8224 | tf_op jit(solution)/shard_map/ppermute | solution.py:520
  16.6 1.9 %collective-permute-done = f32[32,64]{1,0:T(8,128)S(1)} collective-permute-done((f32[32,64]{1,0:T(8,128)}, f32[32,64]{1,0:T(8,128)S(1)}, u32[]{:S(2)}, u32[]{:S(2)}) %collective-permute-start) | collective-permute-done | bytes 8224 | tf_op jit(solution)/shard_map/ppermute | solution.py:520
  19.2 2.0 %collective-permute-start.5 = (f32[32,64]{1,0:T(8,128)S(1)}, f32[32,64]{1,0:T(8,128)S(1)}, u32[]{:S(2)}, u32[]{:S(2)}) collective-permute-start(f32[32,64]{1,0:T(8,128)S(1)} %pad_maximum_fusion.1), channel_id=1, source_target_pairs={{14,0},{15,1},{4,2},{5,3},{2,4},{3,5},{8,6},{9,7},{6,8},{7,9},{12,... | collective-permute-start | bytes 24584 | tf_op jit(solution)/shard_map/ppermute | solution.py:532
  21.2 4.5 %collective-permute-start.4 = (f32[32,64]{1,0:T(8,128)S(1)}, f32[32,64]{1,0:T(8,128)S(1)}, u32[]{:S(2)}, u32[]{:S(2)}) collective-permute-start(f32[32,64]{1,0:T(8,128)S(1)} %pad_maximum_fusion.1), channel_id=1, source_target_pairs={{4,0},{5,1},{14,2},{15,3},{8,4},{9,5},{2,6},{3,7},{12,8},{13,9},{6... | collective-permute-start | bytes 24584 | tf_op jit(solution)/shard_map/ppermute | solution.py:532
  25.7 1.4 %collective-permute-done.4 = f32[32,64]{1,0:T(8,128)S(1)} collective-permute-done((f32[32,64]{1,0:T(8,128)S(1)}, f32[32,64]{1,0:T(8,128)S(1)}, u32[]{:S(2)}, u32[]{:S(2)}) %collective-permute-start.4) | collective-permute-done | bytes 8224 | tf_op jit(solution)/shard_map/ppermute | solution.py:532
  27.1 5.3 %collective-permute-done.3 = f32[32,64]{1,0:T(8,128)S(1)} collective-permute-done((f32[32,64]{1,0:T(8,128)S(1)}, f32[32,64]{1,0:T(8,128)S(1)}, u32[]{:S(2)}, u32[]{:S(2)}) %collective-permute-start.3) | collective-permute-done | bytes 8224 | tf_op jit(solution)/shard_map/ppermute | solution.py:532
  33.0 3.2 %attend.1 = (f32[1024,256]{1,0:T(8,128)}, f32[64,384]{1,0:T(8,128)}) custom-call(f32[1024,256]{1,0:T(8,128)} %get-tuple-element.36.masked_ref, f32[1024,256]{1,0:T(8,128)} %get-tuple-element.37.base_ref, s32[1,256]{1,0:T(1,128)} %bitcast.29, f32[32,64]{1,0:T(8,128)} %pad_maximum_fusion.2.stats_ref, f32[256,384]{1,0:T(8,128)} %get-tuple-element.39.gv_ref), custom_call_target="tpu_custom_call" | custom-call | tf_op jit(solution)/shard_map/attend/pallas_call | solution.py:651
  38.2 1.5 %collective-permute-start.6 = (f32[64,384]{1,0:T(8,128)}, f32[64,384]{1,0:T(8,128)S(1)}, u32[]{:S(2)}, u32[]{:S(2)}) collective-permute-start(f32[64,384]{1,0:T(8,128)} %get-tuple-element.41), channel_id=1, source_target_pairs={{0,1},{1,0},{2,3},{3,2},{4,5},{5,4},{6,7},{7,6},{8,9},{9,8},{10,11... | collective-permute-start | bytes 294920 | tf_op jit(solution)/shard_map/ppermute | solution.py:520
  39.7 2.2 %collective-permute-done.8 = f32[64,384]{1,0:T(8,128)S(1)} collective-permute-done((f32[64,384]{1,0:T(8,128)}, f32[64,384]{1,0:T(8,128)S(1)}, u32[]{:S(2)}, u32[]{:S(2)}) %collective-permute-start.8) | collective-permute-done | bytes 98336 | tf_op jit(solution)/shard_map/ppermute | solution.py:520
  44.0 1.3 %collective-permute-start.11 = (f32[64,384]{1,0:T(8,128)S(1)}, f32[64,384]{1,0:T(8,128)S(1)}, u32[]{:S(2)}, u32[]{:S(2)}) collective-permute-start(f32[64,384]{1,0:T(8,128)S(1)} %add_add_fusion.1.psum0_ref), channel_id=1, source_target_pairs={{14,0},{15,1},{4,2},{5,3},{2,4},{3,5},{8,6},{9,7},{6,8},{7,9},{12,... | collective-permute-start | bytes 294920 | tf_op jit(solution)/shard_map/ppermute | solution.py:532
  46.0 3.9 %collective-permute-start.9 = (f32[64,384]{1,0:T(8,128)S(1)}, f32[64,384]{1,0:T(8,128)S(1)}, u32[]{:S(2)}, u32[]{:S(2)}) collective-permute-start(f32[64,384]{1,0:T(8,128)S(1)} %add_add_fusion.1.psum0_ref), channel_id=1, source_target_pairs={{10,0},{11,1},{8,2},{9,3},{14,4},{15,5},{12,6},{13,7},{2,8},{3,9},... | collective-permute-start | bytes 294920 | tf_op jit(solution)/shard_map/ppermute | solution.py:532
  50.5 1.5 %collective-permute-done.10.psum2_ref = f32[64,384]{1,0:T(8,128)S(1)} collective-permute-done((f32[64,384]{1,0:T(8,128)S(1)}, f32[64,384]{1,0:T(8,128)S(1)}, u32[]{:S(2)}, u32[]{:S(2)}) %collective-permute-start.10) | collective-permute-done | bytes 98336 | tf_op jit(solution)/shard_map/ppermute | solution.py:532
  52.0 1.7 %collective-permute-done.9.psum1_ref = f32[64,384]{1,0:T(8,128)S(1)} collective-permute-done((f32[64,384]{1,0:T(8,128)S(1)}, f32[64,384]{1,0:T(8,128)S(1)}, u32[]{:S(2)}, u32[]{:S(2)}) %collective-permute-start.9) | collective-permute-done | bytes 98336 | tf_op jit(solution)/shard_map/ppermute | solution.py:532
  54.3 7.1 %query_grads.1 = (f32[72,384]{1,0:T(8,128)}, bf16[64,32,256]{2,1,0:T(8,128)(2,1)}, bf16[1024,256]{1,0:T(8,128)(2,1)}, bf16[1024,256]{1,0:T(8,128)(2,1)}, f32[64,384]{1,0:T(8,128)}) custom-call(s32[3]{0:T(128)} %pad_add_fusion.place_ref, f32[1024,256]{1,0:T(8,128)} %get-tuple-element.40.attn_ref, f32[1024,256]{1,0:T(8,128)} %get-tuple-element.37.base_ref, ...), custom_call_target="tpu_custom_call" | custom-call | tf_op jit(solution)/shard_map/query_grads/pallas_call | solution.py:665
  61.4 6.4 %key_grads.1 = (f32[160,384]{1,0:T(8,128)}, f32[160,384]{1,0:T(8,128)}) custom-call(s32[3]{0:T(128)} %pad_add_fusion.place_ref, bf16[64,32,256]{2,1,0:T(8,128)(2,1)} %get-tuple-element.48.both_ref, bf16[1024,256]{1,0:T(8,128)(2,1)} %get-tuple-element.49.dlo_ref, bf16[1024,256]{1,0:T(8,128)(2,1)} %get-tuple-element.50.alo_ref, ...), custom_call_target="tpu_custom_call" | custom-call | flops 2415919104 | bytes 1048576 | tf_op jit(solution)/shard_map/key_grads/pallas_call | solution.py:682
  67.9 1.7 %collective-permute-done.12 = f32[160,384]{1,0:T(8,128)S(1)} collective-permute-done((f32[160,384]{1,0:T(8,128)}, f32[160,384]{1,0:T(8,128)S(1)}, u32[]{:S(2)}, u32[]{:S(2)}) %collective-permute-start.12) | collective-permute-done | bytes 245792 | tf_op jit(solution)/shard_map/ppermute | solution.py:520
  71.0 2.4 %collective-permute-start.15 = (f32[40,384]{1,0:T(8,128)S(1)}, f32[40,384]{1,0:T(8,128)S(1)}, u32[]{:S(2)}, u32[]{:S(2)}) collective-permute-start(f32[40,384]{1,0:T(8,128)S(1)} %get-tuple-element.72), channel_id=1, source_target_pairs={{0,192},{16,208},{32,224},{48,240},{64,128},{80,144},{96,160},{112... | collective-permute-start | bytes 184328 | tf_op jit(solution)/shard_map/ppermute | solution.py:520
  73.4 2.0 %collective-permute-start.13 = (f32[40,384]{1,0:T(8,128)S(1)}, f32[40,384]{1,0:T(8,128)S(1)}, u32[]{:S(2)}, u32[]{:S(2)}) collective-permute-start(f32[40,384]{1,0:T(8,128)S(1)} %get-tuple-element.73), channel_id=1, source_target_pairs={{0,64},{16,80},{32,96},{48,112},{64,0},{80,16},{96,32},{112,48},{1... | collective-permute-start | bytes 184328 | tf_op jit(solution)/shard_map/ppermute | solution.py:520
  75.4 4.8 %pair_grad.1 = bf16[64,256,128]{2,1,0:T(8,128)(2,1)} custom-call(bf16[64,32,256]{2,1,0:T(8,128)(2,1)} %get-tuple-element.48.both_ref, bf16[64,48,128]{2,1,0:T(8,128)(2,1)} %get-tuple-element.59.rhs_ref), custom_call_target="tpu_custom_call" | custom-call | flops 201326592 | bytes 4194304 | tf_op jit(solution)/shard_map/pair_grad/pallas_call | solution.py:715
  80.2 3.1 %collective-permute-start.22 = (f32[40,384]{1,0:T(8,128)S(1)}, f32[40,384]{1,0:T(8,128)S(1)}, u32[]{:S(2)}, u32[]{:S(2)}) collective-permute-start(f32[40,384]{1,0:T(8,128)S(1)} %slice_add_fusion), channel_id=1, source_target_pairs={{0,32},{16,48},{32,0},{48,16},{64,96},{80,112},{96,64},{112,80},{1... | collective-permute-start | bytes 184328 | tf_op jit(solution)/shard_map/ppermute | solution.py:520
  83.3 2.7 %collective-permute-done.22 = f32[40,384]{1,0:T(8,128)S(1)} collective-permute-done((f32[40,384]{1,0:T(8,128)S(1)}, f32[40,384]{1,0:T(8,128)S(1)}, u32[]{:S(2)}, u32[]{:S(2)}) %collective-permute-start.22) | collective-permute-done | bytes 61472 | tf_op jit(solution)/shard_map/ppermute | solution.py:520
  86.6 1.7 %collective-permute-start.24 = (f32[40,384]{1,0:T(8,128)S(1)}, f32[40,384]{1,0:T(8,128)S(1)}, u32[]{:S(2)}, u32[]{:S(2)}) collective-permute-start(f32[40,384]{1,0:T(8,128)S(1)} %add.73), channel_id=1, source_target_pairs={{0,128},{16,144},{32,160},{48,176},{64,192},{80,208},{96,224},{112... | collective-permute-start | bytes 184328 | tf_op jit(solution)/shard_map/ppermute | solution.py:520
  88.3 2.0 %collective-permute-start.23 = (f32[40,384]{1,0:T(8,128)S(1)}, f32[40,384]{1,0:T(8,128)S(1)}, u32[]{:S(2)}, u32[]{:S(2)}) collective-permute-start(f32[40,384]{1,0:T(8,128)S(1)} %add.73), channel_id=1, source_target_pairs={{0,64},{16,80},{32,96},{48,112},{64,0},{80,16},{96,32},{112,48},{1... | collective-permute-start | bytes 184328 | tf_op jit(solution)/shard_map/ppermute | solution.py:520
  90.2 2.0 %collective-permute-start.18 = (f32[72,384]{1,0:T(8,128)S(1)}, f32[72,384]{1,0:T(8,128)S(1)}, u32[]{:S(2)}, u32[]{:S(2)}) collective-permute-start(f32[72,384]{1,0:T(8,128)S(1)} %copy-done.7), channel_id=1, source_target_pairs={{0,3},{1,2},{2,1},{3,0},{4,7},{5,6},{6,5},{7,4},{8,11},{9,10},{10,... | collective-permute-start | bytes 331784 | tf_op jit(solution)/shard_map/ppermute | solution.py:520
  93.8 2.0 %collective-permute-done.18 = f32[72,384]{1,0:T(8,128)S(1)} collective-permute-done((f32[72,384]{1,0:T(8,128)S(1)}, f32[72,384]{1,0:T(8,128)S(1)}, u32[]{:S(2)}, u32[]{:S(2)}) %collective-permute-start.18) | collective-permute-done | bytes 110624 | tf_op jit(solution)/shard_map/ppermute | solution.py:520
  95.9 1.2 %collective-permute-done.17 = f32[72,384]{1,0:T(8,128)S(1)} collective-permute-done((f32[72,384]{1,0:T(8,128)S(1)}, f32[72,384]{1,0:T(8,128)S(1)}, u32[]{:S(2)}, u32[]{:S(2)}) %collective-permute-start.17) | collective-permute-done | bytes 110624 | tf_op jit(solution)/shard_map/ppermute | solution.py:520
  99.1 4.4 %collective-permute-start.20 = (f32[72,384]{1,0:T(8,128)S(1)}, f32[72,384]{1,0:T(8,128)S(1)}, u32[]{:S(2)}, u32[]{:S(2)}) collective-permute-start(f32[72,384]{1,0:T(8,128)S(1)} %add_add_fusion.q0_ref), channel_id=1, source_target_pairs={{4,0},{5,1},{14,2},{15,3},{8,4},{9,5},{2,6},{3,7},{12,8},{13,9},{6... | collective-permute-start | bytes 331784 | tf_op jit(solution)/shard_map/ppermute | solution.py:532
  103.9 4.8 %collective-permute-done.20.q2_ref = f32[72,384]{1,0:T(8,128)S(1)} collective-permute-done((f32[72,384]{1,0:T(8,128)S(1)}, f32[72,384]{1,0:T(8,128)S(1)}, u32[]{:S(2)}, u32[]{:S(2)}) %collective-permute-start.20) | collective-permute-done | bytes 110624 | tf_op jit(solution)/shard_map/ppermute | solution.py:532
  108.7 3.7 %collective-permute-done.19.q1_ref = f32[72,384]{1,0:T(8,128)S(1)} collective-permute-done((f32[72,384]{1,0:T(8,128)S(1)}, f32[72,384]{1,0:T(8,128)S(1)}, u32[]{:S(2)}, u32[]{:S(2)}) %collective-permute-start.19) | collective-permute-done | bytes 110624 | tf_op jit(solution)/shard_map/ppermute | solution.py:532
  113.7 2.1 %finish.1 = (bf16[64,384]{1,0:T(8,128)(2,1)}, f32[3,64]{1,0:T(4,128)}, bf16[256,384]{1,0:T(8,128)(2,1)}, f32[3,256]{1,0:T(4,128)}) custom-call(s32[3]{0:T(128)} %pad_add_fusion.place_ref, f32[72,384]{1,0:T(8,128)} %copy-done.1, f32[72,384]{1,0:T(8,128)} %copy-done.6, f32[72,384]{1,0:T(8,128)} %copy-done.5, f32[72,384]{1,0:T(8,128)} %copy-done.4, ...), custom_call_target="tpu_custom_call" | custom-call | tf_op jit(solution)/shard_map/finish/pallas_call | solution.py:734
  (62 shorter events, 16.6 us)
Async XLA Ops:
  11.4 4.9 %collective-permute-start.2 = (f32[32,64]{1,0:T(8,128)}, f32[32,64]{1,0:T(8,128)S(1)}, u32[]{:S(2)}, u32[]{:S(2)}) collective-permute-start(f32[32,64]{1,0:T(8,128)} %get-tuple-element.38), channel_id=1, source_target_pairs={{0,3},{1,2},{2,1},{3,0},{4,7},{5,6},{6,5},{7,4},{8,11},{9,10},{10,... | collective-permute-start | bytes 24584 | tf_op jit(solution)/shard_map/ppermute | solution.py:520
  12.6 4.0 %collective-permute-start.1 = (f32[32,64]{1,0:T(8,128)}, f32[32,64]{1,0:T(8,128)S(1)}, u32[]{:S(2)}, u32[]{:S(2)}) collective-permute-start(f32[32,64]{1,0:T(8,128)} %get-tuple-element.38), channel_id=1, source_target_pairs={{0,2},{1,3},{2,0},{3,1},{4,6},{5,7},{6,4},{7,5},{8,10},{9,11},{10,... | collective-permute-start | bytes 24584 | tf_op jit(solution)/shard_map/ppermute | solution.py:520
  14.5 3.9 %collective-permute-start = (f32[32,64]{1,0:T(8,128)}, f32[32,64]{1,0:T(8,128)S(1)}, u32[]{:S(2)}, u32[]{:S(2)}) collective-permute-start(f32[32,64]{1,0:T(8,128)} %get-tuple-element.38), channel_id=1, source_target_pairs={{0,1},{1,0},{2,3},{3,2},{4,5},{5,4},{6,7},{7,6},{8,9},{9,8},{10,11... | collective-permute-start | bytes 24584 | tf_op jit(solution)/shard_map/ppermute | solution.py:520
  19.2 6.5 %collective-permute-start.5 = (f32[32,64]{1,0:T(8,128)S(1)}, f32[32,64]{1,0:T(8,128)S(1)}, u32[]{:S(2)}, u32[]{:S(2)}) collective-permute-start(f32[32,64]{1,0:T(8,128)S(1)} %pad_maximum_fusion.1), channel_id=1, source_target_pairs={{14,0},{15,1},{4,2},{5,3},{2,4},{3,5},{8,6},{9,7},{6,8},{7,9},{12,... | collective-permute-start | bytes 24584 | tf_op jit(solution)/shard_map/ppermute | solution.py:532
  21.2 5.9 %collective-permute-start.4 = (f32[32,64]{1,0:T(8,128)S(1)}, f32[32,64]{1,0:T(8,128)S(1)}, u32[]{:S(2)}, u32[]{:S(2)}) collective-permute-start(f32[32,64]{1,0:T(8,128)S(1)} %pad_maximum_fusion.1), channel_id=1, source_target_pairs={{4,0},{5,1},{14,2},{15,3},{8,4},{9,5},{2,6},{3,7},{12,8},{13,9},{6... | collective-permute-start | bytes 24584 | tf_op jit(solution)/shard_map/ppermute | solution.py:532
  25.7 6.7 %collective-permute-start.3 = (f32[32,64]{1,0:T(8,128)S(1)}, f32[32,64]{1,0:T(8,128)S(1)}, u32[]{:S(2)}, u32[]{:S(2)}) collective-permute-start(f32[32,64]{1,0:T(8,128)S(1)} %pad_maximum_fusion.1), channel_id=1, source_target_pairs={{10,0},{11,1},{8,2},{9,3},{14,4},{15,5},{12,6},{13,7},{2,8},{3,9},... | collective-permute-start | bytes 24584 | tf_op jit(solution)/shard_map/ppermute | solution.py:532
  36.2 5.7 %collective-permute-start.8 = (f32[64,384]{1,0:T(8,128)}, f32[64,384]{1,0:T(8,128)S(1)}, u32[]{:S(2)}, u32[]{:S(2)}) collective-permute-start(f32[64,384]{1,0:T(8,128)} %get-tuple-element.41), channel_id=1, source_target_pairs={{0,3},{1,2},{2,1},{3,0},{4,7},{5,6},{6,5},{7,4},{8,11},{9,10},{10,... | collective-permute-start | bytes 294920 | tf_op jit(solution)/shard_map/ppermute | solution.py:520
  37.4 4.8 %collective-permute-start.7 = (f32[64,384]{1,0:T(8,128)}, f32[64,384]{1,0:T(8,128)S(1)}, u32[]{:S(2)}, u32[]{:S(2)}) collective-permute-start(f32[64,384]{1,0:T(8,128)} %get-tuple-element.41), channel_id=1, source_target_pairs={{0,2},{1,3},{2,0},{3,1},{4,6},{5,7},{6,4},{7,5},{8,10},{9,11},{10,... | collective-permute-start | bytes 294920 | tf_op jit(solution)/shard_map/ppermute | solution.py:520
  38.2 4.8 %collective-permute-start.6 = (f32[64,384]{1,0:T(8,128)}, f32[64,384]{1,0:T(8,128)S(1)}, u32[]{:S(2)}, u32[]{:S(2)}) collective-permute-start(f32[64,384]{1,0:T(8,128)} %get-tuple-element.41), channel_id=1, source_target_pairs={{0,1},{1,0},{2,3},{3,2},{4,5},{5,4},{6,7},{7,6},{8,9},{9,8},{10,11... | collective-permute-start | bytes 294920 | tf_op jit(solution)/shard_map/ppermute | solution.py:520
  44.0 9.7 %copy-start.2 = (f32[64,384]{1,0:T(8,128)}, f32[64,384]{1,0:T(8,128)S(1)}, u32[]{:S(2)}) copy-start(f32[64,384]{1,0:T(8,128)S(1)} %add_add_fusion.1.psum0_ref) | copy-start | bytes 294916
  44.0 6.5 %collective-permute-start.11 = (f32[64,384]{1,0:T(8,128)S(1)}, f32[64,384]{1,0:T(8,128)S(1)}, u32[]{:S(2)}, u32[]{:S(2)}) collective-permute-start(f32[64,384]{1,0:T(8,128)S(1)} %add_add_fusion.1.psum0_ref), channel_id=1, source_target_pairs={{14,0},{15,1},{4,2},{5,3},{2,4},{3,5},{8,6},{9,7},{6,8},{7,9},{12,... | collective-permute-start | bytes 294920 | tf_op jit(solution)/shard_map/ppermute | solution.py:532
  45.3 6.7 %collective-permute-start.10 = (f32[64,384]{1,0:T(8,128)S(1)}, f32[64,384]{1,0:T(8,128)S(1)}, u32[]{:S(2)}, u32[]{:S(2)}) collective-permute-start(f32[64,384]{1,0:T(8,128)S(1)} %add_add_fusion.1.psum0_ref), channel_id=1, source_target_pairs={{4,0},{5,1},{14,2},{15,3},{8,4},{9,5},{2,6},{3,7},{12,8},{13,9},{6... | collective-permute-start | bytes 294920 | tf_op jit(solution)/shard_map/ppermute | solution.py:532
  46.0 7.7 %collective-permute-start.9 = (f32[64,384]{1,0:T(8,128)S(1)}, f32[64,384]{1,0:T(8,128)S(1)}, u32[]{:S(2)}, u32[]{:S(2)}) collective-permute-start(f32[64,384]{1,0:T(8,128)S(1)} %add_add_fusion.1.psum0_ref), channel_id=1, source_target_pairs={{10,0},{11,1},{8,2},{9,3},{14,4},{15,5},{12,6},{13,7},{2,8},{3,9},... | collective-permute-start | bytes 294920 | tf_op jit(solution)/shard_map/ppermute | solution.py:532
  67.8 22.4 %copy-start.7 = (f32[72,384]{1,0:T(8,128)S(1)}, f32[72,384]{1,0:T(8,128)}, u32[]{:S(2)}) copy-start(f32[72,384]{1,0:T(8,128)} %get-tuple-element.61) | copy-start | bytes 331780
  67.8 1.8 %collective-permute-start.12 = (f32[160,384]{1,0:T(8,128)}, f32[160,384]{1,0:T(8,128)S(1)}, u32[]{:S(2)}, u32[]{:S(2)}) collective-permute-start(f32[160,384]{1,0:T(8,128)} %get-tuple-element.58), channel_id=1, source_target_pairs={{0,16},{16,0},{32,48},{48,32},{64,80},{80,64},{96,112},{112,96},{1... | collective-permute-start | bytes 737288 | tf_op jit(solution)/shard_map/ppermute | solution.py:520
  70.6 9.6 %collective-permute-start.14 = (f32[40,384]{1,0:T(8,128)S(1)}, f32[40,384]{1,0:T(8,128)S(1)}, u32[]{:S(2)}, u32[]{:S(2)}) collective-permute-start(f32[40,384]{1,0:T(8,128)S(1)} %get-tuple-element.71), channel_id=1, source_target_pairs={{0,128},{16,144},{32,160},{48,176},{64,192},{80,208},{96,224},{112... | collective-permute-start | bytes 184328 | tf_op jit(solution)/shard_map/ppermute | solution.py:520
  71.0 9.1 %collective-permute-start.15 = (f32[40,384]{1,0:T(8,128)S(1)}, f32[40,384]{1,0:T(8,128)S(1)}, u32[]{:S(2)}, u32[]{:S(2)}) collective-permute-start(f32[40,384]{1,0:T(8,128)S(1)} %get-tuple-element.72), channel_id=1, source_target_pairs={{0,192},{16,208},{32,224},{48,240},{64,128},{80,144},{96,160},{112... | collective-permute-start | bytes 184328 | tf_op jit(solution)/shard_map/ppermute | solution.py:520
  73.4 6.7 %collective-permute-start.13 = (f32[40,384]{1,0:T(8,128)S(1)}, f32[40,384]{1,0:T(8,128)S(1)}, u32[]{:S(2)}, u32[]{:S(2)}) collective-permute-start(f32[40,384]{1,0:T(8,128)S(1)} %get-tuple-element.73), channel_id=1, source_target_pairs={{0,64},{16,80},{32,96},{48,112},{64,0},{80,16},{96,32},{112,48},{1... | collective-permute-start | bytes 184328 | tf_op jit(solution)/shard_map/ppermute | solution.py:520
  80.2 5.8 %collective-permute-start.22 = (f32[40,384]{1,0:T(8,128)S(1)}, f32[40,384]{1,0:T(8,128)S(1)}, u32[]{:S(2)}, u32[]{:S(2)}) collective-permute-start(f32[40,384]{1,0:T(8,128)S(1)} %slice_add_fusion), channel_id=1, source_target_pairs={{0,32},{16,48},{32,0},{48,16},{64,96},{80,112},{96,64},{112,80},{1... | collective-permute-start | bytes 184328 | tf_op jit(solution)/shard_map/ppermute | solution.py:520
  86.0 7.1 %collective-permute-start.25 = (f32[40,384]{1,0:T(8,128)S(1)}, f32[40,384]{1,0:T(8,128)S(1)}, u32[]{:S(2)}, u32[]{:S(2)}) collective-permute-start(f32[40,384]{1,0:T(8,128)S(1)} %add.73), channel_id=1, source_target_pairs={{0,192},{16,208},{32,224},{48,240},{64,128},{80,144},{96,160},{112... | collective-permute-start | bytes 184328 | tf_op jit(solution)/shard_map/ppermute | solution.py:520
  86.6 7.1 %collective-permute-start.24 = (f32[40,384]{1,0:T(8,128)S(1)}, f32[40,384]{1,0:T(8,128)S(1)}, u32[]{:S(2)}, u32[]{:S(2)}) collective-permute-start(f32[40,384]{1,0:T(8,128)S(1)} %add.73), channel_id=1, source_target_pairs={{0,128},{16,144},{32,160},{48,176},{64,192},{80,208},{96,224},{112... | collective-permute-start | bytes 184328 | tf_op jit(solution)/shard_map/ppermute | solution.py:520
  88.3 5.5 %collective-permute-start.23 = (f32[40,384]{1,0:T(8,128)S(1)}, f32[40,384]{1,0:T(8,128)S(1)}, u32[]{:S(2)}, u32[]{:S(2)}) collective-permute-start(f32[40,384]{1,0:T(8,128)S(1)} %add.73), channel_id=1, source_target_pairs={{0,64},{16,80},{32,96},{48,112},{64,0},{80,16},{96,32},{112,48},{1... | collective-permute-start | bytes 184328 | tf_op jit(solution)/shard_map/ppermute | solution.py:520
  90.2 5.6 %collective-permute-start.18 = (f32[72,384]{1,0:T(8,128)S(1)}, f32[72,384]{1,0:T(8,128)S(1)}, u32[]{:S(2)}, u32[]{:S(2)}) collective-permute-start(f32[72,384]{1,0:T(8,128)S(1)} %copy-done.7), channel_id=1, source_target_pairs={{0,3},{1,2},{2,1},{3,0},{4,7},{5,6},{6,5},{7,4},{8,11},{9,10},{10,... | collective-permute-start | bytes 331784 | tf_op jit(solution)/shard_map/ppermute | solution.py:520
  92.2 4.9 %collective-permute-start.17 = (f32[72,384]{1,0:T(8,128)S(1)}, f32[72,384]{1,0:T(8,128)S(1)}, u32[]{:S(2)}, u32[]{:S(2)}) collective-permute-start(f32[72,384]{1,0:T(8,128)S(1)} %copy-done.7), channel_id=1, source_target_pairs={{0,2},{1,3},{2,0},{3,1},{4,6},{5,7},{6,4},{7,5},{8,10},{9,11},{10,... | collective-permute-start | bytes 331784 | tf_op jit(solution)/shard_map/ppermute | solution.py:520
  93.2 4.7 %collective-permute-start.16 = (f32[72,384]{1,0:T(8,128)S(1)}, f32[72,384]{1,0:T(8,128)S(1)}, u32[]{:S(2)}, u32[]{:S(2)}) collective-permute-start(f32[72,384]{1,0:T(8,128)S(1)} %copy-done.7), channel_id=1, source_target_pairs={{0,1},{1,0},{2,3},{3,2},{4,5},{5,4},{6,7},{7,6},{8,9},{9,8},{10,11... | collective-permute-start | bytes 331784 | tf_op jit(solution)/shard_map/ppermute | solution.py:520
  93.7 18.7 %copy-start = (f32[160,384]{1,0:T(8,128)}, f32[160,384]{1,0:T(8,128)S(1)}, u32[]{:S(2)}) copy-start(f32[160,384]{1,0:T(8,128)S(1)} %pad_maximum_fusion.mine_ref) | copy-start | bytes 737284
  93.7 18.7 %collective-permute-start.26 = (f32[160,384]{1,0:T(8,128)S(1)}, f32[160,384]{1,0:T(8,128)S(1)}, u32[]{:S(2)}, u32[]{:S(2)}) collective-permute-start(f32[160,384]{1,0:T(8,128)S(1)} %pad_maximum_fusion.mine_ref), channel_id=1, source_target_pairs={{0,16},{16,0},{32,48},{48,32},{64,80},{80,64},{96,112},{112,96},{1... | collective-permute-start | bytes 737288 | tf_op jit(solution)/shard_map/ppermute | solution.py:520
  98.0 14.4 %copy-start.1 = (f32[72,384]{1,0:T(8,128)}, f32[72,384]{1,0:T(8,128)S(1)}, u32[]{:S(2)}) copy-start(f32[72,384]{1,0:T(8,128)S(1)} %add_add_fusion.q0_ref) | copy-start | bytes 331780
  98.0 5.9 %collective-permute-start.21 = (f32[72,384]{1,0:T(8,128)S(1)}, f32[72,384]{1,0:T(8,128)S(1)}, u32[]{:S(2)}, u32[]{:S(2)}) collective-permute-start(f32[72,384]{1,0:T(8,128)S(1)} %add_add_fusion.q0_ref), channel_id=1, source_target_pairs={{14,0},{15,1},{4,2},{5,3},{2,4},{3,5},{8,6},{9,7},{6,8},{7,9},{12,... | collective-permute-start | bytes 331784 | tf_op jit(solution)/shard_map/ppermute | solution.py:532
  99.1 9.7 %collective-permute-start.20 = (f32[72,384]{1,0:T(8,128)S(1)}, f32[72,384]{1,0:T(8,128)S(1)}, u32[]{:S(2)}, u32[]{:S(2)}) collective-permute-start(f32[72,384]{1,0:T(8,128)S(1)} %add_add_fusion.q0_ref), channel_id=1, source_target_pairs={{4,0},{5,1},{14,2},{15,3},{8,4},{9,5},{2,6},{3,7},{12,8},{13,9},{6... | collective-permute-start | bytes 331784 | tf_op jit(solution)/shard_map/ppermute | solution.py:532
  103.4 8.9 %collective-permute-start.19 = (f32[72,384]{1,0:T(8,128)S(1)}, f32[72,384]{1,0:T(8,128)S(1)}, u32[]{:S(2)}, u32[]{:S(2)}) collective-permute-start(f32[72,384]{1,0:T(8,128)S(1)} %add_add_fusion.q0_ref), channel_id=1, source_target_pairs={{10,0},{11,1},{8,2},{9,3},{14,4},{15,5},{12,6},{13,7},{2,8},{3,9},... | collective-permute-start | bytes 331784 | tf_op jit(solution)/shard_map/ppermute | solution.py:532
  103.9 8.5 %copy-start.4 = (f32[72,384]{1,0:T(8,128)}, f32[72,384]{1,0:T(8,128)S(1)}, u32[]{:S(2)}) copy-start(f32[72,384]{1,0:T(8,128)S(1)} %collective-permute-done.21.q3_ref) | copy-start | bytes 331780
  (6 other events, 10.6 us)

commit v2 on v1

--- a/solution.py
+++ b/solution.py
@@ -128,7 +128,7 @@
     cot_ref,
     masked_ref,
     base_ref,
-    stats_ref,
+    sums_ref,
     query_ref,
     key_ref,
     value_ref,
@@ -246,33 +246,53 @@
     valid = (km_ref[...] == 1)[None]
     masked = jnp.where(valid, logit, NEG)
     top = jnp.max(masked, axis=2, keepdims=True)
-    total = jnp.sum(jnp.where(valid, jnp.exp(masked - top), 0.0), axis=2, keepdims=True)
-    masked_ref[...] = masked.reshape(rows * HP, keys)
-    packed = to_lanes(top.reshape(rows * HP, 1)) + to_lanes(total.reshape(rows * HP, 1), HP)
-    stats_ref[...] = packed.T[: 2 * HP]
+    expo = jnp.where(valid, jnp.exp(masked - top), 0.0)
+    total = jnp.sum(expo, axis=2, keepdims=True).reshape(rows * HP, 1)
+    expo = expo.reshape(rows * HP, keys)
+    masked_ref[...] = expo
     dosm = spread(dos_ref[...].astype(F32), cmask).astype(BF)
-    base_ref[...] += nt(dosm, value_ref[...])
-
-
-def attend_kernel(heads, npoint, masked_ref, base_ref, km_ref, stats_ref, gv_ref, attn_ref, out_ref):
-    rows = stats_ref.shape[1]
-    keys = masked_ref.shape[1]
-    stats = jnp.concatenate(
-        [stats_ref[...], jnp.zeros((LANE - stats_ref.shape[0], rows), F32)], axis=0
-    ).T
-    top = to_col(stats)
-    total = to_col(stats, HP)
-    valid = km_ref[...] == 1
-    attn = jnp.where(valid, jnp.exp(masked_ref[...] - top), 0.0) / total
-    attn_ref[...] = attn
-    attn_b = attn.astype(BF)
-    attn_f = attn_b.astype(F32)
+    base = base_ref[...] + nt(dosm, value_ref[...])
+    base_ref[...] = base
+    ehi, elo = split(expo)
     ghi, glo = split(gv_ref[...])
-    opt = nn(attn_b, ghi) + nn(attn_b, glo)
-    pmask = head_mask(heads, npoint, 3 * LANE)
-    delta = jnp.sum(attn_f * base_ref[...], axis=1, keepdims=True)
-    out_ref[...] = gather_heads(opt, pmask)
-    out_ref[:, 0:LANE] += to_lanes(delta, heads * npoint)
+    points = nn(ehi, ghi) + (nn(ehi, glo) + nn(elo, ghi))
+    sums_ref[...] = gather_heads(points, pmask)
+    sums_ref[:, 0:LANE] += to_lanes(jnp.sum(expo * base, axis=1, keepdims=True), hp)
+    sums_ref[:, LANE : 2 * LANE] += to_lanes(top.reshape(rows * HP, 1), hp)
+    sums_ref[:, 2 * LANE : 3 * LANE] += to_lanes(total, hp)
+
+
+def stat_lanes(heads, npoint):
+    lane = iota((1, LANE), 1) - heads * npoint
+    return (lane >= 0) & (lane < heads)
+
+
+def over_lanes(x, heads, npoint):
+    hp = heads * npoint
+    row = iota((LANE, 3 * LANE), 0)
+    full = iota((LANE, 3 * LANE), 1)
+    lane = full % LANE
+    hit = ((lane < hp) & (lane // npoint == row - hp)) | ((lane == row) & (full // LANE != 1))
+    hit = hit & (row >= hp) & (row < hp + heads)
+    x = jnp.where(stat_lanes(heads, npoint), x, 0.0)
+    return nn(x, hit.astype(F32), HIGH)
+
+
+def combined(parts, heads, npoint):
+    tops = [p[:, LANE : 2 * LANE] for p in parts]
+    top = functools.reduce(jnp.maximum, tops)
+    total = sum(
+        p * over_lanes(jnp.exp(t - top), heads, npoint) for p, t in zip(parts, tops)
+    )
+    top = jnp.where(stat_lanes(heads, npoint), top, 0.0)
+    zero = jnp.zeros_like(top)
+    return total + jnp.concatenate([zero, top, zero], axis=1)
+
+
+def combine_kernel(heads, npoint, p0_ref, p1_ref, p2_ref, p3_ref, out_ref):
+    out_ref[...] = combined(
+        [p0_ref[...], p1_ref[...], p2_ref[...], p3_ref[...]], heads, npoint
+    )
 
 
 def frames_of(heads, npoint, qcol_ref, rows):
@@ -304,8 +324,9 @@
     channels,
     npoint,
     place_ref,
-    attn_ref,
+    expo_ref,
     base_ref,
+    own_ref,
     psum0_ref,
     psum1_ref,
     psum2_ref,
@@ -331,7 +352,14 @@
     pmask, qcols, coef_lane = frames_of(heads, npoint, qcol_ref, rows)
     inside = iota((1, LANE), 1) < hp
 
-    psum = (psum0_ref[...] + psum1_ref[...]) + (psum2_ref[...] + psum3_ref[...])
+    psum = combined(
+        [psum0_ref[...], psum1_ref[...], psum2_ref[...], psum3_ref[...]], heads, npoint
+    )
+    stat = stat_lanes(heads, npoint)
+    inv = jnp.where(stat, 1.0 / psum[:, 2 * LANE :], 0.0)
+    own = jnp.where(stat, own_ref[:, LANE : 2 * LANE] - psum[:, LANE : 2 * LANE], 0.0)
+    attn = expo_ref[...] * to_col(jnp.exp(own) * inv, hp)
+    psum = psum * over_lanes(inv, heads, npoint)
     delta0 = to_col(psum[:, :LANE], hp)
     opt = [jnp.where(inside, psum[:, a * LANE : (a + 1) * LANE], 0.0) for a in range(3)]
     moved = [jnp.where(inside, opt[a] - qcols[:, 9 + a : 10 + a], 0.0) for a in range(3)]
@@ -352,7 +380,6 @@
     delta = delta0 + jnp.sum(spread(opt_row * dglob, pmask), axis=1, keepdims=True)
     gvhi, gvlo = split(gv_ref[...])
     dattn = base_ref[...] + nt(dghi, gvhi) + (nt(dghi, gvlo) + nt(dglo, gvhi))
-    attn = attn_ref[...]
     dlogit = attn * (dattn - delta)
     dhi, dlo = split(dlogit)
     ahi, alo = split(attn)
@@ -364,7 +391,7 @@
     gkhi, gklo = split(gk_ref[...])
     dq = scale * gather_heads(nn(dhi, key_ref[...]), cmask)
     qpts = gather_heads(nn(dhi, gkhi) + (nn(dhi, gklo) + nn(dlo, gkhi)), pmask)
-    qsum = jnp.sum(dlogit, axis=1, keepdims=True)
+    qsum = jnp.sum(dlogit + (attn - ahi.astype(F32)) * dattn, axis=1, keepdims=True)
     qsum_lane = gather_heads(jnp.broadcast_to(qsum, (rows * HP, 3 * LANE)), pmask)
     dgq = coef_lane * (qpts - gq_ref[...] * qsum_lane)
     mq = back_rotate(dgq, qcols)
@@ -530,12 +557,6 @@
         source = (z + (hops if z % 2 else -hops) * sign) % ring
         moves.append((source * 2 + low, i))
     return lax.ppermute(x, "col", moves)
-
-
-def merged(parts):
-    top = functools.reduce(jnp.maximum, [p[:HP] for p in parts])
-    total = sum(p[HP:] * jnp.exp(p[:HP] - top) for p in parts)
-    return jnp.concatenate([top, total], axis=0)
 
 
 def body(
@@ -577,9 +598,9 @@
     w_qpoint, w_kpoint, w_vpoint = w_qpoint.T, w_kpoint.T, w_vpoint.T
     w_bias = w_bias.T
     (
-        masked,
+        expo,
         base,
-        stats,
+        sums,
         query,
         key,
         value,
@@ -596,7 +617,7 @@
         out_shape=[
             sds((n, keys), F32),
             sds((n, keys), F32),
-            sds((2 * HP, rows), F32),
+            sds((rows, wide), F32),
             sds((rows, hc), BF),
             sds((keys, hc), BF),
             sds((keys, hc), BF),
@@ -644,20 +665,16 @@
         cotangent,
     )
 
-    parts = [stats] + [permuted(stats, "col", f) for f in (1, 2, 3)]
-    stats = merged(parts)
-    stats = merged([stats] + [around(stats, f) for f in (3, 2, 1)])
-
-    attn, points = pl.pallas_call(
-        functools.partial(attend_kernel, heads, npoint),
-        out_shape=[sds((n, keys), F32), sds((rows, wide), F32)],
-        in_specs=[vmem] * 5,
-        out_specs=[vmem] * 2,
+    parts = [sums] + [permuted(sums, "col", f) for f in (1, 2, 3)]
+    merged = pl.pallas_call(
+        functools.partial(combine_kernel, heads, npoint),
+        out_shape=sds((rows, wide), F32),
+        in_specs=[vmem] * 4,
+        out_specs=vmem,
         compiler_params=params,
-        name="attend",
-    )(masked, base, km, stats, gv)
-    points = points + sum(permuted(points, "col", f) for f in (1, 2, 3))
-    parts = [points] + [around(points, f) for f in (3, 2, 1)]
+        name="combine",
+    )(*parts)
+    parts = [merged] + [around(merged, f) for f in (3, 2, 1)]
 
     me = lax.axis_index("row")
     place = jnp.stack([lax.axis_index("col"), me % 2, me // 4]).astype(jnp.int32)
@@ -671,11 +688,11 @@
             sds((n, keys), BF),
             sds((rows, wide), F32),
         ],
-        in_specs=[smem] + [vmem] * 14,
+        in_specs=[smem] + [vmem] * 15,
         out_specs=[vmem] * 5,
         compiler_params=params,
         name="query_grads",
-    )(place, attn, base, *parts, key, gq, gk, gv, d_pt, qcol, w_query, w_qpoint)
+    )(place, expo, base, sums, *parts, key, gq, gk, gv, d_pt, qcol, w_query, w_qpoint)
 
     first = [qpart] + [permuted(qpart, "col", f) for f in (1, 2, 3)]
     half = sds((keys // 2 + 32, chans), F32)
@@ -706,7 +723,7 @@
         w_kpoint,
         w_vpoint,
     )
-    first[0], mine, other = lax.optimization_barrier((first[0], mine, other))
+    *first, mine, other = lax.optimization_barrier((*first, mine, other))
 
     mine = mine + permuted(other, "row", 1)
     mine = mine.reshape(4, -1, chans)
@@ -729,6 +746,7 @@
     qpart = (first[0] + first[1]) + (first[2] + first[3])
     second = [qpart] + [around(qpart, f) for f in (3, 2, 1)]
     held = held + permuted(held, "row", 2)
+    held, *second = lax.optimization_barrier((held, *second))
     mine = jnp.concatenate([held] + [permuted(held, "row", 4 * f) for f in (1, 2, 3)], axis=0)
     other = permuted(mine, "row", 1)
     grad_q, shift_q, grad_k, shift_k = pl.pallas_call(

time: 116 us -> 95.3 us (0.82)
  the two profiles are of different devices: /device:TPU:48 before, /device:TPU:1 now
where the time goes in v2:
time: 95.3 us; the launch traced here: 95 us
  Pallas kernels  36.1 us (38%)
  starting transfers between devices  35.3 us (37%)
  waiting for transfers between devices  19.4 us (20%)
  local copies, waits for them, and re-layouts  2.69 us (3%)
    ppermute x15, starting transfers between devices, permuted(): return lax.ppermute(x, axis, [(i, i ^ flip) for i in range(size)])  23.1 us
    pallas_call x1, Pallas kernels, body(): pl.pallas_call(functools.partial(logits_kernel, heads, channels, npoint),...  12.7 us
    ppermute x6, starting transfers between devices, around(): return lax.ppermute(x, 'col', moves)  12.2 us
    ppermute x15, waiting for transfers between devices, permuted(): return lax.ppermute(x, axis, [(i, i ^ flip) for i in range(size)])  10.9 us
    ppermute x6, waiting for transfers between devices, around(): return lax.ppermute(x, 'col', moves)  8.49 us
    pallas_call x1, Pallas kernels, body(): pl.pallas_call(functools.partial(query_kernel, heads, channels, npoint),...  7.8 us
    pallas_call x1, Pallas kernels, body(): pl.pallas_call(functools.partial(key_kernel, heads, channels, npoint), ou...  6.46 us
    pallas_call x1, Pallas kernels, body(): pl.pallas_call(pair_kernel, out_shape=sds((rows, keys, depth), BF), in_sp...  4.77 us
  transfers between devices with their start and end apart: 21, of which 8 were waited for; matrix products, arithmetic and copies ran while one was open for 1% of the time, Pallas kernels for 12%

profile of v2, /device:TPU:1, one launch (start us, length us, event | category | flops | bytes accessed | tf_op | source)
XLA Modules:
  0.0 95.0 jit_solution(17577013386320886183)
XLA Ops:
  0.6 12.7 %logits.1 = (f32[1024,256]{1,0:T(8,128)}, f32[1024,256]{1,0:T(8,128)}, f32[64,384]{1,0:T(8,128)}, bf16[64,192]{1,0:T(8,128)(2,1)}, bf16[256,192]{1,0:T(8,128)(2,...) custom-call(bf16[64,256,128]{2,1,0:T(8,128)(2,1)} %pair_hbm.1, ...), custom_call_target="tpu_custom_call" | custom-call | tf_op jit(solution)/shard_map/logits/pallas_call | solution.py:615
  13.4 3.5 %collective-permute-start.2 = (f32[64,384]{1,0:T(8,128)}, f32[64,384]{1,0:T(8,128)S(1)}, u32[]{:S(2)}, u32[]{:S(2)}) collective-permute-start(f32[64,384]{1,0:T(8,128)} %get-tuple-element.44.p0_ref.own_ref), channel_id=1, source_target_pairs={{0,3},{1,2},{2,1},{3,0},{4,7},{5,6},{6,5},{7,4},{8,11},{9,10},{10,... | collective-permute-start | bytes 294920 | tf_op jit(solution)/shard_map/ppermute | solution.py:547
  17.2 1.8 %collective-permute-done.2.p3_ref = f32[64,384]{1,0:T(8,128)S(1)} collective-permute-done((f32[64,384]{1,0:T(8,128)}, f32[64,384]{1,0:T(8,128)S(1)}, u32[]{:S(2)}, u32[]{:S(2)}) %collective-permute-start.2) | collective-permute-done | bytes 98336 | tf_op jit(solution)/shard_map/ppermute | solution.py:547
  19.1 2.4 %collective-permute-done.1.p2_ref = f32[64,384]{1,0:T(8,128)S(1)} collective-permute-done((f32[64,384]{1,0:T(8,128)}, f32[64,384]{1,0:T(8,128)S(1)}, u32[]{:S(2)}, u32[]{:S(2)}) %collective-permute-start.1) | collective-permute-done | bytes 98336 | tf_op jit(solution)/shard_map/ppermute | solution.py:547
  22.2 0.6 copy-done.10
  22.8 2.2 %combine.1.psum0_ref = f32[64,384]{1,0:T(8,128)} custom-call(f32[64,384]{1,0:T(8,128)} %get-tuple-element.44.p0_ref.own_ref, f32[64,384]{1,0:T(8,128)} %copy-done.10, f32[64,384]{1,0:T(8,128)} %copy-done.9, f32[64,384]{1,0:T(8,128)} %copy-done.8), custom_call_target="tpu_custom_call" | custom-call | tf_op jit(solution)/shard_map/combine/pallas_call | solution.py:669
  25.0 5.2 %collective-permute-start.5 = (f32[64,384]{1,0:T(8,128)}, f32[64,384]{1,0:T(8,128)S(1)}, u32[]{:S(2)}, u32[]{:S(2)}) collective-permute-start(f32[64,384]{1,0:T(8,128)} %combine.1.psum0_ref), channel_id=1, source_target_pairs={{14,0},{15,1},{4,2},{5,3},{2,4},{3,5},{8,6},{9,7},{6,8},{7,9},{12,... | collective-permute-start | bytes 294920 | tf_op jit(solution)/shard_map/ppermute | solution.py:559
  30.3 1.2 %collective-permute-start.4 = (f32[64,384]{1,0:T(8,128)}, f32[64,384]{1,0:T(8,128)S(1)}, u32[]{:S(2)}, u32[]{:S(2)}) collective-permute-start(f32[64,384]{1,0:T(8,128)} %combine.1.psum0_ref), channel_id=1, source_target_pairs={{4,0},{5,1},{14,2},{15,3},{8,4},{9,5},{2,6},{3,7},{12,8},{13,9},{6... | collective-permute-start | bytes 294920 | tf_op jit(solution)/shard_map/ppermute | solution.py:559
  31.5 0.9 collective-permute-start.3
  33.0 1.9 %collective-permute-done.4.psum2_ref = f32[64,384]{1,0:T(8,128)S(1)} collective-permute-done((f32[64,384]{1,0:T(8,128)}, f32[64,384]{1,0:T(8,128)S(1)}, u32[]{:S(2)}, u32[]{:S(2)}) %collective-permute-start.4) | collective-permute-done | bytes 98336 | tf_op jit(solution)/shard_map/ppermute | solution.py:559
  34.9 3.8 %collective-permute-done.3.psum1_ref = f32[64,384]{1,0:T(8,128)S(1)} collective-permute-done((f32[64,384]{1,0:T(8,128)}, f32[64,384]{1,0:T(8,128)S(1)}, u32[]{:S(2)}, u32[]{:S(2)}) %collective-permute-start.3) | collective-permute-done | bytes 98336 | tf_op jit(solution)/shard_map/ppermute | solution.py:559
  39.4 7.8 %query_grads.1 = (f32[72,384]{1,0:T(8,128)}, bf16[64,32,256]{2,1,0:T(8,128)(2,1)}, bf16[1024,256]{1,0:T(8,128)(2,1)}, bf16[1024,256]{1,0:T(8,128)(2,1)}, f32[64,384]{1,0:T(8,128)}) custom-call(s32[3]{0:T(128)} %pad_add_fusion.place_ref, f32[1024,256]{1,0:T(8,128)} %get-tuple-element.42.expo_ref, f32[1024,256]{1,0:T(8,128)} %get-tuple-element.43.base_ref, ...), custom_call_target="tpu_custom_call" | custom-call | tf_op jit(solution)/shard_map/query_grads/pallas_call | solution.py:682
  47.1 1.1 %collective-permute-start.8 = (f32[72,384]{1,0:T(8,128)}, f32[72,384]{1,0:T(8,128)S(1)}, u32[]{:S(2)}, u32[]{:S(2)}) collective-permute-start(f32[72,384]{1,0:T(8,128)} %get-tuple-element.66), channel_id=1, source_target_pairs={{0,3},{1,2},{2,1},{3,0},{4,7},{5,6},{6,5},{7,4},{8,11},{9,10},{10,... | collective-permute-start | bytes 331784 | tf_op jit(solution)/shard_map/ppermute | solution.py:547
  48.2 1.0 %collective-permute-start.7 = (f32[72,384]{1,0:T(8,128)}, f32[72,384]{1,0:T(8,128)S(1)}, u32[]{:S(2)}, u32[]{:S(2)}) collective-permute-start(f32[72,384]{1,0:T(8,128)} %get-tuple-element.66), channel_id=1, source_target_pairs={{0,2},{1,3},{2,0},{3,1},{4,6},{5,7},{6,4},{7,5},{8,10},{9,11},{10,... | collective-permute-start | bytes 331784 | tf_op jit(solution)/shard_map/ppermute | solution.py:547
  49.9 6.5 %key_grads.1 = (f32[160,384]{1,0:T(8,128)}, f32[160,384]{1,0:T(8,128)}) custom-call(s32[3]{0:T(128)} %pad_add_fusion.place_ref, bf16[64,32,256]{2,1,0:T(8,128)(2,1)} %get-tuple-element.52.both_ref, bf16[1024,256]{1,0:T(8,128)(2,1)} %get-tuple-element.53.dlo_ref, bf16[1024,256]{1,0:T(8,128)(2,1)} %get-tuple-element.54.alo_ref, ...), custom_call_target="tpu_custom_call" | custom-call | flops 2415919104 | bytes 1048576 | tf_op jit(solution)/shard_map/key_grads/pallas_call | solution.py:699
  56.4 4.1 %collective-permute-start.9 = (f32[160,384]{1,0:T(8,128)}, f32[160,384]{1,0:T(8,128)S(1)}, u32[]{:S(2)}, u32[]{:S(2)}) collective-permute-start(f32[160,384]{1,0:T(8,128)} %get-tuple-element.62), channel_id=1, source_target_pairs={{0,16},{16,0},{32,48},{48,32},{64,80},{80,64},{96,112},{112,96},{1... | collective-permute-start | bytes 737288 | tf_op jit(solution)/shard_map/ppermute | solution.py:547
  60.5 4.8 %pair_grad.1 = bf16[64,256,128]{2,1,0:T(8,128)(2,1)} custom-call(bf16[64,32,256]{2,1,0:T(8,128)(2,1)} %get-tuple-element.52.both_ref, bf16[64,48,128]{2,1,0:T(8,128)(2,1)} %get-tuple-element.63.rhs_ref), custom_call_target="tpu_custom_call" | custom-call | flops 201326592 | bytes 4194304 | tf_op jit(solution)/shard_map/pair_grad/pallas_call | solution.py:732
  65.3 3.0 %collective-permute-start.11 = (f32[40,384]{1,0:T(8,128)S(1)}, f32[40,384]{1,0:T(8,128)S(1)}, u32[]{:S(2)}, u32[]{:S(2)}) collective-permute-start(f32[40,384]{1,0:T(8,128)S(1)} %get-tuple-element.79), channel_id=1, source_target_pairs={{0,128},{16,144},{32,160},{48,176},{64,192},{80,208},{96,224},{112... | collective-permute-start | bytes 184328 | tf_op jit(solution)/shard_map/ppermute | solution.py:547
  68.3 0.8 collective-permute-start.12
  69.1 1.4 %collective-permute-start.16 = (f32[72,384]{1,0:T(8,128)S(1)}, f32[72,384]{1,0:T(8,128)S(1)}, u32[]{:S(2)}, u32[]{:S(2)}) collective-permute-start(f32[72,384]{1,0:T(8,128)S(1)} %add_add_fusion.q0_ref), channel_id=1, source_target_pairs={{14,0},{15,1},{4,2},{5,3},{2,4},{3,5},{8,6},{9,7},{6,8},{7,9},{12,... | collective-permute-start | bytes 331784 | tf_op jit(solution)/shard_map/ppermute | solution.py:559
  70.5 2.2 %collective-permute-start.15 = (f32[72,384]{1,0:T(8,128)S(1)}, f32[72,384]{1,0:T(8,128)S(1)}, u32[]{:S(2)}, u32[]{:S(2)}) collective-permute-start(f32[72,384]{1,0:T(8,128)S(1)} %add_add_fusion.q0_ref), channel_id=1, source_target_pairs={{4,0},{5,1},{14,2},{15,3},{8,4},{9,5},{2,6},{3,7},{12,8},{13,9},{6... | collective-permute-start | bytes 331784 | tf_op jit(solution)/shard_map/ppermute | solution.py:559
  72.7 1.3 %collective-permute-start.14 = (f32[72,384]{1,0:T(8,128)S(1)}, f32[72,384]{1,0:T(8,128)S(1)}, u32[]{:S(2)}, u32[]{:S(2)}) collective-permute-start(f32[72,384]{1,0:T(8,128)S(1)} %add_add_fusion.q0_ref), channel_id=1, source_target_pairs={{10,0},{11,1},{8,2},{9,3},{14,4},{15,5},{12,6},{13,7},{2,8},{3,9},... | collective-permute-start | bytes 331784 | tf_op jit(solution)/shard_map/ppermute | solution.py:559
  74.0 2.5 %collective-permute-start.13 = (f32[40,384]{1,0:T(8,128)S(1)}, f32[40,384]{1,0:T(8,128)S(1)}, u32[]{:S(2)}, u32[]{:S(2)}) collective-permute-start(f32[40,384]{1,0:T(8,128)S(1)} %slice_add_fusion), channel_id=1, source_target_pairs={{0,32},{16,48},{32,0},{48,16},{64,96},{80,112},{96,64},{112,80},{1... | collective-permute-start | bytes 184328 | tf_op jit(solution)/shard_map/ppermute | solution.py:547
  76.6 2.1 %collective-permute-done.13 = f32[40,384]{1,0:T(8,128)S(1)} collective-permute-done((f32[40,384]{1,0:T(8,128)S(1)}, f32[40,384]{1,0:T(8,128)S(1)}, u32[]{:S(2)}, u32[]{:S(2)}) %collective-permute-start.13) | collective-permute-done | bytes 61472 | tf_op jit(solution)/shard_map/ppermute | solution.py:547
  78.7 2.7 %collective-permute-done.14.q1_ref = f32[72,384]{1,0:T(8,128)S(1)} collective-permute-done((f32[72,384]{1,0:T(8,128)S(1)}, f32[72,384]{1,0:T(8,128)S(1)}, u32[]{:S(2)}, u32[]{:S(2)}) %collective-permute-start.14) | collective-permute-done | bytes 110624 | tf_op jit(solution)/shard_map/ppermute | solution.py:559
  81.5 1.5 %collective-permute-start.19 = (f32[40,384]{1,0:T(8,128)S(1)}, f32[40,384]{1,0:T(8,128)S(1)}, u32[]{:S(2)}, u32[]{:S(2)}) collective-permute-start(f32[40,384]{1,0:T(8,128)S(1)} %add.34), channel_id=1, source_target_pairs={{0,192},{16,208},{32,224},{48,240},{64,128},{80,144},{96,160},{112... | collective-permute-start | bytes 184328 | tf_op jit(solution)/shard_map/ppermute | solution.py:547
  82.9 1.7 %collective-permute-start.18 = (f32[40,384]{1,0:T(8,128)S(1)}, f32[40,384]{1,0:T(8,128)S(1)}, u32[]{:S(2)}, u32[]{:S(2)}) collective-permute-start(f32[40,384]{1,0:T(8,128)S(1)} %add.34), channel_id=1, source_target_pairs={{0,128},{16,144},{32,160},{48,176},{64,192},{80,208},{96,224},{112... | collective-permute-start | bytes 184328 | tf_op jit(solution)/shard_map/ppermute | solution.py:547
  84.7 3.4 %collective-permute-done.17 = f32[40,384]{1,0:T(8,128)S(1)} collective-permute-done((f32[40,384]{1,0:T(8,128)S(1)}, f32[40,384]{1,0:T(8,128)S(1)}, u32[]{:S(2)}, u32[]{:S(2)}) %collective-permute-start.17) | collective-permute-done | bytes 61472 | tf_op jit(solution)/shard_map/ppermute | solution.py:547
  88.2 2.9 %collective-permute-start.20 = (f32[160,384]{1,0:T(8,128)S(1)}, f32[160,384]{1,0:T(8,128)S(1)}, u32[]{:S(2)}, u32[]{:S(2)}) collective-permute-start(f32[160,384]{1,0:T(8,128)S(1)} %constant_dynamic-update-slice_fusion.mine_ref), channel_id=1, source_target_pairs={{0,16},{16,0},{32,48},{48,32},{64,80},{80,64},{96,112},{112,96},{1... | collective-permute-start | bytes 737288 | tf_op jit(solution)/shard_map/ppermute | solution.py:547
  91.1 1.1 %collective-permute-done.20.other_ref = f32[160,384]{1,0:T(8,128)S(1)} collective-permute-done((f32[160,384]{1,0:T(8,128)S(1)}, f32[160,384]{1,0:T(8,128)S(1)}, u32[]{:S(2)}, u32[]{:S(2)}) %collective-permute-start.20) | collective-permute-done | bytes 245792 | tf_op jit(solution)/shard_map/ppermute | solution.py:547
  92.2 0.7 copy-done.3
  92.9 2.1 %finish.1 = (bf16[64,384]{1,0:T(8,128)(2,1)}, f32[3,64]{1,0:T(4,128)}, bf16[256,384]{1,0:T(8,128)(2,1)}, f32[3,256]{1,0:T(4,128)}) custom-call(s32[3]{0:T(128)} %pad_add_fusion.place_ref, f32[72,384]{1,0:T(8,128)} %copy-done, f32[72,384]{1,0:T(8,128)} %copy-done.6, f32[72,384]{1,0:T(8,128)} %copy-done.5, f32[72,384]{1,0:T(8,128)} %copy-done.4, ...), custom_call_target="tpu_custom_call" | custom-call | tf_op jit(solution)/shard_map/finish/pallas_call | solution.py:752
  (54 shorter events, 3.1 us)
Async XLA Ops:
  13.4 5.7 %collective-permute-start.2 = (f32[64,384]{1,0:T(8,128)}, f32[64,384]{1,0:T(8,128)S(1)}, u32[]{:S(2)}, u32[]{:S(2)}) collective-permute-start(f32[64,384]{1,0:T(8,128)} %get-tuple-element.44.p0_ref.own_ref), channel_id=1, source_target_pairs={{0,3},{1,2},{2,1},{3,0},{4,7},{5,6},{6,5},{7,4},{8,11},{9,10},{10,... | collective-permute-start | bytes 294920 | tf_op jit(solution)/shard_map/ppermute | solution.py:547
  16.9 4.7 %collective-permute-start.1 = (f32[64,384]{1,0:T(8,128)}, f32[64,384]{1,0:T(8,128)S(1)}, u32[]{:S(2)}, u32[]{:S(2)}) collective-permute-start(f32[64,384]{1,0:T(8,128)} %get-tuple-element.44.p0_ref.own_ref), channel_id=1, source_target_pairs={{0,2},{1,3},{2,0},{3,1},{4,6},{5,7},{6,4},{7,5},{8,10},{9,11},{10,... | collective-permute-start | bytes 294920 | tf_op jit(solution)/shard_map/ppermute | solution.py:547
  16.9 4.7 %collective-permute-start = (f32[64,384]{1,0:T(8,128)}, f32[64,384]{1,0:T(8,128)S(1)}, u32[]{:S(2)}, u32[]{:S(2)}) collective-permute-start(f32[64,384]{1,0:T(8,128)} %get-tuple-element.44.p0_ref.own_ref), channel_id=1, source_target_pairs={{0,1},{1,0},{2,3},{3,2},{4,5},{5,4},{6,7},{7,6},{8,9},{9,8},{10,11... | collective-permute-start | bytes 294920 | tf_op jit(solution)/shard_map/ppermute | solution.py:547
  19.1 2.5 %copy-start.8 = (f32[64,384]{1,0:T(8,128)}, f32[64,384]{1,0:T(8,128)S(1)}, u32[]{:S(2)}) copy-start(f32[64,384]{1,0:T(8,128)S(1)} %collective-permute-done.2.p3_ref) | copy-start | bytes 294916
  25.0 7.9 %collective-permute-start.5 = (f32[64,384]{1,0:T(8,128)}, f32[64,384]{1,0:T(8,128)S(1)}, u32[]{:S(2)}, u32[]{:S(2)}) collective-permute-start(f32[64,384]{1,0:T(8,128)} %combine.1.psum0_ref), channel_id=1, source_target_pairs={{14,0},{15,1},{4,2},{5,3},{2,4},{3,5},{8,6},{9,7},{6,8},{7,9},{12,... | collective-permute-start | bytes 294920 | tf_op jit(solution)/shard_map/ppermute | solution.py:559
  30.3 4.6 %collective-permute-start.4 = (f32[64,384]{1,0:T(8,128)}, f32[64,384]{1,0:T(8,128)S(1)}, u32[]{:S(2)}, u32[]{:S(2)}) collective-permute-start(f32[64,384]{1,0:T(8,128)} %combine.1.psum0_ref), channel_id=1, source_target_pairs={{4,0},{5,1},{14,2},{15,3},{8,4},{9,5},{2,6},{3,7},{12,8},{13,9},{6... | collective-permute-start | bytes 294920 | tf_op jit(solution)/shard_map/ppermute | solution.py:559
  31.5 7.2 %collective-permute-start.3 = (f32[64,384]{1,0:T(8,128)}, f32[64,384]{1,0:T(8,128)S(1)}, u32[]{:S(2)}, u32[]{:S(2)}) collective-permute-start(f32[64,384]{1,0:T(8,128)} %combine.1.psum0_ref), channel_id=1, source_target_pairs={{10,0},{11,1},{8,2},{9,3},{14,4},{15,5},{12,6},{13,7},{2,8},{3,9},... | collective-permute-start | bytes 294920 | tf_op jit(solution)/shard_map/ppermute | solution.py:559
  33.0 5.8 %copy-start.11 = (f32[64,384]{1,0:T(8,128)}, f32[64,384]{1,0:T(8,128)S(1)}, u32[]{:S(2)}) copy-start(f32[64,384]{1,0:T(8,128)S(1)} %collective-permute-done.5.psum3_ref) | copy-start | bytes 294916
  34.9 3.8 %copy-start.12 = (f32[64,384]{1,0:T(8,128)}, f32[64,384]{1,0:T(8,128)S(1)}, u32[]{:S(2)}) copy-start(f32[64,384]{1,0:T(8,128)S(1)} %collective-permute-done.4.psum2_ref) | copy-start | bytes 294916
  47.1 9.2 %collective-permute-start.8 = (f32[72,384]{1,0:T(8,128)}, f32[72,384]{1,0:T(8,128)S(1)}, u32[]{:S(2)}, u32[]{:S(2)}) collective-permute-start(f32[72,384]{1,0:T(8,128)} %get-tuple-element.66), channel_id=1, source_target_pairs={{0,3},{1,2},{2,1},{3,0},{4,7},{5,6},{6,5},{7,4},{8,11},{9,10},{10,... | collective-permute-start | bytes 331784 | tf_op jit(solution)/shard_map/ppermute | solution.py:547
  48.2 8.1 %collective-permute-start.7 = (f32[72,384]{1,0:T(8,128)}, f32[72,384]{1,0:T(8,128)S(1)}, u32[]{:S(2)}, u32[]{:S(2)}) collective-permute-start(f32[72,384]{1,0:T(8,128)} %get-tuple-element.66), channel_id=1, source_target_pairs={{0,2},{1,3},{2,0},{3,1},{4,6},{5,7},{6,4},{7,5},{8,10},{9,11},{10,... | collective-permute-start | bytes 331784 | tf_op jit(solution)/shard_map/ppermute | solution.py:547
  49.3 7.1 %collective-permute-start.6 = (f32[72,384]{1,0:T(8,128)}, f32[72,384]{1,0:T(8,128)S(1)}, u32[]{:S(2)}, u32[]{:S(2)}) collective-permute-start(f32[72,384]{1,0:T(8,128)} %get-tuple-element.66), channel_id=1, source_target_pairs={{0,1},{1,0},{2,3},{3,2},{4,5},{5,4},{6,7},{7,6},{8,9},{9,8},{10,11... | collective-permute-start | bytes 331784 | tf_op jit(solution)/shard_map/ppermute | solution.py:547
  56.3 8.9 %copy-start.2 = (f32[160,384]{1,0:T(8,128)S(1)}, f32[160,384]{1,0:T(8,128)}, u32[]{:S(2)}) copy-start(f32[160,384]{1,0:T(8,128)} %get-tuple-element.61) | copy-start | bytes 737284
  56.3 12.8 %copy-start.7 = (f32[72,384]{1,0:T(8,128)S(1)}, f32[72,384]{1,0:T(8,128)}, u32[]{:S(2)}) copy-start(f32[72,384]{1,0:T(8,128)} %get-tuple-element.66) | copy-start | bytes 331780
  56.4 8.9 %collective-permute-start.9 = (f32[160,384]{1,0:T(8,128)}, f32[160,384]{1,0:T(8,128)S(1)}, u32[]{:S(2)}, u32[]{:S(2)}) collective-permute-start(f32[160,384]{1,0:T(8,128)} %get-tuple-element.62), channel_id=1, source_target_pairs={{0,16},{16,0},{32,48},{48,32},{64,80},{80,64},{96,112},{112,96},{1... | collective-permute-start | bytes 737288 | tf_op jit(solution)/shard_map/ppermute | solution.py:547
  65.3 7.4 %collective-permute-start.11 = (f32[40,384]{1,0:T(8,128)S(1)}, f32[40,384]{1,0:T(8,128)S(1)}, u32[]{:S(2)}, u32[]{:S(2)}) collective-permute-start(f32[40,384]{1,0:T(8,128)S(1)} %get-tuple-element.79), channel_id=1, source_target_pairs={{0,128},{16,144},{32,160},{48,176},{64,192},{80,208},{96,224},{112... | collective-permute-start | bytes 184328 | tf_op jit(solution)/shard_map/ppermute | solution.py:547
  68.3 5.7 %collective-permute-start.12 = (f32[40,384]{1,0:T(8,128)S(1)}, f32[40,384]{1,0:T(8,128)S(1)}, u32[]{:S(2)}, u32[]{:S(2)}) collective-permute-start(f32[40,384]{1,0:T(8,128)S(1)} %get-tuple-element.80), channel_id=1, source_target_pairs={{0,192},{16,208},{32,224},{48,240},{64,128},{80,144},{96,160},{112... | collective-permute-start | bytes 184328 | tf_op jit(solution)/shard_map/ppermute | solution.py:547
  69.1 4.9 %collective-permute-start.10 = (f32[40,384]{1,0:T(8,128)S(1)}, f32[40,384]{1,0:T(8,128)S(1)}, u32[]{:S(2)}, u32[]{:S(2)}) collective-permute-start(f32[40,384]{1,0:T(8,128)S(1)} %get-tuple-element.81), channel_id=1, source_target_pairs={{0,64},{16,80},{32,96},{48,112},{64,0},{80,16},{96,32},{112,48},{1... | collective-permute-start | bytes 184328 | tf_op jit(solution)/shard_map/ppermute | solution.py:547
  69.1 23.1 %copy-start = (f32[72,384]{1,0:T(8,128)}, f32[72,384]{1,0:T(8,128)S(1)}, u32[]{:S(2)}) copy-start(f32[72,384]{1,0:T(8,128)S(1)} %add_add_fusion.q0_ref) | copy-start | bytes 331780
  69.1 9.6 %collective-permute-start.16 = (f32[72,384]{1,0:T(8,128)S(1)}, f32[72,384]{1,0:T(8,128)S(1)}, u32[]{:S(2)}, u32[]{:S(2)}) collective-permute-start(f32[72,384]{1,0:T(8,128)S(1)} %add_add_fusion.q0_ref), channel_id=1, source_target_pairs={{14,0},{15,1},{4,2},{5,3},{2,4},{3,5},{8,6},{9,7},{6,8},{7,9},{12,... | collective-permute-start | bytes 331784 | tf_op jit(solution)/shard_map/ppermute | solution.py:559
  70.5 8.2 %collective-permute-start.15 = (f32[72,384]{1,0:T(8,128)S(1)}, f32[72,384]{1,0:T(8,128)S(1)}, u32[]{:S(2)}, u32[]{:S(2)}) collective-permute-start(f32[72,384]{1,0:T(8,128)S(1)} %add_add_fusion.q0_ref), channel_id=1, source_target_pairs={{4,0},{5,1},{14,2},{15,3},{8,4},{9,5},{2,6},{3,7},{12,8},{13,9},{6... | collective-permute-start | bytes 331784 | tf_op jit(solution)/shard_map/ppermute | solution.py:559
  72.7 8.7 %collective-permute-start.14 = (f32[72,384]{1,0:T(8,128)S(1)}, f32[72,384]{1,0:T(8,128)S(1)}, u32[]{:S(2)}, u32[]{:S(2)}) collective-permute-start(f32[72,384]{1,0:T(8,128)S(1)} %add_add_fusion.q0_ref), channel_id=1, source_target_pairs={{10,0},{11,1},{8,2},{9,3},{14,4},{15,5},{12,6},{13,7},{2,8},{3,9},... | collective-permute-start | bytes 331784 | tf_op jit(solution)/shard_map/ppermute | solution.py:559
  74.0 4.7 %collective-permute-start.13 = (f32[40,384]{1,0:T(8,128)S(1)}, f32[40,384]{1,0:T(8,128)S(1)}, u32[]{:S(2)}, u32[]{:S(2)}) collective-permute-start(f32[40,384]{1,0:T(8,128)S(1)} %slice_add_fusion), channel_id=1, source_target_pairs={{0,32},{16,48},{32,0},{48,16},{64,96},{80,112},{96,64},{112,80},{1... | collective-permute-start | bytes 184328 | tf_op jit(solution)/shard_map/ppermute | solution.py:547
  78.7 13.5 %copy-start.4 = (f32[72,384]{1,0:T(8,128)}, f32[72,384]{1,0:T(8,128)S(1)}, u32[]{:S(2)}) copy-start(f32[72,384]{1,0:T(8,128)S(1)} %collective-permute-done.16.q3_ref) | copy-start | bytes 331780
  78.7 13.5 %copy-start.5 = (f32[72,384]{1,0:T(8,128)}, f32[72,384]{1,0:T(8,128)S(1)}, u32[]{:S(2)}) copy-start(f32[72,384]{1,0:T(8,128)S(1)} %collective-permute-done.15.q2_ref) | copy-start | bytes 331780
  81.5 10.7 %copy-start.6 = (f32[72,384]{1,0:T(8,128)}, f32[72,384]{1,0:T(8,128)S(1)}, u32[]{:S(2)}) copy-start(f32[72,384]{1,0:T(8,128)S(1)} %collective-permute-done.14.q1_ref) | copy-start | bytes 331780
  81.5 6.7 %collective-permute-start.19 = (f32[40,384]{1,0:T(8,128)S(1)}, f32[40,384]{1,0:T(8,128)S(1)}, u32[]{:S(2)}, u32[]{:S(2)}) collective-permute-start(f32[40,384]{1,0:T(8,128)S(1)} %add.34), channel_id=1, source_target_pairs={{0,192},{16,208},{32,224},{48,240},{64,128},{80,144},{96,160},{112... | collective-permute-start | bytes 184328 | tf_op jit(solution)/shard_map/ppermute | solution.py:547
  82.9 5.2 %collective-permute-start.18 = (f32[40,384]{1,0:T(8,128)S(1)}, f32[40,384]{1,0:T(8,128)S(1)}, u32[]{:S(2)}, u32[]{:S(2)}) collective-permute-start(f32[40,384]{1,0:T(8,128)S(1)} %add.34), channel_id=1, source_target_pairs={{0,128},{16,144},{32,160},{48,176},{64,192},{80,208},{96,224},{112... | collective-permute-start | bytes 184328 | tf_op jit(solution)/shard_map/ppermute | solution.py:547
  84.6 3.5 %collective-permute-start.17 = (f32[40,384]{1,0:T(8,128)S(1)}, f32[40,384]{1,0:T(8,128)S(1)}, u32[]{:S(2)}, u32[]{:S(2)}) collective-permute-start(f32[40,384]{1,0:T(8,128)S(1)} %add.34), channel_id=1, source_target_pairs={{0,64},{16,80},{32,96},{48,112},{64,0},{80,16},{96,32},{112,48},{1... | collective-permute-start | bytes 184328 | tf_op jit(solution)/shard_map/ppermute | solution.py:547
  88.2 4.0 %copy-start.1 = (f32[160,384]{1,0:T(8,128)}, f32[160,384]{1,0:T(8,128)S(1)}, u32[]{:S(2)}) copy-start(f32[160,384]{1,0:T(8,128)S(1)} %constant_dynamic-update-slice_fusion.mine_ref) | copy-start | bytes 737284
  88.2 4.0 %collective-permute-start.20 = (f32[160,384]{1,0:T(8,128)S(1)}, f32[160,384]{1,0:T(8,128)S(1)}, u32[]{:S(2)}, u32[]{:S(2)}) collective-permute-start(f32[160,384]{1,0:T(8,128)S(1)} %constant_dynamic-update-slice_fusion.mine_ref), channel_id=1, source_target_pairs={{0,16},{16,0},{32,48},{48,32},{64,80},{80,64},{96,112},{112,96},{1... | collective-permute-start | bytes 737288 | tf_op jit(solution)/shard_map/ppermute | solution.py:547
  92.2 0.7 copy-start.3
  (3 other events, 1.9 us)

commit v3 on v1

--- a/solution.py
+++ b/solution.py
@@ -14,7 +14,7 @@
 HP = 16
 LANE = 128
 NEG = -1e30
-LIMIT = 56 * 1024 * 1024
+LIMIT = 24 * 1024 * 1024
 
 
 def nn(a, b, precision=None):
@@ -99,6 +99,25 @@
 def back_rotate(x, cols):
     parts = [x[:, a * LANE : (a + 1) * LANE] for a in range(3)]
     return [sum(cols[:, 3 * a + b : 3 * a + b + 1] * parts[a] for a in range(3)) for b in range(3)]
+
+
+def load_pair(pair_hbm, pair_ref, sems):
+    nchunk = sems.shape[0]
+    step = pair_hbm.shape[0] // nchunk
+    copies = [
+        pltpu.make_async_copy(
+            pair_hbm.at[pl.ds(c * step, step)], pair_ref.at[pl.ds(c * step, step)], sems.at[c]
+        )
+        for c in range(nchunk)
+    ]
+    for copy in copies:
+        copy.start()
+    return copies, step
+
+
+def padded_bias(wb_ref):
+    heads, depth = wb_ref.shape
+    return jnp.concatenate([wb_ref[...].astype(F32), jnp.zeros((HP - heads, depth), F32)], axis=0)
 
 
 def logits_kernel(
@@ -110,12 +129,9 @@
     sk_ref,
     wq_ref,
     wk_ref,
-    wv_ref,
     wqp_ref,
     wkp_ref,
-    wvp_ref,
     wb_ref,
-    wout_ref,
     gamma_ref,
     chainb_ref,
     rotq_ref,
@@ -125,40 +141,22 @@
     cq_ref,
     ck_ref,
     km_ref,
-    cot_ref,
     masked_ref,
-    base_ref,
     stats_ref,
     query_ref,
     key_ref,
-    value_ref,
     gq_ref,
     gk_ref,
-    gv_ref,
-    dos_ref,
-    dpt_ref,
-    rhs_ref,
     qcol_ref,
     kcol_ref,
     pair_ref,
-    lhs_ref,
     tq_ref,
     tk_ref,
     sems,
 ):
     rows, keys, depth = pair_hbm.shape
     hp = heads * npoint
-    nchunk = sems.shape[0]
-    step = rows // nchunk
-    copies = [
-        pltpu.make_async_copy(
-            pair_hbm.at[pl.ds(c * step, step)], pair_ref.at[pl.ds(c * step, step)], sems.at[c]
-        )
-        for c in range(nchunk)
-    ]
-    for copy in copies:
-        copy.start()
-
+    copies, step = load_pair(pair_hbm, pair_ref, sems)
     w_logit = math.sqrt(1.0 / 3.0)
     w_point = math.sqrt(2.0 / (9.0 * npoint))
     tq_ref[...] = jnp.zeros_like(tq_ref)
@@ -179,49 +177,22 @@
 
     sq = sq_ref[...]
     sk = sk_ref[...]
-    cot = cot_ref[...]
     query = nt(sq, wq_ref[...]).astype(BF)
     key = nt(sk, wk_ref[...]).astype(BF)
     query_ref[...] = query
     key_ref[...] = key
-    value_ref[...] = nt(sk, wv_ref[...]).astype(BF)
     gq = rotate_points(nt(sq, wqp_ref[...]), qcols, hp)
     gk = rotate_points(nt(sk, wkp_ref[...]), kcols, hp)
     gq_ref[...] = gq
     gk_ref[...] = gk
-    gv_ref[...] = rotate_points(nt(sk, wvp_ref[...]), kcols, hp)
-
-    nos = heads * channels
-    first = nos + heads * depth
-    dos_ref[...] = nt(cot, wout_ref[0:nos, :]).astype(BF)
-    for b in range(4):
-        d = nt(cot, wout_ref[first + b * hp : first + (b + 1) * hp, :]).astype(BF).astype(F32)
-        dpt_ref[:, b * LANE : (b + 1) * LANE] = pad_lanes(d)
-    doz = nt(cot, wout_ref[nos:first, :]).astype(BF).astype(F32)
-    wbt = jnp.concatenate(
-        [wb_ref[...].astype(F32), jnp.zeros((HP - heads, depth), F32)], axis=0
-    )
-    wb_wide = jnp.broadcast_to(wbt[None], (rows, HP, depth))
-    lhs_ref[...] = jnp.zeros_like(lhs_ref)
-    for h in range(heads):
-        lhs_ref[pl.ds(HP + h, rows, stride=2 * HP), :] = doz[:, h * depth : (h + 1) * depth]
-    lhs3 = lhs_ref[...].reshape(rows, 2 * HP, depth)
-    doz_b = lhs3[:, HP:, :]
-    whi, wlo = split(w_logit * wb_wide)
-    rhs_ref[:, 0:HP, :] = whi
-    rhs_ref[:, HP : 2 * HP, :] = wlo
-    rhs_ref[:, 2 * HP : 3 * HP, :] = doz_b.astype(BF)
-    lhs_ref[...] = jnp.concatenate([wb_wide, doz_b], axis=1).reshape(rows * 2 * HP, depth)
-
-    for c in range(nchunk):
-        copies[c].wait()
+
+    wbt = padded_bias(wb_ref).astype(BF)
+    for c, copy in enumerate(copies):
+        copy.wait()
 
         def one(i, carry):
-            r = pl.multiple_of(i * 2 * HP, 2 * HP)
-            g = nt(lhs_ref[pl.ds(r, 2 * HP), :].astype(BF), pair_ref[i])
             r = pl.multiple_of(i * HP, HP)
-            masked_ref[pl.ds(r, HP), :] = g[:HP]
-            base_ref[pl.ds(r, HP), :] = g[HP:]
+            masked_ref[pl.ds(r, HP), :] = nt(wbt, pair_ref[i])
             return carry
 
         lax.fori_loop(c * step, (c + 1) * step, one, 0, unroll=8)
@@ -250,8 +221,58 @@
     masked_ref[...] = masked.reshape(rows * HP, keys)
     packed = to_lanes(top.reshape(rows * HP, 1)) + to_lanes(total.reshape(rows * HP, 1), HP)
     stats_ref[...] = packed.T[: 2 * HP]
-    dosm = spread(dos_ref[...].astype(F32), cmask).astype(BF)
-    base_ref[...] += nt(dosm, value_ref[...])
+
+
+def base_kernel(
+    heads,
+    channels,
+    npoint,
+    pair_hbm,
+    sk_ref,
+    cot_ref,
+    wv_ref,
+    wvp_ref,
+    wout_ref,
+    kcol_ref,
+    base_ref,
+    gv_ref,
+    dos_ref,
+    dpt_ref,
+    doz_ref,
+    pair_ref,
+    lhs_ref,
+    sems,
+):
+    rows, keys, depth = pair_hbm.shape
+    hp = heads * npoint
+    copies, step = load_pair(pair_hbm, pair_ref, sems)
+    sk = sk_ref[...]
+    cot = cot_ref[...]
+    value = nt(sk, wv_ref[...]).astype(BF)
+    gv_ref[...] = rotate_points(nt(sk, wvp_ref[...]), kcol_ref[...], hp)
+    nos = heads * channels
+    first = nos + heads * depth
+    dos = nt(cot, wout_ref[0:nos, :]).astype(BF)
+    dos_ref[...] = dos
+    for b in range(4):
+        d = nt(cot, wout_ref[first + b * hp : first + (b + 1) * hp, :]).astype(BF).astype(F32)
+        dpt_ref[:, b * LANE : (b + 1) * LANE] = pad_lanes(d)
+    doz = nt(cot, wout_ref[nos:first, :]).astype(BF).astype(F32)
+    lhs_ref[...] = jnp.zeros_like(lhs_ref)
+    for h in range(heads):
+        lhs_ref[pl.ds(h, rows, stride=HP), :] = doz[:, h * depth : (h + 1) * depth]
+    doz_ref[...] = lhs_ref[...].astype(BF)
+    dosm = spread(dos.astype(F32), channel_mask(heads, channels)).astype(BF)
+    base_ref[...] = nt(dosm, value)
+    for c, copy in enumerate(copies):
+        copy.wait()
+
+        def one(i, carry):
+            r = pl.multiple_of(i * HP, HP)
+            base_ref[pl.ds(r, HP), :] += nt(doz_ref[pl.ds(r, HP), :], pair_ref[i])
+            return carry
+
+        lax.fori_loop(c * step, (c + 1) * step, one, 0, unroll=8)
 
 
 def attend_kernel(heads, npoint, masked_ref, base_ref, km_ref, stats_ref, gv_ref, attn_ref, out_ref):
@@ -503,16 +524,50 @@
     shiftk_ref[...] = shift_ref[0:3, :]
 
 
-def pair_kernel(both_ref, rhs_ref, out_ref):
+def pair_kernel(both_ref, doz_ref, wb_ref, *refs):
+    out_ref = refs[-1]
     rows = both_ref.shape[0]
+    whi, wlo = split(math.sqrt(1.0 / 3.0) * padded_bias(wb_ref))
 
     def one(i, carry):
         both = both_ref[i]
-        left = jnp.concatenate([both[:HP], both[:HP], both[HP:]], axis=0)
-        out_ref[i] = tn(left, rhs_ref[i]).astype(BF)
+        left = jnp.concatenate([both[:HP], both], axis=0)
+        doz = doz_ref[pl.ds(pl.multiple_of(i * HP, HP), HP), :]
+        right = jnp.concatenate([wlo, whi, doz], axis=0)
+        out_ref[i] = tn(left, right).astype(BF)
         return carry
 
     lax.fori_loop(0, rows, one, 0, unroll=True)
+
+
+def pair_part(part, parts, both, doz, w_bias, before, params):
+    rows, _, keys = both.shape
+    depth = doz.shape[1]
+    step = rows // parts
+    specs = [
+        pl.BlockSpec((step, 2 * HP, keys), lambda g: (part, 0, 0)),
+        pl.BlockSpec((step * HP, depth), lambda g: (part, 0)),
+        pl.BlockSpec(w_bias.shape, lambda g: (0, 0)),
+    ]
+    operands = [both, doz, w_bias]
+    if before is not None:
+        specs.append(pl.BlockSpec(memory_space=pl.ANY))
+        operands.append(before)
+    return pl.pallas_call(
+        pair_kernel,
+        grid=(1,),
+        out_shape=jax.ShapeDtypeStruct((rows, keys, depth), BF),
+        in_specs=specs,
+        out_specs=pl.BlockSpec((step, keys, depth), lambda g: (part, 0, 0)),
+        input_output_aliases={} if before is None else {3: 0},
+        compiler_params=params,
+        name="pair_grad",
+        cost_estimate=pl.CostEstimate(
+            flops=2 * step * keys * depth * 3 * HP,
+            bytes_accessed=2 * step * keys * depth,
+            transcendentals=0,
+        ),
+    )(*operands)
 
 
 def permuted(x, axis, flip):
@@ -576,44 +631,22 @@
     w_query, w_key, w_value = w_query.T, w_key.T, w_value.T
     w_qpoint, w_kpoint, w_vpoint = w_qpoint.T, w_kpoint.T, w_vpoint.T
     w_bias = w_bias.T
-    (
-        masked,
-        base,
-        stats,
-        query,
-        key,
-        value,
-        gq,
-        gk,
-        gv,
-        d_os,
-        d_pt,
-        rhs,
-        qcol,
-        kcol,
-    ) = pl.pallas_call(
+    masked, stats, query, key, gq, gk, qcol, kcol = pl.pallas_call(
         functools.partial(logits_kernel, heads, channels, npoint),
         out_shape=[
-            sds((n, keys), F32),
             sds((n, keys), F32),
             sds((2 * HP, rows), F32),
             sds((rows, hc), BF),
             sds((keys, hc), BF),
-            sds((keys, hc), BF),
             sds((rows, wide), F32),
             sds((keys, wide), F32),
-            sds((keys, wide), F32),
-            sds((rows, hc), BF),
-            sds((rows, 4 * LANE), F32),
-            sds((rows, 3 * HP, depth), BF),
             sds((LANE, LANE), F32),
             sds((keys, LANE), F32),
         ],
-        in_specs=[pl.BlockSpec(memory_space=pl.ANY)] + [vmem] * 20,
-        out_specs=[vmem] * 14,
+        in_specs=[pl.BlockSpec(memory_space=pl.ANY)] + [vmem] * 16,
+        out_specs=[vmem] * 8,
         scratch_shapes=[
             pltpu.VMEM((rows, keys, depth), BF),
-            pltpu.VMEM((rows * 2 * HP, depth), F32),
             pltpu.VMEM((LANE, LANE), F32),
             pltpu.VMEM((LANE, keys), F32),
             pltpu.SemaphoreType.DMA((4,)),
@@ -626,12 +659,9 @@
         single_k,
         w_query,
         w_key,
-        w_value,
         w_qpoint,
         w_kpoint,
-        w_vpoint,
         w_bias,
-        w_out,
         head_gamma.reshape(1, heads),
         chain_bias.reshape(1, heads),
         rot_q,
@@ -641,11 +671,32 @@
         chain_q.reshape(1, rows),
         chain_k.reshape(1, keys),
         km,
-        cotangent,
-    )
-
-    parts = [stats] + [permuted(stats, "col", f) for f in (1, 2, 3)]
-    stats = merged(parts)
+    )
+
+    first = [stats] + [permuted(stats, "col", f) for f in (1, 2, 3)]
+    base, gv, d_os, d_pt, doz = pl.pallas_call(
+        functools.partial(base_kernel, heads, channels, npoint),
+        out_shape=[
+            sds((n, keys), F32),
+            sds((keys, wide), F32),
+            sds((rows, hc), BF),
+            sds((rows, 4 * LANE), F32),
+            sds((n, depth), BF),
+        ],
+        in_specs=[pl.BlockSpec(memory_space=pl.ANY)] + [vmem] * 6,
+        out_specs=[vmem] * 5,
+        scratch_shapes=[
+            pltpu.VMEM((rows, keys, depth), BF),
+            pltpu.VMEM((n, depth), F32),
+            pltpu.SemaphoreType.DMA((4,)),
+        ],
+        compiler_params=params,
+        name="base",
+        cost_estimate=pl.CostEstimate(
+            flops=8 * n * keys * wide, bytes_accessed=4 * rows * keys * depth, transcendentals=0
+        ),
+    )(pair, single_k, cotangent, w_value, w_vpoint, w_out, kcol)
+    stats = merged(first)
     stats = merged([stats] + [around(stats, f) for f in (3, 2, 1)])
 
     attn, points = pl.pallas_call(
@@ -657,7 +708,7 @@
         name="attend",
     )(masked, base, km, stats, gv)
     points = points + sum(permuted(points, "col", f) for f in (1, 2, 3))
-    parts = [points] + [around(points, f) for f in (3, 2, 1)]
+    parts = [points] + [around(points, f) for f in (1, 2, 3)]
 
     me = lax.axis_index("row")
     place = jnp.stack([lax.axis_index("col"), me % 2, me // 4]).astype(jnp.int32)
@@ -706,29 +757,19 @@
         w_kpoint,
         w_vpoint,
     )
-    first[0], mine, other = lax.optimization_barrier((first[0], mine, other))
+    *first, mine, other = lax.optimization_barrier((*first, mine, other))
 
     mine = mine + permuted(other, "row", 1)
+    mine, both = lax.optimization_barrier((mine, both))
     mine = mine.reshape(4, -1, chans)
     held = mine[0] + sum(permuted(mine[f], "row", 4 * f) for f in (1, 2, 3))
-
-    pair_grad = pl.pallas_call(
-        pair_kernel,
-        out_shape=sds((rows, keys, depth), BF),
-        in_specs=[vmem] * 2,
-        out_specs=vmem,
-        compiler_params=params,
-        name="pair_grad",
-        cost_estimate=pl.CostEstimate(
-            flops=2 * rows * keys * depth * 3 * HP,
-            bytes_accessed=2 * rows * keys * depth,
-            transcendentals=0,
-        ),
-    )(both, rhs)
-    held, pair_grad = lax.optimization_barrier((held, pair_grad))
+    pair_grad = pair_part(0, 2, both, doz, w_bias, None, params)
+    held, both, pair_grad = lax.optimization_barrier((held, both, pair_grad))
     qpart = (first[0] + first[1]) + (first[2] + first[3])
-    second = [qpart] + [around(qpart, f) for f in (3, 2, 1)]
+    second = [qpart] + [around(qpart, f) for f in (1, 2, 3)]
     held = held + permuted(held, "row", 2)
+    pair_grad = pair_part(1, 2, both, doz, w_bias, pair_grad, params)
+    held, pair_grad, *second = lax.optimization_barrier((held, pair_grad, *second))
     mine = jnp.concatenate([held] + [permuted(held, "row", 4 * f) for f in (1, 2, 3)], axis=0)
     other = permuted(mine, "row", 1)
     grad_q, shift_q, grad_k, shift_k = pl.pallas_call(

time: 116 us -> 114 us (0.983)
  the two profiles are of different devices: /device:TPU:48 before, /device:TPU:1 now
where the time goes in v3:
time: 114 us
  starting transfers between devices  49.6 us (44%)
  Pallas kernels  26.7 us (23%)
  local copies, waits for them, and re-layouts  19.6 us (17%)
  waiting for transfers between devices  15.4 us (14%)
  other arithmetic  1.27 us (1%)
    ppermute x18, starting transfers between devices, permuted(): return lax.ppermute(x, axis, [(i, i ^ flip) for i in range(size)])  30.9 us
    unnamed x87, local copies, waits for them, and re-layouts  19.6 us
    ppermute x9, starting transfers between devices, around(): return lax.ppermute(x, 'col', moves)  18.7 us
    ppermute x18, waiting for transfers between devices, permuted(): return lax.ppermute(x, axis, [(i, i ^ flip) for i in range(size)])  10.9 us
    pallas_call x1, Pallas kernels, body(): pl.pallas_call(functools.partial(logits_kernel, heads, channels, npoint),...  6.7 us
    pallas_call x1, Pallas kernels, body(): pl.pallas_call(functools.partial(query_kernel, heads, channels, npoint),...  4.88 us
    ppermute x9, waiting for transfers between devices, around(): return lax.ppermute(x, 'col', moves)  4.47 us
    pallas_call x1, Pallas kernels, body(): pl.pallas_call(functools.partial(key_kernel, heads, channels, npoint), ou...  4.28 us
  transfers between devices with their start and end apart: 27, of which 13 were waited for; matrix products, arithmetic and copies ran while one was open for 0% of the time, Pallas kernels for 11%

profile of v3, /device:TPU:1, one launch (start us, length us, event | category | flops | bytes accessed | tf_op | source)
XLA Modules:
  0.0 113.6 jit_solution(15145587698411335583)
XLA Ops:
  0.6 2.2 %copy-done = bf16[64,256,128]{2,1,0:T(8,128)(2,1)S(1)} copy-done((bf16[64,256,128]{2,1,0:T(8,128)(2,1)S(1)}, bf16[64,256,128]{2,1,0:T(8,128)(2,1)}, u32[]{:S(2)}) %copy-start) | copy-done | bytes 4194328
  15.1 6.7 %logits.1 = (f32[1024,256]{1,0:T(8,128)S(1)}, f32[32,64]{1,0:T(8,128)S(1)}, bf16[64,192]{1,0:T(8,128)(2,1)S(1)}, bf16[256,192]{1,0:T(8,128)(2,1)S(1)}, f32[64,38...) custom-call(bf16[64,256,128]{2,1,0:T(8,128)(2,1)S(1)} %copy-done, ...), custom_call_target="tpu_custom_call" | custom-call | tf_op jit(solution)/shard_map/logits/pallas_call | solution.py:634
  21.8 3.5 %collective-permute-start.2 = (f32[32,64]{1,0:T(8,128)S(1)}, f32[32,64]{1,0:T(8,128)S(1)}, u32[]{:S(2)}, u32[]{:S(2)}) collective-permute-start(f32[32,64]{1,0:T(8,128)S(1)} %get-tuple-element.51), channel_id=1, source_target_pairs={{0,3},{1,2},{2,1},{3,0},{4,7},{5,6},{6,5},{7,4},{8,11},{9,10},{10,... | collective-permute-start | bytes 24584 | tf_op jit(solution)/shard_map/ppermute | solution.py:575
  26.4 1.5 %collective-permute-done.1 = f32[32,64]{1,0:T(8,128)S(1)} collective-permute-done((f32[32,64]{1,0:T(8,128)S(1)}, f32[32,64]{1,0:T(8,128)S(1)}, u32[]{:S(2)}, u32[]{:S(2)}) %collective-permute-start.1) | collective-permute-done | bytes 8224 | tf_op jit(solution)/shard_map/ppermute | solution.py:575
  27.9 5.5 %collective-permute-start.5 = (f32[32,64]{1,0:T(8,128)S(1)}, f32[32,64]{1,0:T(8,128)S(1)}, u32[]{:S(2)}, u32[]{:S(2)}) collective-permute-start(f32[32,64]{1,0:T(8,128)S(1)} %pad_maximum_fusion), channel_id=1, source_target_pairs={{14,0},{15,1},{4,2},{5,3},{2,4},{3,5},{8,6},{9,7},{6,8},{7,9},{12,... | collective-permute-start | bytes 24584 | tf_op jit(solution)/shard_map/ppermute | solution.py:587
  33.4 1.2 %collective-permute-start.4 = (f32[32,64]{1,0:T(8,128)S(1)}, f32[32,64]{1,0:T(8,128)S(1)}, u32[]{:S(2)}, u32[]{:S(2)}) collective-permute-start(f32[32,64]{1,0:T(8,128)S(1)} %pad_maximum_fusion), channel_id=1, source_target_pairs={{4,0},{5,1},{14,2},{15,3},{8,4},{9,5},{2,6},{3,7},{12,8},{13,9},{6... | collective-permute-start | bytes 24584 | tf_op jit(solution)/shard_map/ppermute | solution.py:587
  34.6 1.0 collective-permute-start.3
  35.6 3.8 %base.1 = (f32[1024,256]{1,0:T(8,128)S(1)}, f32[256,384]{1,0:T(8,128)S(1)}, bf16[64,192]{1,0:T(8,128)(2,1)S(1)}, f32[64,512]{1,0:T(8,128)S(1)}, bf16[1024,128]{1,0:T(8,128)(2,1)S(1)}) custom-call(bf16[64,256,128]{2,1,0:T(8,128)(2,1)S(1)} %copy-done, bf16[256,384]{1,0:T(8,128)(2,1)S(1)} %copy-done.5, bf16[64,384]{1,0:T(8,128)(2,1)S(1)} %copy-done.27, ...), custom_call_target="tpu_custom_call" | custom-call | flops 805306368 | bytes 8388608 | tf_op jit(solution)/shard_map/base/pallas_call | solution.py:677
  40.2 1.5 %attend.1 = (f32[1024,256]{1,0:T(8,128)S(1)}, f32[64,384]{1,0:T(8,128)}) custom-call(f32[1024,256]{1,0:T(8,128)S(1)} %get-tuple-element.48.masked_ref, f32[1024,256]{1,0:T(8,128)S(1)} %get-tuple-element.50.base_ref, s32[1,256]{1,0:T(1,128)S(1)} %bitcast.31, f32[32,64]{1,0:T(8,128)S(1)} %pad_maximum_fusion.1.stats_ref, f32[256,384]{1,0:T(8,128)S(1)} %get-tuple-element.52.gv_ref), custom_call_target="tpu_custom_call" | custom-call | tf_op jit(solution)/shard_map/attend/pallas_call | solution.py:702
  43.3 1.2 %collective-permute-start.6 = (f32[64,384]{1,0:T(8,128)}, f32[64,384]{1,0:T(8,128)}, u32[]{:S(2)}, u32[]{:S(2)}) collective-permute-start(f32[64,384]{1,0:T(8,128)} %get-tuple-element.54), channel_id=1, source_target_pairs={{0,1},{1,0},{2,3},{3,2},{4,5},{5,4},{6,7},{7,6},{8,9},{9,8},{10,11... | collective-permute-start | bytes 294920 | tf_op jit(solution)/shard_map/ppermute | solution.py:575
  44.5 2.1 %collective-permute-done.8 = f32[64,384]{1,0:T(8,128)} collective-permute-done((f32[64,384]{1,0:T(8,128)}, f32[64,384]{1,0:T(8,128)}, u32[]{:S(2)}, u32[]{:S(2)}) %collective-permute-start.8) | collective-permute-done | bytes 98336 | tf_op jit(solution)/shard_map/ppermute | solution.py:575
  47.6 1.1 add_add_fusion.1.psum0_ref
  48.7 2.9 %collective-permute-start.11 = (f32[64,384]{1,0:T(8,128)S(1)}, f32[64,384]{1,0:T(8,128)S(1)}, u32[]{:S(2)}, u32[]{:S(2)}) collective-permute-start(f32[64,384]{1,0:T(8,128)S(1)} %add_add_fusion.1.psum0_ref), channel_id=1, source_target_pairs={{10,0},{11,1},{8,2},{9,3},{14,4},{15,5},{12,6},{13,7},{2,8},{3,9},... | collective-permute-start | bytes 294920 | tf_op jit(solution)/shard_map/ppermute | solution.py:587
  51.6 1.2 %collective-permute-start.10 = (f32[64,384]{1,0:T(8,128)S(1)}, f32[64,384]{1,0:T(8,128)S(1)}, u32[]{:S(2)}, u32[]{:S(2)}) collective-permute-start(f32[64,384]{1,0:T(8,128)S(1)} %add_add_fusion.1.psum0_ref), channel_id=1, source_target_pairs={{4,0},{5,1},{14,2},{15,3},{8,4},{9,5},{2,6},{3,7},{12,8},{13,9},{6... | collective-permute-start | bytes 294920 | tf_op jit(solution)/shard_map/ppermute | solution.py:587
  52.8 1.9 %collective-permute-start.9 = (f32[64,384]{1,0:T(8,128)S(1)}, f32[64,384]{1,0:T(8,128)S(1)}, u32[]{:S(2)}, u32[]{:S(2)}) collective-permute-start(f32[64,384]{1,0:T(8,128)S(1)} %add_add_fusion.1.psum0_ref), channel_id=1, source_target_pairs={{14,0},{15,1},{4,2},{5,3},{2,4},{3,5},{8,6},{9,7},{6,8},{7,9},{12,... | collective-permute-start | bytes 294920 | tf_op jit(solution)/shard_map/ppermute | solution.py:587
  55.3 1.5 %collective-permute-done.10.psum2_ref = f32[64,384]{1,0:T(8,128)S(1)} collective-permute-done((f32[64,384]{1,0:T(8,128)S(1)}, f32[64,384]{1,0:T(8,128)S(1)}, u32[]{:S(2)}, u32[]{:S(2)}) %collective-permute-start.10) | collective-permute-done | bytes 98336 | tf_op jit(solution)/shard_map/ppermute | solution.py:587
  61.3 4.9 %query_grads.1 = (f32[72,384]{1,0:T(8,128)S(1)}, bf16[64,32,256]{2,1,0:T(8,128)(2,1)S(1)}, bf16[1024,256]{1,0:T(8,128)(2,1)S(1)}, bf16[1024,256]{1,0:T(8,128)(2,1)S(1)}, f32[64,384]{1,0:T(8,128)S(1)}) custom-call(s32[3]{0:T(128)S(1)} %pad_add_fusion.place_ref, f32[1024,256]{1,0:T(8,128)S(1)} %get-tuple-element.53.attn_ref, ...), custom_call_target="tpu_custom_call" | custom-call | tf_op jit(solution)/shard_map/query_grads/pallas_call | solution.py:716
  70.5 4.3 %key_grads.1 = (f32[160,384]{1,0:T(8,128)S(1)}, f32[160,384]{1,0:T(8,128)S(1)}) custom-call(s32[3]{0:T(128)S(1)} %pad_add_fusion.place_ref, bf16[64,32,256]{2,1,0:T(8,128)(2,1)S(1)} %get-tuple-element.75.both_ref, bf16[1024,256]{1,0:T(8,128)(2,1)S(1)} %get-tuple-element.62.dlo_ref, bf16[1024,256]{1,0:T(8,128)(2,1)S(1)} %get-tuple-element.63.alo_ref, ...), custom_call_target="tpu_custom_call" | custom-call | flops 2415919104 | bytes 1048576 | tf_op jit(solution)/shard_map/key_grads/pallas_call | solution.py:733
  74.9 7.7 %collective-permute-start.15 = (f32[160,384]{1,0:T(8,128)S(1)}, f32[160,384]{1,0:T(8,128)S(1)}, u32[]{:S(2)}, u32[]{:S(2)}) collective-permute-start(f32[160,384]{1,0:T(8,128)S(1)} %get-tuple-element.70), channel_id=1, source_target_pairs={{0,16},{16,0},{32,48},{48,32},{64,80},{80,64},{96,112},{112,96},{1... | collective-permute-start | bytes 737288 | tf_op jit(solution)/shard_map/ppermute | solution.py:575
  82.6 1.1 %collective-permute-done.15 = f32[160,384]{1,0:T(8,128)S(1)} collective-permute-done((f32[160,384]{1,0:T(8,128)S(1)}, f32[160,384]{1,0:T(8,128)S(1)}, u32[]{:S(2)}, u32[]{:S(2)}) %collective-permute-start.15) | collective-permute-done | bytes 245792 | tf_op jit(solution)/shard_map/ppermute | solution.py:575
  83.8 3.2 %collective-permute-start.17 = (f32[40,384]{1,0:T(8,128)S(1)}, f32[40,384]{1,0:T(8,128)S(1)}, u32[]{:S(2)}, u32[]{:S(2)}) collective-permute-start(f32[40,384]{1,0:T(8,128)S(1)} %get-tuple-element.95), channel_id=1, source_target_pairs={{0,128},{16,144},{32,160},{48,176},{64,192},{80,208},{96,224},{112... | collective-permute-start | bytes 184328 | tf_op jit(solution)/shard_map/ppermute | solution.py:575
  87.8 1.2 %collective-permute-start.22 = (f32[72,384]{1,0:T(8,128)S(1)}, f32[72,384]{1,0:T(8,128)S(1)}, u32[]{:S(2)}, u32[]{:S(2)}) collective-permute-start(f32[72,384]{1,0:T(8,128)S(1)} %add_add_fusion.q0_ref), channel_id=1, source_target_pairs={{10,0},{11,1},{8,2},{9,3},{14,4},{15,5},{12,6},{13,7},{2,8},{3,9},... | collective-permute-start | bytes 331784 | tf_op jit(solution)/shard_map/ppermute | solution.py:587
  89.0 2.9 %collective-permute-start.21 = (f32[72,384]{1,0:T(8,128)S(1)}, f32[72,384]{1,0:T(8,128)S(1)}, u32[]{:S(2)}, u32[]{:S(2)}) collective-permute-start(f32[72,384]{1,0:T(8,128)S(1)} %add_add_fusion.q0_ref), channel_id=1, source_target_pairs={{4,0},{5,1},{14,2},{15,3},{8,4},{9,5},{2,6},{3,7},{12,8},{13,9},{6... | collective-permute-start | bytes 331784 | tf_op jit(solution)/shard_map/ppermute | solution.py:587
  91.9 2.1 %pair_grad.2.refs_0_ = bf16[64,256,128]{2,1,0:T(8,128)(2,1)} custom-call(bf16[64,32,256]{2,1,0:T(8,128)(2,1)S(1)} %get-tuple-element.75.both_ref, bf16[1024,128]{1,0:T(8,128)(2,1)S(1)} %get-tuple-element.73.doz_ref, bf16[12,128]{1,0:T(8,128)(2,1)S(1)} %bitcast.28), custom_call_target="tpu_custom_call" | custom-call | flops 100663296 | bytes 2097152 | tf_op jit(solution)/shard_map/pair_grad/pallas_call | solution.py:556
  94.9 2.9 %collective-permute-start.19 = (f32[40,384]{1,0:T(8,128)S(1)}, f32[40,384]{1,0:T(8,128)S(1)}, u32[]{:S(2)}, u32[]{:S(2)}) collective-permute-start(f32[40,384]{1,0:T(8,128)S(1)} %add_add_fusion.2), channel_id=1, source_target_pairs={{0,32},{16,48},{32,0},{48,16},{64,96},{80,112},{96,64},{112,80},{1... | collective-permute-start | bytes 184328 | tf_op jit(solution)/shard_map/ppermute | solution.py:575
  97.8 2.1 %pair_grad.3 = bf16[64,256,128]{2,1,0:T(8,128)(2,1)} custom-call(bf16[64,32,256]{2,1,0:T(8,128)(2,1)S(1)} %get-tuple-element.75.both_ref, bf16[1024,128]{1,0:T(8,128)(2,1)S(1)} %get-tuple-element.73.doz_ref, bf16[12,128]{1,0:T(8,128)(2,1)S(1)} %bitcast.29, bf16[64,256,128]{2,1,0:T(8,128)(2,1)} %pair_grad.2.refs_0_), custom_call_target="tpu_custom_call", output_to_operand_aliasing={{}: (3, {})} | custom-call | flops 100663296 | bytes 2097152 | tf_op jit(solution)/shard_map/pair_grad/pallas_call | solution.py:556
  100.7 2.0 %collective-permute-start.25 = (f32[40,384]{1,0:T(8,128)S(1)}, f32[40,384]{1,0:T(8,128)S(1)}, u32[]{:S(2)}, u32[]{:S(2)}) collective-permute-start(f32[40,384]{1,0:T(8,128)S(1)} %add.70), channel_id=1, source_target_pairs={{0,192},{16,208},{32,224},{48,240},{64,128},{80,144},{96,160},{112... | collective-permute-start | bytes 184328 | tf_op jit(solution)/shard_map/ppermute | solution.py:575
  102.7 1.4 %collective-permute-start.24 = (f32[40,384]{1,0:T(8,128)S(1)}, f32[40,384]{1,0:T(8,128)S(1)}, u32[]{:S(2)}, u32[]{:S(2)}) collective-permute-start(f32[40,384]{1,0:T(8,128)S(1)} %add.70), channel_id=1, source_target_pairs={{0,128},{16,144},{32,160},{48,176},{64,192},{80,208},{96,224},{112... | collective-permute-start | bytes 184328 | tf_op jit(solution)/shard_map/ppermute | solution.py:575
  104.1 3.4 %collective-permute-done.23 = f32[40,384]{1,0:T(8,128)S(1)} collective-permute-done((f32[40,384]{1,0:T(8,128)S(1)}, f32[40,384]{1,0:T(8,128)S(1)}, u32[]{:S(2)}, u32[]{:S(2)}) %collective-permute-start.23) | collective-permute-done | bytes 61472 | tf_op jit(solution)/shard_map/ppermute | solution.py:575
  107.5 3.6 %collective-permute-start.26 = (f32[160,384]{1,0:T(8,128)S(1)}, f32[160,384]{1,0:T(8,128)S(1)}, u32[]{:S(2)}, u32[]{:S(2)}) collective-permute-start(f32[160,384]{1,0:T(8,128)S(1)} %constant_dynamic-update-slice_fusion.mine_ref), channel_id=1, source_target_pairs={{0,16},{16,0},{32,48},{48,32},{64,80},{80,64},{96,112},{112,96},{1... | collective-permute-start | bytes 737288 | tf_op jit(solution)/shard_map/ppermute | solution.py:575
  111.1 1.1 %collective-permute-done.26.other_ref = f32[160,384]{1,0:T(8,128)S(1)} collective-permute-done((f32[160,384]{1,0:T(8,128)S(1)}, f32[160,384]{1,0:T(8,128)S(1)}, u32[]{:S(2)}, u32[]{:S(2)}) %collective-permute-start.26) | collective-permute-done | bytes 245792 | tf_op jit(solution)/shard_map/ppermute | solution.py:575
  112.2 1.4 %finish.1 = (bf16[64,384]{1,0:T(8,128)(2,1)}, f32[3,64]{1,0:T(4,128)}, bf16[256,384]{1,0:T(8,128)(2,1)}, f32[3,256]{1,0:T(4,128)}) custom-call(s32[3]{0:T(128)S(1)} %pad_add_fusion.place_ref, f32[72,384]{1,0:T(8,128)S(1)} %add_add_fusion.q0_ref, f32[72,384]{1,0:T(8,128)S(1)} %collective-permute-done.20.q1_ref, f32[72,384]{1,0:T(8,128)S(1)} %collective-permute-done.21.q2_ref, ...), custom_call_target="tpu_custom_call" | custom-call | tf_op jit(solution)/shard_map/finish/pallas_call | solution.py:775
  (129 shorter events, 28.7 us)
Async XLA Ops:
  21.8 4.6 %collective-permute-start.2 = (f32[32,64]{1,0:T(8,128)S(1)}, f32[32,64]{1,0:T(8,128)S(1)}, u32[]{:S(2)}, u32[]{:S(2)}) collective-permute-start(f32[32,64]{1,0:T(8,128)S(1)} %get-tuple-element.51), channel_id=1, source_target_pairs={{0,3},{1,2},{2,1},{3,0},{4,7},{5,6},{6,5},{7,4},{8,11},{9,10},{10,... | collective-permute-start | bytes 24584 | tf_op jit(solution)/shard_map/ppermute | solution.py:575
  25.3 2.6 %collective-permute-start.1 = (f32[32,64]{1,0:T(8,128)S(1)}, f32[32,64]{1,0:T(8,128)S(1)}, u32[]{:S(2)}, u32[]{:S(2)}) collective-permute-start(f32[32,64]{1,0:T(8,128)S(1)} %get-tuple-element.51), channel_id=1, source_target_pairs={{0,2},{1,3},{2,0},{3,1},{4,6},{5,7},{6,4},{7,5},{8,10},{9,11},{10,... | collective-permute-start | bytes 24584 | tf_op jit(solution)/shard_map/ppermute | solution.py:575
  25.3 2.6 %collective-permute-start = (f32[32,64]{1,0:T(8,128)S(1)}, f32[32,64]{1,0:T(8,128)S(1)}, u32[]{:S(2)}, u32[]{:S(2)}) collective-permute-start(f32[32,64]{1,0:T(8,128)S(1)} %get-tuple-element.51), channel_id=1, source_target_pairs={{0,1},{1,0},{2,3},{3,2},{4,5},{5,4},{6,7},{7,6},{8,9},{9,8},{10,11... | collective-permute-start | bytes 24584 | tf_op jit(solution)/shard_map/ppermute | solution.py:575
  27.9 11.6 %collective-permute-start.5 = (f32[32,64]{1,0:T(8,128)S(1)}, f32[32,64]{1,0:T(8,128)S(1)}, u32[]{:S(2)}, u32[]{:S(2)}) collective-permute-start(f32[32,64]{1,0:T(8,128)S(1)} %pad_maximum_fusion), channel_id=1, source_target_pairs={{14,0},{15,1},{4,2},{5,3},{2,4},{3,5},{8,6},{9,7},{6,8},{7,9},{12,... | collective-permute-start | bytes 24584 | tf_op jit(solution)/shard_map/ppermute | solution.py:587
  33.4 6.1 %collective-permute-start.4 = (f32[32,64]{1,0:T(8,128)S(1)}, f32[32,64]{1,0:T(8,128)S(1)}, u32[]{:S(2)}, u32[]{:S(2)}) collective-permute-start(f32[32,64]{1,0:T(8,128)S(1)} %pad_maximum_fusion), channel_id=1, source_target_pairs={{4,0},{5,1},{14,2},{15,3},{8,4},{9,5},{2,6},{3,7},{12,8},{13,9},{6... | collective-permute-start | bytes 24584 | tf_op jit(solution)/shard_map/ppermute | solution.py:587
  34.6 5.6 %collective-permute-start.3 = (f32[32,64]{1,0:T(8,128)S(1)}, f32[32,64]{1,0:T(8,128)S(1)}, u32[]{:S(2)}, u32[]{:S(2)}) collective-permute-start(f32[32,64]{1,0:T(8,128)S(1)} %pad_maximum_fusion), channel_id=1, source_target_pairs={{10,0},{11,1},{8,2},{9,3},{14,4},{15,5},{12,6},{13,7},{2,8},{3,9},... | collective-permute-start | bytes 24584 | tf_op jit(solution)/shard_map/ppermute | solution.py:587
  41.8 4.8 %collective-permute-start.8 = (f32[64,384]{1,0:T(8,128)}, f32[64,384]{1,0:T(8,128)}, u32[]{:S(2)}, u32[]{:S(2)}) collective-permute-start(f32[64,384]{1,0:T(8,128)} %get-tuple-element.54), channel_id=1, source_target_pairs={{0,3},{1,2},{2,1},{3,0},{4,7},{5,6},{6,5},{7,4},{8,11},{9,10},{10,... | collective-permute-start | bytes 294920 | tf_op jit(solution)/shard_map/ppermute | solution.py:575
  42.6 4.1 %collective-permute-start.7 = (f32[64,384]{1,0:T(8,128)}, f32[64,384]{1,0:T(8,128)}, u32[]{:S(2)}, u32[]{:S(2)}) collective-permute-start(f32[64,384]{1,0:T(8,128)} %get-tuple-element.54), channel_id=1, source_target_pairs={{0,2},{1,3},{2,0},{3,1},{4,6},{5,7},{6,4},{7,5},{8,10},{9,11},{10,... | collective-permute-start | bytes 294920 | tf_op jit(solution)/shard_map/ppermute | solution.py:575
  43.3 4.3 %collective-permute-start.6 = (f32[64,384]{1,0:T(8,128)}, f32[64,384]{1,0:T(8,128)}, u32[]{:S(2)}, u32[]{:S(2)}) collective-permute-start(f32[64,384]{1,0:T(8,128)} %get-tuple-element.54), channel_id=1, source_target_pairs={{0,1},{1,0},{2,3},{3,2},{4,5},{5,4},{6,7},{7,6},{8,9},{9,8},{10,11... | collective-permute-start | bytes 294920 | tf_op jit(solution)/shard_map/ppermute | solution.py:575
  44.5 24.4 %copy-start.9 = (bf16[384,288]{0,1:T(8,128)(2,1)S(1)}, bf16[384,288]{0,1:T(8,128)(2,1)}, u32[]{:S(2)}) copy-start(bf16[384,288]{0,1:T(8,128)(2,1)} %param.29) | copy-start | bytes 663556
  44.5 24.4 %copy-start.11 = (bf16[384,288]{0,1:T(8,128)(2,1)S(1)}, bf16[384,288]{0,1:T(8,128)(2,1)}, u32[]{:S(2)}) copy-start(bf16[384,288]{0,1:T(8,128)(2,1)} %param.28) | copy-start | bytes 663556
  44.5 24.4 %copy-start.13 = (bf16[384,192]{0,1:T(8,128)(2,1)S(1)}, bf16[384,192]{0,1:T(8,128)(2,1)}, u32[]{:S(2)}) copy-start(bf16[384,192]{0,1:T(8,128)(2,1)} %param.26) | copy-start | bytes 442372
  44.5 24.4 %copy-start.15 = (bf16[384,192]{0,1:T(8,128)(2,1)S(1)}, bf16[384,192]{0,1:T(8,128)(2,1)}, u32[]{:S(2)}) copy-start(bf16[384,192]{0,1:T(8,128)(2,1)} %param.25) | copy-start | bytes 442372
  44.5 24.4 %copy-start.17 = (f32[256,128]{1,0:T(8,128)S(1)}, f32[256,128]{1,0:T(8,128)}, u32[]{:S(2)}) copy-start(f32[256,128]{1,0:T(8,128)} %copy-done.16) | copy-start | bytes 393220
  48.7 6.7 %collective-permute-start.11 = (f32[64,384]{1,0:T(8,128)S(1)}, f32[64,384]{1,0:T(8,128)S(1)}, u32[]{:S(2)}, u32[]{:S(2)}) collective-permute-start(f32[64,384]{1,0:T(8,128)S(1)} %add_add_fusion.1.psum0_ref), channel_id=1, source_target_pairs={{10,0},{11,1},{8,2},{9,3},{14,4},{15,5},{12,6},{13,7},{2,8},{3,9},... | collective-permute-start | bytes 294920 | tf_op jit(solution)/shard_map/ppermute | solution.py:587
  51.6 5.3 %collective-permute-start.10 = (f32[64,384]{1,0:T(8,128)S(1)}, f32[64,384]{1,0:T(8,128)S(1)}, u32[]{:S(2)}, u32[]{:S(2)}) collective-permute-start(f32[64,384]{1,0:T(8,128)S(1)} %add_add_fusion.1.psum0_ref), channel_id=1, source_target_pairs={{4,0},{5,1},{14,2},{15,3},{8,4},{9,5},{2,6},{3,7},{12,8},{13,9},{6... | collective-permute-start | bytes 294920 | tf_op jit(solution)/shard_map/ppermute | solution.py:587
  52.8 5.0 %collective-permute-start.9 = (f32[64,384]{1,0:T(8,128)S(1)}, f32[64,384]{1,0:T(8,128)S(1)}, u32[]{:S(2)}, u32[]{:S(2)}) collective-permute-start(f32[64,384]{1,0:T(8,128)S(1)} %add_add_fusion.1.psum0_ref), channel_id=1, source_target_pairs={{14,0},{15,1},{4,2},{5,3},{2,4},{3,5},{8,6},{9,7},{6,8},{7,9},{12,... | collective-permute-start | bytes 294920 | tf_op jit(solution)/shard_map/ppermute | solution.py:587
  66.2 8.7 %collective-permute-start.14 = (f32[72,384]{1,0:T(8,128)S(1)}, f32[72,384]{1,0:T(8,128)S(1)}, u32[]{:S(2)}, u32[]{:S(2)}) collective-permute-start(f32[72,384]{1,0:T(8,128)S(1)} %get-tuple-element.77), channel_id=1, source_target_pairs={{0,3},{1,2},{2,1},{3,0},{4,7},{5,6},{6,5},{7,4},{8,11},{9,10},{10,... | collective-permute-start | bytes 331784 | tf_op jit(solution)/shard_map/ppermute | solution.py:575
  67.1 7.7 %collective-permute-start.13 = (f32[72,384]{1,0:T(8,128)S(1)}, f32[72,384]{1,0:T(8,128)S(1)}, u32[]{:S(2)}, u32[]{:S(2)}) collective-permute-start(f32[72,384]{1,0:T(8,128)S(1)} %get-tuple-element.77), channel_id=1, source_target_pairs={{0,2},{1,3},{2,0},{3,1},{4,6},{5,7},{6,4},{7,5},{8,10},{9,11},{10,... | collective-permute-start | bytes 331784 | tf_op jit(solution)/shard_map/ppermute | solution.py:575
  68.2 6.7 %collective-permute-start.12 = (f32[72,384]{1,0:T(8,128)S(1)}, f32[72,384]{1,0:T(8,128)S(1)}, u32[]{:S(2)}, u32[]{:S(2)}) collective-permute-start(f32[72,384]{1,0:T(8,128)S(1)} %get-tuple-element.77), channel_id=1, source_target_pairs={{0,1},{1,0},{2,3},{3,2},{4,5},{5,4},{6,7},{7,6},{8,9},{9,8},{10,11... | collective-permute-start | bytes 331784 | tf_op jit(solution)/shard_map/ppermute | solution.py:575
  74.9 8.9 %collective-permute-start.15 = (f32[160,384]{1,0:T(8,128)S(1)}, f32[160,384]{1,0:T(8,128)S(1)}, u32[]{:S(2)}, u32[]{:S(2)}) collective-permute-start(f32[160,384]{1,0:T(8,128)S(1)} %get-tuple-element.70), channel_id=1, source_target_pairs={{0,16},{16,0},{32,48},{48,32},{64,80},{80,64},{96,112},{112,96},{1... | collective-permute-start | bytes 737288 | tf_op jit(solution)/shard_map/ppermute | solution.py:575
  83.8 10.2 %collective-permute-start.17 = (f32[40,384]{1,0:T(8,128)S(1)}, f32[40,384]{1,0:T(8,128)S(1)}, u32[]{:S(2)}, u32[]{:S(2)}) collective-permute-start(f32[40,384]{1,0:T(8,128)S(1)} %get-tuple-element.95), channel_id=1, source_target_pairs={{0,128},{16,144},{32,160},{48,176},{64,192},{80,208},{96,224},{112... | collective-permute-start | bytes 184328 | tf_op jit(solution)/shard_map/ppermute | solution.py:575
  87.0 7.9 %collective-permute-start.18 = (f32[40,384]{1,0:T(8,128)S(1)}, f32[40,384]{1,0:T(8,128)S(1)}, u32[]{:S(2)}, u32[]{:S(2)}) collective-permute-start(f32[40,384]{1,0:T(8,128)S(1)} %get-tuple-element.96), channel_id=1, source_target_pairs={{0,192},{16,208},{32,224},{48,240},{64,128},{80,144},{96,160},{112... | collective-permute-start | bytes 184328 | tf_op jit(solution)/shard_map/ppermute | solution.py:575
  87.8 7.1 %collective-permute-start.16 = (f32[40,384]{1,0:T(8,128)S(1)}, f32[40,384]{1,0:T(8,128)S(1)}, u32[]{:S(2)}, u32[]{:S(2)}) collective-permute-start(f32[40,384]{1,0:T(8,128)S(1)} %get-tuple-element.97), channel_id=1, source_target_pairs={{0,64},{16,80},{32,96},{48,112},{64,0},{80,16},{96,32},{112,48},{1... | collective-permute-start | bytes 184328 | tf_op jit(solution)/shard_map/ppermute | solution.py:575
  87.8 12.1 %collective-permute-start.22 = (f32[72,384]{1,0:T(8,128)S(1)}, f32[72,384]{1,0:T(8,128)S(1)}, u32[]{:S(2)}, u32[]{:S(2)}) collective-permute-start(f32[72,384]{1,0:T(8,128)S(1)} %add_add_fusion.q0_ref), channel_id=1, source_target_pairs={{10,0},{11,1},{8,2},{9,3},{14,4},{15,5},{12,6},{13,7},{2,8},{3,9},... | collective-permute-start | bytes 331784 | tf_op jit(solution)/shard_map/ppermute | solution.py:587
  89.0 10.9 %collective-permute-start.21 = (f32[72,384]{1,0:T(8,128)S(1)}, f32[72,384]{1,0:T(8,128)S(1)}, u32[]{:S(2)}, u32[]{:S(2)}) collective-permute-start(f32[72,384]{1,0:T(8,128)S(1)} %add_add_fusion.q0_ref), channel_id=1, source_target_pairs={{4,0},{5,1},{14,2},{15,3},{8,4},{9,5},{2,6},{3,7},{12,8},{13,9},{6... | collective-permute-start | bytes 331784 | tf_op jit(solution)/shard_map/ppermute | solution.py:587
  94.0 6.7 %collective-permute-start.20 = (f32[72,384]{1,0:T(8,128)S(1)}, f32[72,384]{1,0:T(8,128)S(1)}, u32[]{:S(2)}, u32[]{:S(2)}) collective-permute-start(f32[72,384]{1,0:T(8,128)S(1)} %add_add_fusion.q0_ref), channel_id=1, source_target_pairs={{14,0},{15,1},{4,2},{5,3},{2,4},{3,5},{8,6},{9,7},{6,8},{7,9},{12,... | collective-permute-start | bytes 331784 | tf_op jit(solution)/shard_map/ppermute | solution.py:587
  94.9 4.9 %collective-permute-start.19 = (f32[40,384]{1,0:T(8,128)S(1)}, f32[40,384]{1,0:T(8,128)S(1)}, u32[]{:S(2)}, u32[]{:S(2)}) collective-permute-start(f32[40,384]{1,0:T(8,128)S(1)} %add_add_fusion.2), channel_id=1, source_target_pairs={{0,32},{16,48},{32,0},{48,16},{64,96},{80,112},{96,64},{112,80},{1... | collective-permute-start | bytes 184328 | tf_op jit(solution)/shard_map/ppermute | solution.py:575
  100.7 6.7 %collective-permute-start.25 = (f32[40,384]{1,0:T(8,128)S(1)}, f32[40,384]{1,0:T(8,128)S(1)}, u32[]{:S(2)}, u32[]{:S(2)}) collective-permute-start(f32[40,384]{1,0:T(8,128)S(1)} %add.70), channel_id=1, source_target_pairs={{0,192},{16,208},{32,224},{48,240},{64,128},{80,144},{96,160},{112... | collective-permute-start | bytes 184328 | tf_op jit(solution)/shard_map/ppermute | solution.py:575
  102.7 4.7 %collective-permute-start.24 = (f32[40,384]{1,0:T(8,128)S(1)}, f32[40,384]{1,0:T(8,128)S(1)}, u32[]{:S(2)}, u32[]{:S(2)}) collective-permute-start(f32[40,384]{1,0:T(8,128)S(1)} %add.70), channel_id=1, source_target_pairs={{0,128},{16,144},{32,160},{48,176},{64,192},{80,208},{96,224},{112... | collective-permute-start | bytes 184328 | tf_op jit(solution)/shard_map/ppermute | solution.py:575
  104.1 3.4 %collective-permute-start.23 = (f32[40,384]{1,0:T(8,128)S(1)}, f32[40,384]{1,0:T(8,128)S(1)}, u32[]{:S(2)}, u32[]{:S(2)}) collective-permute-start(f32[40,384]{1,0:T(8,128)S(1)} %add.70), channel_id=1, source_target_pairs={{0,64},{16,80},{32,96},{48,112},{64,0},{80,16},{96,32},{112,48},{1... | collective-permute-start | bytes 184328 | tf_op jit(solution)/shard_map/ppermute | solution.py:575
  107.5 4.7 %collective-permute-start.26 = (f32[160,384]{1,0:T(8,128)S(1)}, f32[160,384]{1,0:T(8,128)S(1)}, u32[]{:S(2)}, u32[]{:S(2)}) collective-permute-start(f32[160,384]{1,0:T(8,128)S(1)} %constant_dynamic-update-slice_fusion.mine_ref), channel_id=1, source_target_pairs={{0,16},{16,0},{32,48},{48,32},{64,80},{80,64},{96,112},{112,96},{1... | collective-permute-start | bytes 737288 | tf_op jit(solution)/shard_map/ppermute | solution.py:575
  (37 other events, 273.2 us)

commit v4 on v3

--- a/solution.py
+++ b/solution.py
@@ -15,6 +15,25 @@
 LANE = 128
 NEG = -1e30
 LIMIT = 24 * 1024 * 1024
+ALONE = 56 * 1024 * 1024
+
+
+VMEM = pl.BlockSpec(memory_space=pltpu.VMEM)
+SMEM = pl.BlockSpec(memory_space=pltpu.SMEM)
+ANY = pl.BlockSpec(memory_space=pl.ANY)
+
+
+def call(kernel, name, outs, smem, hbm, vmem, scratch=(), cost=None, limit=LIMIT):
+    return pl.pallas_call(
+        kernel,
+        out_shape=outs,
+        in_specs=[SMEM] * len(smem) + [ANY] * len(hbm) + [VMEM] * len(vmem),
+        out_specs=[VMEM] * len(outs),
+        scratch_shapes=list(scratch),
+        compiler_params=pltpu.CompilerParams(vmem_limit_bytes=limit),
+        name=name,
+        cost_estimate=cost,
+    )(*smem, *hbm, *vmem)
 
 
 def nn(a, b, precision=None):
@@ -228,12 +247,12 @@
     channels,
     npoint,
     pair_hbm,
+    kcol_ref,
     sk_ref,
     cot_ref,
     wv_ref,
     wvp_ref,
     wout_ref,
-    kcol_ref,
     base_ref,
     gv_ref,
     dos_ref,
@@ -275,9 +294,18 @@
         lax.fori_loop(c * step, (c + 1) * step, one, 0, unroll=8)
 
 
-def attend_kernel(heads, npoint, masked_ref, base_ref, km_ref, stats_ref, gv_ref, attn_ref, out_ref):
+def attend_kernel(
+    heads,
+    npoint,
+    masked_ref,
+    base_ref,
+    gv_ref,
+    km_ref,
+    stats_ref,
+    attn_ref,
+    out_ref,
+):
     rows = stats_ref.shape[1]
-    keys = masked_ref.shape[1]
     stats = jnp.concatenate(
         [stats_ref[...], jnp.zeros((LANE - stats_ref.shape[0], rows), F32)], axis=0
     ).T
@@ -327,16 +355,13 @@
     place_ref,
     attn_ref,
     base_ref,
-    psum0_ref,
-    psum1_ref,
-    psum2_ref,
-    psum3_ref,
     key_ref,
     gq_ref,
     gk_ref,
     gv_ref,
     dpt_ref,
     qcol_ref,
+    psum_ref,
     wq_ref,
     wqp_ref,
     qout_ref,
@@ -352,7 +377,7 @@
     pmask, qcols, coef_lane = frames_of(heads, npoint, qcol_ref, rows)
     inside = iota((1, LANE), 1) < hp
 
-    psum = (psum0_ref[...] + psum1_ref[...]) + (psum2_ref[...] + psum3_ref[...])
+    psum = psum_ref[...]
     delta0 = to_col(psum[:, :LANE], hp)
     opt = [jnp.where(inside, psum[:, a * LANE : (a + 1) * LANE], 0.0) for a in range(3)]
     moved = [jnp.where(inside, opt[a] - qcols[:, 9 + a : 10 + a], 0.0) for a in range(3)]
@@ -483,8 +508,6 @@
     place_ref,
     q0_ref,
     q1_ref,
-    q2_ref,
-    q3_ref,
     mine_ref,
     other_ref,
     gradq_ref,
@@ -496,7 +519,7 @@
     rows = gradq_ref.shape[0]
     keys = gradk_ref.shape[0]
     piece = keys // 8
-    total = (q0_ref[...] + q1_ref[...]) + (q2_ref[...] + q3_ref[...])
+    total = q0_ref[...] + q1_ref[...]
     gradq_ref[...] = total[:rows].astype(BF)
     shiftq_ref[...] = total[rows : rows + 3, :rows]
     core, quarter = place_ref[1], place_ref[2]
@@ -578,11 +601,10 @@
 def around(x, hops):
     size = lax.axis_size("col")
     ring = size // 2
-    sign = -1 if hops == 2 else 1
     moves = []
     for i in range(size):
         z, low = i // 2, i % 2
-        source = (z + (hops if z % 2 else -hops) * sign) % ring
+        source = (z + (hops if z % 2 else -hops)) % ring
         moves.append((source * 2 + low, i))
     return lax.ppermute(x, "col", moves)
 
@@ -625,15 +647,17 @@
     n = rows * HP
     sds = jax.ShapeDtypeStruct
     params = pltpu.CompilerParams(vmem_limit_bytes=LIMIT)
-    vmem = pl.BlockSpec(memory_space=pltpu.VMEM)
     wide = 3 * LANE
     km = key_mask.reshape(1, keys)
     w_query, w_key, w_value = w_query.T, w_key.T, w_value.T
     w_qpoint, w_kpoint, w_vpoint = w_qpoint.T, w_kpoint.T, w_vpoint.T
     w_bias = w_bias.T
-    masked, stats, query, key, gq, gk, qcol, kcol = pl.pallas_call(
+    frames = [head_gamma.reshape(1, heads), chain_bias.reshape(1, heads)]
+    frames += [rot_q, trans_q, rot_k, trans_k, chain_q.reshape(1, rows), chain_k.reshape(1, keys)]
+    masked, stats, query, key, gq, gk, qcol, kcol = call(
         functools.partial(logits_kernel, heads, channels, npoint),
-        out_shape=[
+        "logits",
+        [
             sds((n, keys), F32),
             sds((2 * HP, rows), F32),
             sds((rows, hc), BF),
@@ -643,149 +667,121 @@
             sds((LANE, LANE), F32),
             sds((keys, LANE), F32),
         ],
-        in_specs=[pl.BlockSpec(memory_space=pl.ANY)] + [vmem] * 16,
-        out_specs=[vmem] * 8,
-        scratch_shapes=[
+        [],
+        [pair],
+        [single_q, single_k, w_query, w_key, w_qpoint, w_kpoint, w_bias, *frames, km],
+        [
             pltpu.VMEM((rows, keys, depth), BF),
             pltpu.VMEM((LANE, LANE), F32),
             pltpu.VMEM((LANE, keys), F32),
             pltpu.SemaphoreType.DMA((4,)),
         ],
-        compiler_params=params,
-        name="logits",
-    )(
-        pair,
-        single_q,
-        single_k,
-        w_query,
-        w_key,
-        w_qpoint,
-        w_kpoint,
-        w_bias,
-        head_gamma.reshape(1, heads),
-        chain_bias.reshape(1, heads),
-        rot_q,
-        trans_q,
-        rot_k,
-        trans_k,
-        chain_q.reshape(1, rows),
-        chain_k.reshape(1, keys),
-        km,
+        limit=ALONE,
     )
 
     first = [stats] + [permuted(stats, "col", f) for f in (1, 2, 3)]
-    base, gv, d_os, d_pt, doz = pl.pallas_call(
+    base, gv, d_os, d_pt, doz = call(
         functools.partial(base_kernel, heads, channels, npoint),
-        out_shape=[
+        "base",
+        [
             sds((n, keys), F32),
             sds((keys, wide), F32),
             sds((rows, hc), BF),
             sds((rows, 4 * LANE), F32),
             sds((n, depth), BF),
         ],
-        in_specs=[pl.BlockSpec(memory_space=pl.ANY)] + [vmem] * 6,
-        out_specs=[vmem] * 5,
-        scratch_shapes=[
+        [],
+        [pair],
+        [kcol, single_k, cotangent, w_value, w_vpoint, w_out],
+        [
             pltpu.VMEM((rows, keys, depth), BF),
             pltpu.VMEM((n, depth), F32),
             pltpu.SemaphoreType.DMA((4,)),
         ],
-        compiler_params=params,
-        name="base",
-        cost_estimate=pl.CostEstimate(
+        pl.CostEstimate(
             flops=8 * n * keys * wide, bytes_accessed=4 * rows * keys * depth, transcendentals=0
         ),
-    )(pair, single_k, cotangent, w_value, w_vpoint, w_out, kcol)
+    )
     stats = merged(first)
-    stats = merged([stats] + [around(stats, f) for f in (3, 2, 1)])
-
-    attn, points = pl.pallas_call(
+    stats = merged([stats] + [around(stats, f) for f in (3, -2, 1)])
+
+    attn, points = call(
         functools.partial(attend_kernel, heads, npoint),
-        out_shape=[sds((n, keys), F32), sds((rows, wide), F32)],
-        in_specs=[vmem] * 5,
-        out_specs=[vmem] * 2,
-        compiler_params=params,
-        name="attend",
-    )(masked, base, km, stats, gv)
+        "attend",
+        [sds((n, keys), F32), sds((rows, wide), F32)],
+        [],
+        [],
+        [masked, base, gv, km, stats],
+    )
     points = points + sum(permuted(points, "col", f) for f in (1, 2, 3))
-    parts = [points] + [around(points, f) for f in (1, 2, 3)]
+    points = points + sum(around(points, f) for f in (1, -2, 3))
 
     me = lax.axis_index("row")
     place = jnp.stack([lax.axis_index("col"), me % 2, me // 4]).astype(jnp.int32)
-    smem = pl.BlockSpec(memory_space=pltpu.SMEM)
-    qpart, both, dlo, alo, dglob = pl.pallas_call(
+    qpart, both, dlo, alo, dglob = call(
         functools.partial(query_kernel, heads, channels, npoint),
-        out_shape=[
+        "query_grads",
+        [
             sds((rows + 8, chans), F32),
             sds((rows, 2 * HP, keys), BF),
             sds((n, keys), BF),
             sds((n, keys), BF),
             sds((rows, wide), F32),
         ],
-        in_specs=[smem] + [vmem] * 14,
-        out_specs=[vmem] * 5,
-        compiler_params=params,
-        name="query_grads",
-    )(place, attn, base, *parts, key, gq, gk, gv, d_pt, qcol, w_query, w_qpoint)
-
-    first = [qpart] + [permuted(qpart, "col", f) for f in (1, 2, 3)]
+        [place],
+        [],
+        [attn, base, key, gq, gk, gv, d_pt, qcol, points, w_query, w_qpoint],
+    )
+
+    moved = permuted(qpart, "col", 1)
     half = sds((keys // 2 + 32, chans), F32)
-    mine, other = pl.pallas_call(
+    mine, other = call(
         functools.partial(key_kernel, heads, channels, npoint),
-        out_shape=[half, half],
-        in_specs=[smem] + [vmem] * 14,
-        out_specs=[vmem] * 2,
-        compiler_params=params,
-        name="key_grads",
-        cost_estimate=pl.CostEstimate(
+        "key_grads",
+        [half, half],
+        [place],
+        [],
+        [both, dlo, alo, dglob, query, gq, gk, d_os, qcol, kcol, w_key, w_value, w_kpoint, w_vpoint],
+        [],
+        pl.CostEstimate(
             flops=2 * n * keys * 12 * wide, bytes_accessed=4 * n * keys, transcendentals=0
         ),
-    )(
-        place,
-        both,
-        dlo,
-        alo,
-        dglob,
-        query,
-        gq,
-        gk,
-        d_os,
-        qcol,
-        kcol,
-        w_key,
-        w_value,
-        w_kpoint,
-        w_vpoint,
-    )
-    *first, mine, other = lax.optimization_barrier((*first, mine, other))
-
+    )
+    moved, mine, other = lax.optimization_barrier((moved, mine, other))
+
+    qpart = qpart + moved
     mine = mine + permuted(other, "row", 1)
     mine, both = lax.optimization_barrier((mine, both))
     mine = mine.reshape(4, -1, chans)
     held = mine[0] + sum(permuted(mine[f], "row", 4 * f) for f in (1, 2, 3))
+    moved = permuted(qpart, "col", 2)
     pair_grad = pair_part(0, 2, both, doz, w_bias, None, params)
-    held, both, pair_grad = lax.optimization_barrier((held, both, pair_grad))
-    qpart = (first[0] + first[1]) + (first[2] + first[3])
-    second = [qpart] + [around(qpart, f) for f in (1, 2, 3)]
-    held = held + permuted(held, "row", 2)
+    held, both, pair_grad, moved = lax.optimization_barrier((held, both, pair_grad, moved))
+    qpart = qpart + moved
+    received = permuted(held, "row", 2)
+    moved = around(qpart, 1)
     pair_grad = pair_part(1, 2, both, doz, w_bias, pair_grad, params)
-    held, pair_grad, *second = lax.optimization_barrier((held, pair_grad, *second))
+    received, moved, pair_grad = lax.optimization_barrier((received, moved, pair_grad))
+    held = held + received
+    qpart = qpart + moved
     mine = jnp.concatenate([held] + [permuted(held, "row", 4 * f) for f in (1, 2, 3)], axis=0)
+    moved = around(qpart, -3)
+    mine, moved = lax.optimization_barrier((mine, moved))
     other = permuted(mine, "row", 1)
-    grad_q, shift_q, grad_k, shift_k = pl.pallas_call(
+    grad_q, shift_q, grad_k, shift_k = call(
         finish_kernel,
-        out_shape=[
+        "finish",
+        [
             sds((rows, chans), BF),
             sds((3, rows), F32),
             sds((keys, chans), BF),
             sds((3, keys), F32),
         ],
-        in_specs=[smem] + [vmem] * 6,
-        out_specs=[vmem] * 4,
-        scratch_shapes=[pltpu.VMEM((8, keys), F32)],
-        compiler_params=params,
-        name="finish",
-    )(place, *second, mine, other)
+        [place],
+        [],
+        [qpart, moved, mine, other],
+        [pltpu.VMEM((8, keys), F32)],
+    )
     return pair_grad, grad_q, shift_q, grad_k, shift_k
 
 

time: 114 us -> 105 us (0.921)
  local copies, waits for them, and re-layouts: 19.6 us -> 5.96 us
  waiting for transfers between devices: 15.4 us -> 18.8 us
  Pallas kernels: 26.7 us -> 28.7 us
  starting transfers between devices: 49.6 us -> 47.8 us
    unnamed x87 -> x52, local copies, waits for them, and re-layouts: 19.6 us -> 5.95 us
    ppermute x9 -> x8, waiting for transfers between devices: 4.47 us -> 6.58 us  [around(): return lax.ppermute(x, 'col', moves)]
    pallas_call x6, Pallas kernels: 22.6 us -> 24.6 us  [call(): pl.pallas_call(kernel, out_shape=outs, in_specs=[SMEM] * len(smem) + [ANY...]
    ppermute x18 -> x17, waiting for transfers between devices: 10.9 us -> 12.2 us  [permuted(): return lax.ppermute(x, axis, [(i, i ^ flip) for i in range(size)])]
    ppermute x18 -> x17, starting transfers between devices: 30.9 us -> 29.8 us  [permuted(): return lax.ppermute(x, axis, [(i, i ^ flip) for i in range(size)])]
    ppermute x9 -> x8, starting transfers between devices: 18.7 us -> 18.1 us  [around(): return lax.ppermute(x, 'col', moves)]
  transfers between devices with their start and end apart: 27 -> 25, of which waited for: 13 -> 13; matrix products, arithmetic and copies ran while one was open for 0% -> 0% of each run, Pallas kernels for 11% -> 12%
where the time goes in v4:
time: 105 us; the launch traced here: 104 us
  starting transfers between devices  47.8 us (46%)
  Pallas kernels  28.7 us (27%)
  waiting for transfers between devices  18.8 us (18%)
  local copies, waits for them, and re-layouts  5.96 us (6%)
  other arithmetic  2.04 us (2%)
    ppermute x17, starting transfers between devices, permuted(): return lax.ppermute(x, axis, [(i, i ^ flip) for i in range(size)])  29.8 us
    pallas_call x6, Pallas kernels, call(): pl.pallas_call(kernel, out_shape=outs, in_specs=[SMEM] * len(smem) + [ANY...  24.6 us
    ppermute x8, starting transfers between devices, around(): return lax.ppermute(x, 'col', moves)  18.1 us
    ppermute x17, waiting for transfers between devices, permuted(): return lax.ppermute(x, axis, [(i, i ^ flip) for i in range(size)])  12.2 us
    ppermute x8, waiting for transfers between devices, around(): return lax.ppermute(x, 'col', moves)  6.58 us
    unnamed x52, local copies, waits for them, and re-layouts  5.95 us
    pallas_call x2, Pallas kernels, pair_part(): pl.pallas_call(pair_kernel, grid=(1,), out_shape=jax.ShapeDtypeStruct((ro...  4.16 us
  transfers between devices with their start and end apart: 25, of which 13 were waited for; matrix products, arithmetic and copies ran while one was open for 0% of the time, Pallas kernels for 12%

profile of v4, /device:TPU:1, one launch (start us, length us, event | category | flops | bytes accessed | tf_op | source)
XLA Modules:
  0.0 104.3 jit_solution(5315546747543352030)
XLA Ops:
  0.7 8.7 %logits.1 = (f32[1024,256]{1,0:T(8,128)}, f32[32,64]{1,0:T(8,128)}, bf16[64,192]{1,0:T(8,128)(2,1)}, bf16[256,192]{1,0:T(8,128)(2,1)}, f32[64,384]{1,0:T(8,128)}...) custom-call(bf16[64,256,128]{2,1,0:T(8,128)(2,1)} %pair_hbm.3, bf16[64,384]{1,0:T(8,128)(2,1)} %sq_ref.1, ...), custom_call_target="tpu_custom_call" | custom-call | tf_op jit(solution)/shard_map/logits/pallas_call | solution.py:27
  9.4 2.1 %collective-permute-start = (f32[32,64]{1,0:T(8,128)}, f32[32,64]{1,0:T(8,128)S(1)}, u32[]{:S(2)}, u32[]{:S(2)}) collective-permute-start(f32[32,64]{1,0:T(8,128)} %get-tuple-element.49), channel_id=1, source_target_pairs={{0,1},{1,0},{2,3},{3,2},{4,5},{5,4},{6,7},{7,6},{8,9},{9,8},{10,11... | collective-permute-start | bytes 24584 | tf_op jit(solution)/shard_map/ppermute | solution.py:598
  11.5 1.7 %collective-permute-start.1 = (f32[32,64]{1,0:T(8,128)}, f32[32,64]{1,0:T(8,128)S(1)}, u32[]{:S(2)}, u32[]{:S(2)}) collective-permute-start(f32[32,64]{1,0:T(8,128)} %get-tuple-element.49), channel_id=1, source_target_pairs={{0,2},{1,3},{2,0},{3,1},{4,6},{5,7},{6,4},{7,5},{8,10},{9,11},{10,... | collective-permute-start | bytes 24584 | tf_op jit(solution)/shard_map/ppermute | solution.py:598
  13.2 1.4 %collective-permute-done.1 = f32[32,64]{1,0:T(8,128)S(1)} collective-permute-done((f32[32,64]{1,0:T(8,128)}, f32[32,64]{1,0:T(8,128)S(1)}, u32[]{:S(2)}, u32[]{:S(2)}) %collective-permute-start.1) | collective-permute-done | bytes 8224 | tf_op jit(solution)/shard_map/ppermute | solution.py:598
  14.6 2.3 %collective-permute-done.2 = f32[32,64]{1,0:T(8,128)S(1)} collective-permute-done((f32[32,64]{1,0:T(8,128)}, f32[32,64]{1,0:T(8,128)S(1)}, u32[]{:S(2)}, u32[]{:S(2)}) %collective-permute-start.2) | collective-permute-done | bytes 8224 | tf_op jit(solution)/shard_map/ppermute | solution.py:598
  17.6 5.6 %collective-permute-start.3 = (f32[32,64]{1,0:T(8,128)S(1)}, f32[32,64]{1,0:T(8,128)S(1)}, u32[]{:S(2)}, u32[]{:S(2)}) collective-permute-start(f32[32,64]{1,0:T(8,128)S(1)} %pad_maximum_fusion.1), channel_id=1, source_target_pairs={{10,0},{11,1},{8,2},{9,3},{14,4},{15,5},{12,6},{13,7},{2,8},{3,9},... | collective-permute-start | bytes 24584 | tf_op jit(solution)/shard_map/ppermute | solution.py:609
  23.3 3.1 %collective-permute-start.5 = (f32[32,64]{1,0:T(8,128)S(1)}, f32[32,64]{1,0:T(8,128)S(1)}, u32[]{:S(2)}, u32[]{:S(2)}) collective-permute-start(f32[32,64]{1,0:T(8,128)S(1)} %pad_maximum_fusion.1), channel_id=1, source_target_pairs={{14,0},{15,1},{4,2},{5,3},{2,4},{3,5},{8,6},{9,7},{6,8},{7,9},{12,... | collective-permute-start | bytes 24584 | tf_op jit(solution)/shard_map/ppermute | solution.py:609
  26.4 1.4 %copy-done.1 = bf16[2112,384]{1,0:T(8,128)(2,1)S(1)} copy-done((bf16[2112,384]{1,0:T(8,128)(2,1)S(1)}, bf16[2112,384]{1,0:T(8,128)(2,1)}, u32[]{:S(2)}) %copy-start.1) | copy-done | bytes 1622040
  28.8 3.8 %base.1 = (f32[1024,256]{1,0:T(8,128)S(1)}, f32[256,384]{1,0:T(8,128)S(1)}, bf16[64,192]{1,0:T(8,128)(2,1)S(1)}, f32[64,512]{1,0:T(8,128)S(1)}, bf16[1024,128]{1,0:T(8,128)(2,1)S(1)}) custom-call(bf16[64,256,128]{2,1,0:T(8,128)(2,1)S(1)} %copy-done, f32[256,128]{1,0:T(8,128)S(1)} %copy-done.13, bf16[256,384]{1,0:T(8,128)(2,1)S(1)} %copy-done.4, ...), custom_call_target="tpu_custom_call" | custom-call | flops 805306368 | bytes 8388608 | tf_op jit(solution)/shard_map/base/pallas_call | solution.py:27
  32.7 1.6 %attend.1 = (f32[1024,256]{1,0:T(8,128)S(1)}, f32[64,384]{1,0:T(8,128)}) custom-call(f32[1024,256]{1,0:T(8,128)S(1)} %copy-done.2, f32[1024,256]{1,0:T(8,128)S(1)} %get-tuple-element.47.base_ref, f32[256,384]{1,0:T(8,128)S(1)} %get-tuple-element.48.gv_ref, s32[1,256]{1,0:T(1,128)S(1)} %bitcast.31, f32[32,64]{1,0:T(8,128)S(1)} %pad_maximum_fusion.2.stats_ref), custom_call_target="tpu_custom_call" | custom-call | tf_op jit(solution)/shard_map/attend/pallas_call | solution.py:27
  34.6 2.4 %collective-permute-start.8 = (f32[64,384]{1,0:T(8,128)}, f32[64,384]{1,0:T(8,128)}, u32[]{:S(2)}, u32[]{:S(2)}) collective-permute-start(f32[64,384]{1,0:T(8,128)} %get-tuple-element.56), channel_id=1, source_target_pairs={{0,3},{1,2},{2,1},{3,0},{4,7},{5,6},{6,5},{7,4},{8,11},{9,10},{10,... | collective-permute-start | bytes 294920 | tf_op jit(solution)/shard_map/ppermute | solution.py:598
  38.3 2.0 %collective-permute-done.8 = f32[64,384]{1,0:T(8,128)} collective-permute-done((f32[64,384]{1,0:T(8,128)}, f32[64,384]{1,0:T(8,128)}, u32[]{:S(2)}, u32[]{:S(2)}) %collective-permute-start.8) | collective-permute-done | bytes 98336 | tf_op jit(solution)/shard_map/ppermute | solution.py:598
  41.6 1.9 %collective-permute-start.11 = (f32[64,384]{1,0:T(8,128)S(1)}, f32[64,384]{1,0:T(8,128)S(1)}, u32[]{:S(2)}, u32[]{:S(2)}) collective-permute-start(f32[64,384]{1,0:T(8,128)S(1)} %add_add_fusion.1), channel_id=1, source_target_pairs={{10,0},{11,1},{8,2},{9,3},{14,4},{15,5},{12,6},{13,7},{2,8},{3,9},... | collective-permute-start | bytes 294920 | tf_op jit(solution)/shard_map/ppermute | solution.py:609
  43.5 2.7 %collective-permute-start.9 = (f32[64,384]{1,0:T(8,128)S(1)}, f32[64,384]{1,0:T(8,128)S(1)}, u32[]{:S(2)}, u32[]{:S(2)}) collective-permute-start(f32[64,384]{1,0:T(8,128)S(1)} %add_add_fusion.1), channel_id=1, source_target_pairs={{14,0},{15,1},{4,2},{5,3},{2,4},{3,5},{8,6},{9,7},{6,8},{7,9},{12,... | collective-permute-start | bytes 294920 | tf_op jit(solution)/shard_map/ppermute | solution.py:609
  46.3 1.9 %collective-permute-done.11 = f32[64,384]{1,0:T(8,128)S(1)} collective-permute-done((f32[64,384]{1,0:T(8,128)S(1)}, f32[64,384]{1,0:T(8,128)S(1)}, u32[]{:S(2)}, u32[]{:S(2)}) %collective-permute-start.11) | collective-permute-done | bytes 98336 | tf_op jit(solution)/shard_map/ppermute | solution.py:609
  48.2 2.1 %collective-permute-done.9 = f32[64,384]{1,0:T(8,128)S(1)} collective-permute-done((f32[64,384]{1,0:T(8,128)S(1)}, f32[64,384]{1,0:T(8,128)S(1)}, u32[]{:S(2)}, u32[]{:S(2)}) %collective-permute-start.9) | collective-permute-done | bytes 98336 | tf_op jit(solution)/shard_map/ppermute | solution.py:609
  54.0 4.9 %query_grads.1 = (f32[72,384]{1,0:T(8,128)S(1)}, bf16[64,32,256]{2,1,0:T(8,128)(2,1)S(1)}, bf16[1024,256]{1,0:T(8,128)(2,1)S(1)}, bf16[1024,256]{1,0:T(8,128)(2,1)S(1)}, f32[64,384]{1,0:T(8,128)S(1)}) custom-call(s32[3]{0:T(128)S(1)} %pad_add_fusion.place_ref, f32[1024,256]{1,0:T(8,128)S(1)} %get-tuple-element.50.attn_ref, ...), custom_call_target="tpu_custom_call" | custom-call | tf_op jit(solution)/shard_map/query_grads/pallas_call | solution.py:27
  59.7 4.3 %key_grads.1 = (f32[160,384]{1,0:T(8,128)S(1)}, f32[160,384]{1,0:T(8,128)S(1)}) custom-call(s32[3]{0:T(128)S(1)} %pad_add_fusion.place_ref, bf16[64,32,256]{2,1,0:T(8,128)(2,1)S(1)} %get-tuple-element.74.both_ref, bf16[1024,256]{1,0:T(8,128)(2,1)S(1)} %get-tuple-element.59.dlo_ref, bf16[1024,256]{1,0:T(8,128)(2,1)S(1)} %get-tuple-element.60.alo_ref, ...), custom_call_target="tpu_custom_call" | custom-call | flops 2415919104 | bytes 1048576 | tf_op jit(solution)/shard_map/key_grads/pallas_call | solution.py:27
  64.0 5.9 %collective-permute-start.13 = (f32[160,384]{1,0:T(8,128)S(1)}, f32[160,384]{1,0:T(8,128)S(1)}, u32[]{:S(2)}, u32[]{:S(2)}) collective-permute-start(f32[160,384]{1,0:T(8,128)S(1)} %get-tuple-element.67), channel_id=1, source_target_pairs={{0,16},{16,0},{32,48},{48,32},{64,80},{80,64},{96,112},{112,96},{1... | collective-permute-start | bytes 737288 | tf_op jit(solution)/shard_map/ppermute | solution.py:598
  71.1 1.4 %collective-permute-start.14 = (f32[40,384]{1,0:T(8,128)S(1)}, f32[40,384]{1,0:T(8,128)S(1)}, u32[]{:S(2)}, u32[]{:S(2)}) collective-permute-start(f32[40,384]{1,0:T(8,128)S(1)} %get-tuple-element.91), channel_id=1, source_target_pairs={{0,64},{16,80},{32,96},{48,112},{64,0},{80,16},{96,32},{112,48},{1... | collective-permute-start | bytes 184328 | tf_op jit(solution)/shard_map/ppermute | solution.py:598
  72.5 2.6 %collective-permute-start.15 = (f32[40,384]{1,0:T(8,128)S(1)}, f32[40,384]{1,0:T(8,128)S(1)}, u32[]{:S(2)}, u32[]{:S(2)}) collective-permute-start(f32[40,384]{1,0:T(8,128)S(1)} %get-tuple-element.89), channel_id=1, source_target_pairs={{0,128},{16,144},{32,160},{48,176},{64,192},{80,208},{96,224},{112... | collective-permute-start | bytes 184328 | tf_op jit(solution)/shard_map/ppermute | solution.py:598
  75.1 1.7 %collective-permute-start.17 = (f32[72,384]{1,0:T(8,128)S(1)}, f32[72,384]{1,0:T(8,128)S(1)}, u32[]{:S(2)}, u32[]{:S(2)}) collective-permute-start(f32[72,384]{1,0:T(8,128)S(1)} %add.82), channel_id=1, source_target_pairs={{0,2},{1,3},{2,0},{3,1},{4,6},{5,7},{6,4},{7,5},{8,10},{9,11},{10,... | collective-permute-start | bytes 331784 | tf_op jit(solution)/shard_map/ppermute | solution.py:598
  76.8 2.1 %pair_grad.2.refs_0_ = bf16[64,256,128]{2,1,0:T(8,128)(2,1)} custom-call(bf16[64,32,256]{2,1,0:T(8,128)(2,1)S(1)} %get-tuple-element.74.both_ref, bf16[1024,128]{1,0:T(8,128)(2,1)S(1)} %get-tuple-element.70.doz_ref, bf16[12,128]{1,0:T(8,128)(2,1)S(1)} %bitcast.28), custom_call_target="tpu_custom_call" | custom-call | flops 100663296 | bytes 2097152 | tf_op jit(solution)/shard_map/pair_grad/pallas_call | solution.py:579
  79.4 2.7 %collective-permute-start.19 = (f32[72,384]{1,0:T(8,128)S(1)}, f32[72,384]{1,0:T(8,128)S(1)}, u32[]{:S(2)}, u32[]{:S(2)}) collective-permute-start(f32[72,384]{1,0:T(8,128)S(1)} %add.83), channel_id=1, source_target_pairs={{14,0},{15,1},{4,2},{5,3},{2,4},{3,5},{8,6},{9,7},{6,8},{7,9},{12,... | collective-permute-start | bytes 331784 | tf_op jit(solution)/shard_map/ppermute | solution.py:609
  82.2 2.0 %collective-permute-start.18 = (f32[40,384]{1,0:T(8,128)S(1)}, f32[40,384]{1,0:T(8,128)S(1)}, u32[]{:S(2)}, u32[]{:S(2)}) collective-permute-start(f32[40,384]{1,0:T(8,128)S(1)} %add_add_fusion.2), channel_id=1, source_target_pairs={{0,32},{16,48},{32,0},{48,16},{64,96},{80,112},{96,64},{112,80},{1... | collective-permute-start | bytes 184328 | tf_op jit(solution)/shard_map/ppermute | solution.py:598
  84.2 2.1 %pair_grad.3 = bf16[64,256,128]{2,1,0:T(8,128)(2,1)} custom-call(bf16[64,32,256]{2,1,0:T(8,128)(2,1)S(1)} %get-tuple-element.74.both_ref, bf16[1024,128]{1,0:T(8,128)(2,1)S(1)} %get-tuple-element.70.doz_ref, bf16[12,128]{1,0:T(8,128)(2,1)S(1)} %bitcast.29, bf16[64,256,128]{2,1,0:T(8,128)(2,1)} %pair_grad.2.refs_0_), custom_call_target="tpu_custom_call", output_to_operand_aliasing={{}: (3, {})} | custom-call | flops 100663296 | bytes 2097152 | tf_op jit(solution)/shard_map/pair_grad/pallas_call | solution.py:579
  86.9 3.2 %collective-permute-start.21 = (f32[40,384]{1,0:T(8,128)S(1)}, f32[40,384]{1,0:T(8,128)S(1)}, u32[]{:S(2)}, u32[]{:S(2)}) collective-permute-start(f32[40,384]{1,0:T(8,128)S(1)} %add.85), channel_id=1, source_target_pairs={{0,128},{16,144},{32,160},{48,176},{64,192},{80,208},{96,224},{112... | collective-permute-start | bytes 184328 | tf_op jit(solution)/shard_map/ppermute | solution.py:598
  90.7 1.7 %collective-permute-start.23 = (f32[72,384]{1,0:T(8,128)S(1)}, f32[72,384]{1,0:T(8,128)S(1)}, u32[]{:S(2)}, u32[]{:S(2)}) collective-permute-start(f32[72,384]{1,0:T(8,128)S(1)} %add.84.q0_ref), channel_id=1, source_target_pairs={{6,0},{7,1},{12,2},{13,3},{10,4},{11,5},{0,6},{1,7},{14,8},{15,9},... | collective-permute-start | bytes 331784 | tf_op jit(solution)/shard_map/ppermute | solution.py:609
  92.5 1.9 %collective-permute-done.22 = f32[40,384]{1,0:T(8,128)S(1)} collective-permute-done((f32[40,384]{1,0:T(8,128)S(1)}, f32[40,384]{1,0:T(8,128)S(1)}, u32[]{:S(2)}, u32[]{:S(2)}) %collective-permute-start.22) | collective-permute-done | bytes 61472 | tf_op jit(solution)/shard_map/ppermute | solution.py:598
  94.4 2.5 %collective-permute-done.23.q1_ref = f32[72,384]{1,0:T(8,128)S(1)} collective-permute-done((f32[72,384]{1,0:T(8,128)S(1)}, f32[72,384]{1,0:T(8,128)S(1)}, u32[]{:S(2)}, u32[]{:S(2)}) %collective-permute-start.23) | collective-permute-done | bytes 110624 | tf_op jit(solution)/shard_map/ppermute | solution.py:609
  96.9 5.0 %collective-permute-start.24 = (f32[160,384]{1,0:T(8,128)S(1)}, f32[160,384]{1,0:T(8,128)S(1)}, u32[]{:S(2)}, u32[]{:S(2)}) collective-permute-start(f32[160,384]{1,0:T(8,128)S(1)} %pad_maximum_fusion.mine_ref), channel_id=1, source_target_pairs={{0,16},{16,0},{32,48},{48,32},{64,80},{80,64},{96,112},{112,96},{1... | collective-permute-start | bytes 737288 | tf_op jit(solution)/shard_map/ppermute | solution.py:598
  103.0 1.3 %finish.1 = (bf16[64,384]{1,0:T(8,128)(2,1)}, f32[3,64]{1,0:T(4,128)}, bf16[256,384]{1,0:T(8,128)(2,1)}, f32[3,256]{1,0:T(4,128)}) custom-call(s32[3]{0:T(128)S(1)} %pad_add_fusion.place_ref, f32[72,384]{1,0:T(8,128)S(1)} %add.84.q0_ref, f32[72,384]{1,0:T(8,128)S(1)} %collective-permute-done.23.q1_ref, f32[160,384]{1,0:T(8,128)S(1)} %pad_maximum_fusion.mine_ref, ...), custom_call_target="tpu_custom_call" | custom-call | tf_op jit(solution)/shard_map/finish/pallas_call | solution.py:27
  (93 shorter events, 13.3 us)
Async XLA Ops:
  0.6 25.8 %copy-start = (bf16[64,256,128]{2,1,0:T(8,128)(2,1)S(1)}, bf16[64,256,128]{2,1,0:T(8,128)(2,1)}, u32[]{:S(2)}) copy-start(bf16[64,256,128]{2,1,0:T(8,128)(2,1)} %pair_hbm.3) | copy-start | bytes 12582916
  0.6 25.8 %copy-start.4 = (bf16[256,384]{1,0:T(8,128)(2,1)S(1)}, bf16[256,384]{1,0:T(8,128)(2,1)}, u32[]{:S(2)}) copy-start(bf16[256,384]{1,0:T(8,128)(2,1)} %sk_ref.3) | copy-start | bytes 589828
  0.7 25.8 %copy-start.10 = (bf16[384,192]{0,1:T(8,128)(2,1)S(1)}, bf16[384,192]{0,1:T(8,128)(2,1)}, u32[]{:S(2)}) copy-start(bf16[384,192]{0,1:T(8,128)(2,1)} %param.26) | copy-start | bytes 442372
  0.7 25.7 %copy-start.7 = (bf16[384,288]{0,1:T(8,128)(2,1)S(1)}, bf16[384,288]{0,1:T(8,128)(2,1)}, u32[]{:S(2)}) copy-start(bf16[384,288]{0,1:T(8,128)(2,1)} %param.29) | copy-start | bytes 663556
  0.7 25.7 %copy-start.20 = (bf16[64,384]{1,0:T(8,128)(2,1)S(1)}, bf16[64,384]{1,0:T(8,128)(2,1)}, u32[]{:S(2)}) copy-start(bf16[64,384]{1,0:T(8,128)(2,1)} %cot_ref.1) | copy-start | bytes 147460
  9.4 23.3 %copy-start.22 = (s32[256]{0:T(256)S(1)}, s32[256]{0:T(256)}, u32[]{:S(2)}) copy-start(s32[256]{0:T(256)} %param.40) | copy-start | bytes 3076
  9.4 3.8 %collective-permute-start = (f32[32,64]{1,0:T(8,128)}, f32[32,64]{1,0:T(8,128)S(1)}, u32[]{:S(2)}, u32[]{:S(2)}) collective-permute-start(f32[32,64]{1,0:T(8,128)} %get-tuple-element.49), channel_id=1, source_target_pairs={{0,1},{1,0},{2,3},{3,2},{4,5},{5,4},{6,7},{7,6},{8,9},{9,8},{10,11... | collective-permute-start | bytes 24584 | tf_op jit(solution)/shard_map/ppermute | solution.py:598
  11.5 3.0 %collective-permute-start.1 = (f32[32,64]{1,0:T(8,128)}, f32[32,64]{1,0:T(8,128)S(1)}, u32[]{:S(2)}, u32[]{:S(2)}) collective-permute-start(f32[32,64]{1,0:T(8,128)} %get-tuple-element.49), channel_id=1, source_target_pairs={{0,2},{1,3},{2,0},{3,1},{4,6},{5,7},{6,4},{7,5},{8,10},{9,11},{10,... | collective-permute-start | bytes 24584 | tf_op jit(solution)/shard_map/ppermute | solution.py:598
  13.2 3.7 %collective-permute-start.2 = (f32[32,64]{1,0:T(8,128)}, f32[32,64]{1,0:T(8,128)S(1)}, u32[]{:S(2)}, u32[]{:S(2)}) collective-permute-start(f32[32,64]{1,0:T(8,128)} %get-tuple-element.49), channel_id=1, source_target_pairs={{0,3},{1,2},{2,1},{3,0},{4,7},{5,6},{6,5},{7,4},{8,11},{9,10},{10,... | collective-permute-start | bytes 24584 | tf_op jit(solution)/shard_map/ppermute | solution.py:598
  17.6 15.0 %collective-permute-start.3 = (f32[32,64]{1,0:T(8,128)S(1)}, f32[32,64]{1,0:T(8,128)S(1)}, u32[]{:S(2)}, u32[]{:S(2)}) collective-permute-start(f32[32,64]{1,0:T(8,128)S(1)} %pad_maximum_fusion.1), channel_id=1, source_target_pairs={{10,0},{11,1},{8,2},{9,3},{14,4},{15,5},{12,6},{13,7},{2,8},{3,9},... | collective-permute-start | bytes 24584 | tf_op jit(solution)/shard_map/ppermute | solution.py:609
  23.3 9.4 %collective-permute-start.4 = (f32[32,64]{1,0:T(8,128)S(1)}, f32[32,64]{1,0:T(8,128)S(1)}, u32[]{:S(2)}, u32[]{:S(2)}) collective-permute-start(f32[32,64]{1,0:T(8,128)S(1)} %pad_maximum_fusion.1), channel_id=1, source_target_pairs={{4,0},{5,1},{14,2},{15,3},{8,4},{9,5},{2,6},{3,7},{12,8},{13,9},{6... | collective-permute-start | bytes 24584 | tf_op jit(solution)/shard_map/ppermute | solution.py:609
  23.3 9.4 %collective-permute-start.5 = (f32[32,64]{1,0:T(8,128)S(1)}, f32[32,64]{1,0:T(8,128)S(1)}, u32[]{:S(2)}, u32[]{:S(2)}) collective-permute-start(f32[32,64]{1,0:T(8,128)S(1)} %pad_maximum_fusion.1), channel_id=1, source_target_pairs={{14,0},{15,1},{4,2},{5,3},{2,4},{3,5},{8,6},{9,7},{6,8},{7,9},{12,... | collective-permute-start | bytes 24584 | tf_op jit(solution)/shard_map/ppermute | solution.py:609
  32.6 27.1 %copy-start.23 = (bf16[64,192]{1,0:T(8,128)(2,1)S(1)}, bf16[64,192]{1,0:T(8,128)(2,1)}, u32[]{:S(2)}) copy-start(bf16[64,192]{1,0:T(8,128)(2,1)} %get-tuple-element.62.query_ref) | copy-start | bytes 73732
  34.3 3.8 %collective-permute-start.6 = (f32[64,384]{1,0:T(8,128)}, f32[64,384]{1,0:T(8,128)}, u32[]{:S(2)}, u32[]{:S(2)}) collective-permute-start(f32[64,384]{1,0:T(8,128)} %get-tuple-element.56), channel_id=1, source_target_pairs={{0,1},{1,0},{2,3},{3,2},{4,5},{5,4},{6,7},{7,6},{8,9},{9,8},{10,11... | collective-permute-start | bytes 294920 | tf_op jit(solution)/shard_map/ppermute | solution.py:598
  34.6 3.8 %collective-permute-start.7 = (f32[64,384]{1,0:T(8,128)}, f32[64,384]{1,0:T(8,128)}, u32[]{:S(2)}, u32[]{:S(2)}) collective-permute-start(f32[64,384]{1,0:T(8,128)} %get-tuple-element.56), channel_id=1, source_target_pairs={{0,2},{1,3},{2,0},{3,1},{4,6},{5,7},{6,4},{7,5},{8,10},{9,11},{10,... | collective-permute-start | bytes 294920 | tf_op jit(solution)/shard_map/ppermute | solution.py:598
  34.6 5.7 %collective-permute-start.8 = (f32[64,384]{1,0:T(8,128)}, f32[64,384]{1,0:T(8,128)}, u32[]{:S(2)}, u32[]{:S(2)}) collective-permute-start(f32[64,384]{1,0:T(8,128)} %get-tuple-element.56), channel_id=1, source_target_pairs={{0,3},{1,2},{2,1},{3,0},{4,7},{5,6},{6,5},{7,4},{8,11},{9,10},{10,... | collective-permute-start | bytes 294920 | tf_op jit(solution)/shard_map/ppermute | solution.py:598
  41.4 4.9 %collective-permute-start.10 = (f32[64,384]{1,0:T(8,128)S(1)}, f32[64,384]{1,0:T(8,128)S(1)}, u32[]{:S(2)}, u32[]{:S(2)}) collective-permute-start(f32[64,384]{1,0:T(8,128)S(1)} %add_add_fusion.1), channel_id=1, source_target_pairs={{4,0},{5,1},{14,2},{15,3},{8,4},{9,5},{2,6},{3,7},{12,8},{13,9},{6... | collective-permute-start | bytes 294920 | tf_op jit(solution)/shard_map/ppermute | solution.py:609
  41.6 6.6 %collective-permute-start.11 = (f32[64,384]{1,0:T(8,128)S(1)}, f32[64,384]{1,0:T(8,128)S(1)}, u32[]{:S(2)}, u32[]{:S(2)}) collective-permute-start(f32[64,384]{1,0:T(8,128)S(1)} %add_add_fusion.1), channel_id=1, source_target_pairs={{10,0},{11,1},{8,2},{9,3},{14,4},{15,5},{12,6},{13,7},{2,8},{3,9},... | collective-permute-start | bytes 294920 | tf_op jit(solution)/shard_map/ppermute | solution.py:609
  43.5 6.8 %collective-permute-start.9 = (f32[64,384]{1,0:T(8,128)S(1)}, f32[64,384]{1,0:T(8,128)S(1)}, u32[]{:S(2)}, u32[]{:S(2)}) collective-permute-start(f32[64,384]{1,0:T(8,128)S(1)} %add_add_fusion.1), channel_id=1, source_target_pairs={{14,0},{15,1},{4,2},{5,3},{2,4},{3,5},{8,6},{9,7},{6,8},{7,9},{12,... | collective-permute-start | bytes 294920 | tf_op jit(solution)/shard_map/ppermute | solution.py:609
  58.8 5.2 %collective-permute-start.12 = (f32[72,384]{1,0:T(8,128)S(1)}, f32[72,384]{1,0:T(8,128)S(1)}, u32[]{:S(2)}, u32[]{:S(2)}) collective-permute-start(f32[72,384]{1,0:T(8,128)S(1)} %get-tuple-element.57), channel_id=1, source_target_pairs={{0,1},{1,0},{2,3},{3,2},{4,5},{5,4},{6,7},{7,6},{8,9},{9,8},{10,11... | collective-permute-start | bytes 331784 | tf_op jit(solution)/shard_map/ppermute | solution.py:598
  64.0 7.0 %collective-permute-start.13 = (f32[160,384]{1,0:T(8,128)S(1)}, f32[160,384]{1,0:T(8,128)S(1)}, u32[]{:S(2)}, u32[]{:S(2)}) collective-permute-start(f32[160,384]{1,0:T(8,128)S(1)} %get-tuple-element.67), channel_id=1, source_target_pairs={{0,16},{16,0},{32,48},{48,32},{64,80},{80,64},{96,112},{112,96},{1... | collective-permute-start | bytes 737288 | tf_op jit(solution)/shard_map/ppermute | solution.py:598
  71.1 7.8 %collective-permute-start.14 = (f32[40,384]{1,0:T(8,128)S(1)}, f32[40,384]{1,0:T(8,128)S(1)}, u32[]{:S(2)}, u32[]{:S(2)}) collective-permute-start(f32[40,384]{1,0:T(8,128)S(1)} %get-tuple-element.91), channel_id=1, source_target_pairs={{0,64},{16,80},{32,96},{48,112},{64,0},{80,16},{96,32},{112,48},{1... | collective-permute-start | bytes 184328 | tf_op jit(solution)/shard_map/ppermute | solution.py:598
  72.5 6.4 %collective-permute-start.15 = (f32[40,384]{1,0:T(8,128)S(1)}, f32[40,384]{1,0:T(8,128)S(1)}, u32[]{:S(2)}, u32[]{:S(2)}) collective-permute-start(f32[40,384]{1,0:T(8,128)S(1)} %get-tuple-element.89), channel_id=1, source_target_pairs={{0,128},{16,144},{32,160},{48,176},{64,192},{80,208},{96,224},{112... | collective-permute-start | bytes 184328 | tf_op jit(solution)/shard_map/ppermute | solution.py:598
  75.1 4.3 %collective-permute-start.16 = (f32[40,384]{1,0:T(8,128)S(1)}, f32[40,384]{1,0:T(8,128)S(1)}, u32[]{:S(2)}, u32[]{:S(2)}) collective-permute-start(f32[40,384]{1,0:T(8,128)S(1)} %get-tuple-element.90), channel_id=1, source_target_pairs={{0,192},{16,208},{32,224},{48,240},{64,128},{80,144},{96,160},{112... | collective-permute-start | bytes 184328 | tf_op jit(solution)/shard_map/ppermute | solution.py:598
  75.1 4.3 %collective-permute-start.17 = (f32[72,384]{1,0:T(8,128)S(1)}, f32[72,384]{1,0:T(8,128)S(1)}, u32[]{:S(2)}, u32[]{:S(2)}) collective-permute-start(f32[72,384]{1,0:T(8,128)S(1)} %add.82), channel_id=1, source_target_pairs={{0,2},{1,3},{2,0},{3,1},{4,6},{5,7},{6,4},{7,5},{8,10},{9,11},{10,... | collective-permute-start | bytes 331784 | tf_op jit(solution)/shard_map/ppermute | solution.py:598
  79.4 7.3 %collective-permute-start.19 = (f32[72,384]{1,0:T(8,128)S(1)}, f32[72,384]{1,0:T(8,128)S(1)}, u32[]{:S(2)}, u32[]{:S(2)}) collective-permute-start(f32[72,384]{1,0:T(8,128)S(1)} %add.83), channel_id=1, source_target_pairs={{14,0},{15,1},{4,2},{5,3},{2,4},{3,5},{8,6},{9,7},{6,8},{7,9},{12,... | collective-permute-start | bytes 331784 | tf_op jit(solution)/shard_map/ppermute | solution.py:609
  82.2 4.6 %collective-permute-start.18 = (f32[40,384]{1,0:T(8,128)S(1)}, f32[40,384]{1,0:T(8,128)S(1)}, u32[]{:S(2)}, u32[]{:S(2)}) collective-permute-start(f32[40,384]{1,0:T(8,128)S(1)} %add_add_fusion.2), channel_id=1, source_target_pairs={{0,32},{16,48},{32,0},{48,16},{64,96},{80,112},{96,64},{112,80},{1... | collective-permute-start | bytes 184328 | tf_op jit(solution)/shard_map/ppermute | solution.py:598
  86.8 5.7 %collective-permute-start.20 = (f32[40,384]{1,0:T(8,128)S(1)}, f32[40,384]{1,0:T(8,128)S(1)}, u32[]{:S(2)}, u32[]{:S(2)}) collective-permute-start(f32[40,384]{1,0:T(8,128)S(1)} %add.85), channel_id=1, source_target_pairs={{0,64},{16,80},{32,96},{48,112},{64,0},{80,16},{96,32},{112,48},{1... | collective-permute-start | bytes 184328 | tf_op jit(solution)/shard_map/ppermute | solution.py:598
  86.9 5.6 %collective-permute-start.21 = (f32[40,384]{1,0:T(8,128)S(1)}, f32[40,384]{1,0:T(8,128)S(1)}, u32[]{:S(2)}, u32[]{:S(2)}) collective-permute-start(f32[40,384]{1,0:T(8,128)S(1)} %add.85), channel_id=1, source_target_pairs={{0,128},{16,144},{32,160},{48,176},{64,192},{80,208},{96,224},{112... | collective-permute-start | bytes 184328 | tf_op jit(solution)/shard_map/ppermute | solution.py:598
  90.1 4.3 %collective-permute-start.22 = (f32[40,384]{1,0:T(8,128)S(1)}, f32[40,384]{1,0:T(8,128)S(1)}, u32[]{:S(2)}, u32[]{:S(2)}) collective-permute-start(f32[40,384]{1,0:T(8,128)S(1)} %add.85), channel_id=1, source_target_pairs={{0,192},{16,208},{32,224},{48,240},{64,128},{80,144},{96,160},{112... | collective-permute-start | bytes 184328 | tf_op jit(solution)/shard_map/ppermute | solution.py:598
  90.7 6.1 %collective-permute-start.23 = (f32[72,384]{1,0:T(8,128)S(1)}, f32[72,384]{1,0:T(8,128)S(1)}, u32[]{:S(2)}, u32[]{:S(2)}) collective-permute-start(f32[72,384]{1,0:T(8,128)S(1)} %add.84.q0_ref), channel_id=1, source_target_pairs={{6,0},{7,1},{12,2},{13,3},{10,4},{11,5},{0,6},{1,7},{14,8},{15,9},... | collective-permute-start | bytes 331784 | tf_op jit(solution)/shard_map/ppermute | solution.py:609
  96.9 6.1 %collective-permute-start.24 = (f32[160,384]{1,0:T(8,128)S(1)}, f32[160,384]{1,0:T(8,128)S(1)}, u32[]{:S(2)}, u32[]{:S(2)}) collective-permute-start(f32[160,384]{1,0:T(8,128)S(1)} %pad_maximum_fusion.mine_ref), channel_id=1, source_target_pairs={{0,16},{16,0},{32,48},{48,32},{64,80},{80,64},{96,112},{112,96},{1... | collective-permute-start | bytes 737288 | tf_op jit(solution)/shard_map/ppermute | solution.py:598
  (19 other events, 231.8 us)

commit v5 on v4

--- a/solution.py
+++ b/solution.py
@@ -137,6 +137,29 @@
 def padded_bias(wb_ref):
     heads, depth = wb_ref.shape
     return jnp.concatenate([wb_ref[...].astype(F32), jnp.zeros((HP - heads, depth), F32)], axis=0)
+
+
+class packing:
+    def __init__(self, rows, keys, hc):
+        first = keys + rows
+        second = first + LANE
+        self.shape = (second + keys, 3 * LANE)
+        self.gk = (slice(0, keys), slice(0, 3 * LANE))
+        self.gq = (slice(keys, first), slice(0, 3 * LANE))
+        self.qcol = (slice(first, second), slice(0, LANE))
+        self.query = (slice(first, first + rows), slice(LANE, LANE + hc))
+        self.key = (slice(second, second + keys), slice(0, hc))
+        self.kcol = (slice(second, second + keys), slice(2 * LANE, 3 * LANE))
+
+
+class value_packing:
+    def __init__(self, rows, keys, hc):
+        first = keys + rows
+        self.shape = (first + rows, 3 * LANE)
+        self.gv = (slice(0, keys), slice(0, 3 * LANE))
+        self.dol = [(slice(keys, first), slice(b * LANE, (b + 1) * LANE)) for b in range(3)]
+        self.don = (slice(first, first + rows), slice(0, LANE))
+        self.dos = (slice(first, first + rows), slice(LANE, LANE + hc))
 
 
 def logits_kernel(
@@ -162,12 +185,7 @@
     km_ref,
     masked_ref,
     stats_ref,
-    query_ref,
-    key_ref,
-    gq_ref,
-    gk_ref,
-    qcol_ref,
-    kcol_ref,
+    pack_ref,
     pair_ref,
     tq_ref,
     tk_ref,
@@ -176,6 +194,7 @@
     rows, keys, depth = pair_hbm.shape
     hp = heads * npoint
     copies, step = load_pair(pair_hbm, pair_ref, sems)
+    place = packing(rows, keys, channels * heads)
     w_logit = math.sqrt(1.0 / 3.0)
     w_point = math.sqrt(2.0 / (9.0 * npoint))
     tq_ref[...] = jnp.zeros_like(tq_ref)
@@ -187,34 +206,23 @@
     qcols_all = tq_ref[...].T
     qcols = qcols_all[:rows]
     head_cols = qcols_all[:HP]
-    qcol_ref[...] = qcols_all
+    pack_ref[place.qcol] = qcols_all
     tk_ref[...] = jnp.zeros_like(tk_ref)
     tk_ref[0:9, :] = rotk_ref[...]
     tk_ref[9:12, :] = trk_ref[...]
     kcols = tk_ref[...].T
-    kcol_ref[...] = kcols
+    pack_ref[place.kcol] = kcols
 
     sq = sq_ref[...]
     sk = sk_ref[...]
     query = nt(sq, wq_ref[...]).astype(BF)
     key = nt(sk, wk_ref[...]).astype(BF)
-    query_ref[...] = query
-    key_ref[...] = key
+    pack_ref[place.query] = query.astype(F32)
+    pack_ref[place.key] = key.astype(F32)
     gq = rotate_points(nt(sq, wqp_ref[...]), qcols, hp)
     gk = rotate_points(nt(sk, wkp_ref[...]), kcols, hp)
-    gq_ref[...] = gq
-    gk_ref[...] = gk
-
-    wbt = padded_bias(wb_ref).astype(BF)
-    for c, copy in enumerate(copies):
-        copy.wait()
-
-        def one(i, carry):
-            r = pl.multiple_of(i * HP, HP)
-            masked_ref[pl.ds(r, HP), :] = nt(wbt, pair_ref[i])
-            return carry
-
-        lax.fori_loop(c * step, (c + 1) * step, one, 0, unroll=8)
+    pack_ref[place.gq] = gq
+    pack_ref[place.gk] = gk
 
     pmask = head_mask(heads, npoint, 3 * LANE)
     cmask = channel_mask(heads, channels)
@@ -227,14 +235,25 @@
     same = (qcols[:, 12:13] == ck_ref[...].astype(F32)).astype(F32)
     shape = (rows, HP, keys)
     dist = (sqq.reshape(rows, HP, 1) + sqk[None]) - 2.0 * cross.reshape(shape)
-    inner = (
-        qk.reshape(shape) * (1.0 / math.sqrt(channels))
-        + masked_ref[...].reshape(shape)
-        + head_cols[:, 14:15][None] * jnp.broadcast_to(same[:, None, :], shape)
-    )
+    inner = qk.reshape(shape) * (1.0 / math.sqrt(channels)) + head_cols[:, 14:15][
+        None
+    ] * jnp.broadcast_to(same[:, None, :], shape)
     logit = w_logit * inner - (0.5 * coef)[None] * dist
+    masked_ref[...] = logit.reshape(rows * HP, keys)
+
+    wbt = padded_bias(wb_ref).astype(BF)
+    for c, copy in enumerate(copies):
+        copy.wait()
+
+        def one(i, carry):
+            r = pl.multiple_of(i * HP, HP)
+            masked_ref[pl.ds(r, HP), :] += w_logit * nt(wbt, pair_ref[i])
+            return carry
+
+        lax.fori_loop(c * step, (c + 1) * step, one, 0, unroll=16)
+
     valid = (km_ref[...] == 1)[None]
-    masked = jnp.where(valid, logit, NEG)
+    masked = jnp.where(valid, masked_ref[...].reshape(shape), NEG)
     top = jnp.max(masked, axis=2, keepdims=True)
     total = jnp.sum(jnp.where(valid, jnp.exp(masked - top), 0.0), axis=2, keepdims=True)
     masked_ref[...] = masked.reshape(rows * HP, keys)
@@ -247,16 +266,14 @@
     channels,
     npoint,
     pair_hbm,
-    kcol_ref,
+    pack_ref,
     sk_ref,
     cot_ref,
     wv_ref,
     wvp_ref,
     wout_ref,
     base_ref,
-    gv_ref,
-    dos_ref,
-    dpt_ref,
+    vals_ref,
     doz_ref,
     pair_ref,
     lhs_ref,
@@ -268,14 +285,16 @@
     sk = sk_ref[...]
     cot = cot_ref[...]
     value = nt(sk, wv_ref[...]).astype(BF)
-    gv_ref[...] = rotate_points(nt(sk, wvp_ref[...]), kcol_ref[...], hp)
     nos = heads * channels
+    place = value_packing(rows, keys, nos)
+    kcols = pack_ref[packing(rows, keys, nos).kcol]
+    vals_ref[place.gv] = rotate_points(nt(sk, wvp_ref[...]), kcols, hp)
     first = nos + heads * depth
     dos = nt(cot, wout_ref[0:nos, :]).astype(BF)
-    dos_ref[...] = dos
+    vals_ref[place.dos] = dos.astype(F32)
     for b in range(4):
         d = nt(cot, wout_ref[first + b * hp : first + (b + 1) * hp, :]).astype(BF).astype(F32)
-        dpt_ref[:, b * LANE : (b + 1) * LANE] = pad_lanes(d)
+        vals_ref[(place.dol + [place.don])[b]] = pad_lanes(d)
     doz = nt(cot, wout_ref[nos:first, :]).astype(BF).astype(F32)
     lhs_ref[...] = jnp.zeros_like(lhs_ref)
     for h in range(heads):
@@ -291,7 +310,7 @@
             base_ref[pl.ds(r, HP), :] += nt(doz_ref[pl.ds(r, HP), :], pair_ref[i])
             return carry
 
-        lax.fori_loop(c * step, (c + 1) * step, one, 0, unroll=8)
+        lax.fori_loop(c * step, (c + 1) * step, one, 0, unroll=16)
 
 
 def attend_kernel(
@@ -299,7 +318,7 @@
     npoint,
     masked_ref,
     base_ref,
-    gv_ref,
+    vals_ref,
     km_ref,
     stats_ref,
     attn_ref,
@@ -316,7 +335,7 @@
     attn_ref[...] = attn
     attn_b = attn.astype(BF)
     attn_f = attn_b.astype(F32)
-    ghi, glo = split(gv_ref[...])
+    ghi, glo = split(vals_ref[0 : masked_ref.shape[1], :])
     opt = nn(attn_b, ghi) + nn(attn_b, glo)
     pmask = head_mask(heads, npoint, 3 * LANE)
     delta = jnp.sum(attn_f * base_ref[...], axis=1, keepdims=True)
@@ -324,9 +343,8 @@
     out_ref[:, 0:LANE] += to_lanes(delta, heads * npoint)
 
 
-def frames_of(heads, npoint, qcol_ref, rows):
+def frames_of(heads, npoint, qall, rows):
     pmask = head_mask(heads, npoint, 3 * LANE)
-    qall = qcol_ref[...]
     w_logit = math.sqrt(1.0 / 3.0)
     w_point = math.sqrt(2.0 / (9.0 * npoint))
     coef = (w_logit * w_point) * qall[:HP, 13:14]
@@ -355,12 +373,8 @@
     place_ref,
     attn_ref,
     base_ref,
-    key_ref,
-    gq_ref,
-    gk_ref,
-    gv_ref,
-    dpt_ref,
-    qcol_ref,
+    pack_ref,
+    vals_ref,
     psum_ref,
     wq_ref,
     wqp_ref,
@@ -370,11 +384,13 @@
     alo_ref,
     dglob_ref,
 ):
-    rows, keys = gq_ref.shape[0], gk_ref.shape[0]
+    rows, keys = psum_ref.shape[0], base_ref.shape[1]
+    place = packing(rows, keys, heads * channels)
+    vplace = value_packing(rows, keys, heads * channels)
     hp = heads * npoint
     scale = math.sqrt(1.0 / 3.0) / math.sqrt(channels)
     cmask = channel_mask(heads, channels)
-    pmask, qcols, coef_lane = frames_of(heads, npoint, qcol_ref, rows)
+    pmask, qcols, coef_lane = frames_of(heads, npoint, pack_ref[place.qcol], rows)
     inside = iota((1, LANE), 1) < hp
 
     psum = psum_ref[...]
@@ -383,8 +399,8 @@
     moved = [jnp.where(inside, opt[a] - qcols[:, 9 + a : 10 + a], 0.0) for a in range(3)]
     oloc = back_rotate(jnp.concatenate(moved, axis=1), qcols)
     onorm = jnp.sqrt(1.0 + (oloc[0] * oloc[0] + oloc[1] * oloc[1] + oloc[2] * oloc[2]))
-    ratio = dpt_ref[:, 3 * LANE : 4 * LANE] / onorm
-    dloc = [dpt_ref[:, b * LANE : (b + 1) * LANE] + ratio * oloc[b] for b in range(3)]
+    ratio = vals_ref[vplace.don] / onorm
+    dloc = [vals_ref[vplace.dol[b]] + ratio * oloc[b] for b in range(3)]
     dglob = jnp.concatenate(
         [
             sum(qcols[:, 3 * a + b : 3 * a + b + 1] * dloc[b] for b in range(3))
@@ -396,7 +412,7 @@
     dghi, dglo = split(spread(dglob, pmask))
     opt_row = jnp.concatenate(opt, axis=1)
     delta = delta0 + jnp.sum(spread(opt_row * dglob, pmask), axis=1, keepdims=True)
-    gvhi, gvlo = split(gv_ref[...])
+    gvhi, gvlo = split(vals_ref[vplace.gv])
     dattn = base_ref[...] + nt(dghi, gvhi) + (nt(dghi, gvlo) + nt(dglo, gvhi))
     attn = attn_ref[...]
     dlogit = attn * (dattn - delta)
@@ -407,12 +423,12 @@
     dlo_ref[...] = dlo
     alo_ref[...] = alo
 
-    gkhi, gklo = split(gk_ref[...])
-    dq = scale * gather_heads(nn(dhi, key_ref[...]), cmask)
+    gkhi, gklo = split(pack_ref[place.gk])
+    dq = scale * gather_heads(nn(dhi, pack_ref[place.key].astype(BF)), cmask)
     qpts = gather_heads(nn(dhi, gkhi) + (nn(dhi, gklo) + nn(dlo, gkhi)), pmask)
     qsum = jnp.sum(dlogit, axis=1, keepdims=True)
     qsum_lane = gather_heads(jnp.broadcast_to(qsum, (rows * HP, 3 * LANE)), pmask)
-    dgq = coef_lane * (qpts - gq_ref[...] * qsum_lane)
+    dgq = coef_lane * (qpts - pack_ref[place.gq] * qsum_lane)
     mq = back_rotate(dgq, qcols)
     width = qout_ref.shape[1]
     qout_ref[0:rows, :] = project(
@@ -434,12 +450,8 @@
     dlo_ref,
     alo_ref,
     dglob_ref,
-    query_ref,
-    gq_ref,
-    gk_ref,
-    dos_ref,
-    qcol_ref,
-    kcol_ref,
+    pack_ref,
+    vals_ref,
     wk_ref,
     wv_ref,
     wkp_ref,
@@ -447,29 +459,31 @@
     mine_ref,
     other_ref,
 ):
-    rows, keys = gq_ref.shape[0], gk_ref.shape[0]
+    rows, keys = dglob_ref.shape[0], dlo_ref.shape[1]
+    place = packing(rows, keys, heads * channels)
+    vplace = value_packing(rows, keys, heads * channels)
     hp = heads * npoint
     scale = math.sqrt(1.0 / 3.0) / math.sqrt(channels)
     cmask = channel_mask(heads, channels)
-    pmask, qcols, coef_lane = frames_of(heads, npoint, qcol_ref, rows)
-    kcols = kcol_ref[...]
+    pmask, qcols, coef_lane = frames_of(heads, npoint, pack_ref[place.qcol], rows)
+    kcols = pack_ref[place.kcol]
     dhi = both_ref[:, 0:HP, :].reshape(rows * HP, keys)
     ahi = both_ref[:, HP : 2 * HP, :].reshape(rows * HP, keys)
     dlo, alo = dlo_ref[...], alo_ref[...]
     dghi, dglo = split(spread(dglob_ref[...], pmask))
-    gqhi, gqlo = split(spread(gq_ref[...], pmask))
+    gqhi, gqlo = split(spread(pack_ref[place.gq], pmask))
     ones = jnp.broadcast_to(pmask[None], (rows, HP, 3 * LANE)).astype(F32).reshape(
         rows * HP, 3 * LANE
     )
     ones = ones.astype(BF)
-    qm = spread(query_ref[...].astype(F32), cmask).astype(BF)
-    dosm = spread(dos_ref[...].astype(F32), cmask).astype(BF)
+    qm = spread(pack_ref[place.query], cmask).astype(BF)
+    dosm = spread(vals_ref[vplace.dos], cmask).astype(BF)
     dk = scale * tn(dhi, qm)
     dv = tn(ahi, dosm)
     kpts = tn(dhi, gqhi) + (tn(dhi, gqlo) + tn(dlo, gqhi))
     ksum = tn(dhi, ones) + tn(dlo, ones)
     vpts = tn(ahi, dghi) + (tn(ahi, dglo) + tn(alo, dghi))
-    dgk = coef_lane * (kpts - gk_ref[...] * ksum)
+    dgk = coef_lane * (kpts - pack_ref[place.gk] * ksum)
     mk = back_rotate(dgk, kcols)
     mv = back_rotate(vpts, kcols)
     width = mine_ref.shape[1]
@@ -654,49 +668,43 @@
     w_bias = w_bias.T
     frames = [head_gamma.reshape(1, heads), chain_bias.reshape(1, heads)]
     frames += [rot_q, trans_q, rot_k, trans_k, chain_q.reshape(1, rows), chain_k.reshape(1, keys)]
-    masked, stats, query, key, gq, gk, qcol, kcol = call(
+    inputs = [single_q, single_k, w_query, w_key, w_qpoint, w_kpoint, w_bias, *frames, km]
+    masked, stats, pack = call(
         functools.partial(logits_kernel, heads, channels, npoint),
         "logits",
         [
             sds((n, keys), F32),
             sds((2 * HP, rows), F32),
-            sds((rows, hc), BF),
-            sds((keys, hc), BF),
-            sds((rows, wide), F32),
-            sds((keys, wide), F32),
-            sds((LANE, LANE), F32),
-            sds((keys, LANE), F32),
+            sds(packing(rows, keys, hc).shape, F32),
         ],
         [],
         [pair],
-        [single_q, single_k, w_query, w_key, w_qpoint, w_kpoint, w_bias, *frames, km],
+        inputs,
         [
             pltpu.VMEM((rows, keys, depth), BF),
             pltpu.VMEM((LANE, LANE), F32),
             pltpu.VMEM((LANE, keys), F32),
-            pltpu.SemaphoreType.DMA((4,)),
+            pltpu.SemaphoreType.DMA((1,)),
         ],
         limit=ALONE,
     )
 
     first = [stats] + [permuted(stats, "col", f) for f in (1, 2, 3)]
-    base, gv, d_os, d_pt, doz = call(
+    base, vals, doz = call(
         functools.partial(base_kernel, heads, channels, npoint),
         "base",
         [
             sds((n, keys), F32),
-            sds((keys, wide), F32),
-            sds((rows, hc), BF),
-            sds((rows, 4 * LANE), F32),
+            sds(value_packing(rows, keys, hc).shape, F32),
             sds((n, depth), BF),
         ],
         [],
         [pair],
-        [kcol, single_k, cotangent, w_value, w_vpoint, w_out],
+        [pack, single_k, cotangent, w_value, w_vpoint, w_out],
         [
             pltpu.VMEM((rows, keys, depth), BF),
             pltpu.VMEM((n, depth), F32),
-            pltpu.SemaphoreType.DMA((4,)),
+            pltpu.SemaphoreType.DMA((1,)),
         ],
         pl.CostEstimate(
             flops=8 * n * keys * wide, bytes_accessed=4 * rows * keys * depth, transcendentals=0
@@ -711,7 +719,7 @@
         [sds((n, keys), F32), sds((rows, wide), F32)],
         [],
         [],
-        [masked, base, gv, km, stats],
+        [masked, base, vals, km, stats],
     )
     points = points + sum(permuted(points, "col", f) for f in (1, 2, 3))
     points = points + sum(around(points, f) for f in (1, -2, 3))
@@ -730,7 +738,7 @@
         ],
         [place],
         [],
-        [attn, base, key, gq, gk, gv, d_pt, qcol, points, w_query, w_qpoint],
+        [attn, base, pack, vals, points, w_query, w_qpoint],
     )
 
     moved = permuted(qpart, "col", 1)
@@ -741,7 +749,7 @@
         [half, half],
         [place],
         [],
-        [both, dlo, alo, dglob, query, gq, gk, d_os, qcol, kcol, w_key, w_value, w_kpoint, w_vpoint],
+        [both, dlo, alo, dglob, pack, vals, w_key, w_value, w_kpoint, w_vpoint],
         [],
         pl.CostEstimate(
             flops=2 * n * keys * 12 * wide, bytes_accessed=4 * n * keys, transcendentals=0

time: 105 us -> 103 us (0.981)
  Pallas kernels: 28.7 us -> 27.6 us
    pallas_call x6, Pallas kernels: 24.6 us -> 23.5 us  [call(): pl.pallas_call(kernel, out_shape=outs, in_specs=[SMEM] * len(smem) + [ANY...]
    unnamed x52 -> x38, local copies, waits for them, and re-layouts: 5.95 us -> 4.94 us
  transfers between devices with their start and end apart: 25 -> 25, of which waited for: 13 -> 14; matrix products, arithmetic and copies ran while one was open for 0% -> 0% of each run, Pallas kernels for 12% -> 11%
where the time goes in v5:
time: 103 us; the launch traced here: 102 us
  starting transfers between devices  48.2 us (47%)
  Pallas kernels  27.6 us (27%)
  waiting for transfers between devices  18.6 us (18%)
  local copies, waits for them, and re-layouts  4.96 us (5%)
  other arithmetic  2.05 us (2%)
    ppermute x17, starting transfers between devices, permuted(): return lax.ppermute(x, axis, [(i, i ^ flip) for i in range(size)])  30 us
    pallas_call x6, Pallas kernels, call(): pl.pallas_call(kernel, out_shape=outs, in_specs=[SMEM] * len(smem) + [ANY...  23.5 us
    ppermute x8, starting transfers between devices, around(): return lax.ppermute(x, 'col', moves)  18.3 us
    ppermute x17, waiting for transfers between devices, permuted(): return lax.ppermute(x, axis, [(i, i ^ flip) for i in range(size)])  12.2 us
    ppermute x8, waiting for transfers between devices, around(): return lax.ppermute(x, 'col', moves)  6.35 us
    unnamed x38, local copies, waits for them, and re-layouts  4.94 us
    pallas_call x2, Pallas kernels, pair_part(): pl.pallas_call(pair_kernel, grid=(1,), out_shape=jax.ShapeDtypeStruct((ro...  4.16 us
  transfers between devices with their start and end apart: 25, of which 14 were waited for; matrix products, arithmetic and copies ran while one was open for 0% of the time, Pallas kernels for 11%

profile of v5, /device:TPU:1, one launch (start us, length us, event | category | flops | bytes accessed | tf_op | source)
XLA Modules:
  0.0 102.4 jit_solution(17246784534383801822)
XLA Ops:
  0.7 8.1 %logits.1 = (f32[1024,256]{1,0:T(8,128)}, f32[32,64]{1,0:T(8,128)}, f32[704,384]{1,0:T(8,128)}) custom-call(bf16[64,256,128]{2,1,0:T(8,128)(2,1)} %pair_hbm.3, bf16[64,384]{1,0:T(8,128)(2,1)} %sq_ref.1, bf16[256,384]{1,0:T(8,128)(2,1)} %sk_ref.3, bf16[192,384]{1,0:T(8,128)(2,1)} %bitcast.17, bf16[192,384]{1,0:T(8,128)(2,1)} %bitcast.23, ...), custom_call_target="tpu_custom_call" | custom-call | tf_op jit(solution)/shard_map/logits/pallas_call | solution.py:27
  8.8 2.1 %collective-permute-start = (f32[32,64]{1,0:T(8,128)}, f32[32,64]{1,0:T(8,128)S(1)}, u32[]{:S(2)}, u32[]{:S(2)}) collective-permute-start(f32[32,64]{1,0:T(8,128)} %get-tuple-element.42), channel_id=1, source_target_pairs={{0,1},{1,0},{2,3},{3,2},{4,5},{5,4},{6,7},{7,6},{8,9},{9,8},{10,11... | collective-permute-start | bytes 24584 | tf_op jit(solution)/shard_map/ppermute | solution.py:612
  10.9 1.6 %collective-permute-start.1 = (f32[32,64]{1,0:T(8,128)}, f32[32,64]{1,0:T(8,128)S(1)}, u32[]{:S(2)}, u32[]{:S(2)}) collective-permute-start(f32[32,64]{1,0:T(8,128)} %get-tuple-element.42), channel_id=1, source_target_pairs={{0,2},{1,3},{2,0},{3,1},{4,6},{5,7},{6,4},{7,5},{8,10},{9,11},{10,... | collective-permute-start | bytes 24584 | tf_op jit(solution)/shard_map/ppermute | solution.py:612
  12.6 1.4 %collective-permute-done.1 = f32[32,64]{1,0:T(8,128)S(1)} collective-permute-done((f32[32,64]{1,0:T(8,128)}, f32[32,64]{1,0:T(8,128)S(1)}, u32[]{:S(2)}, u32[]{:S(2)}) %collective-permute-start.1) | collective-permute-done | bytes 8224 | tf_op jit(solution)/shard_map/ppermute | solution.py:612
  13.9 2.3 %collective-permute-done.2 = f32[32,64]{1,0:T(8,128)S(1)} collective-permute-done((f32[32,64]{1,0:T(8,128)}, f32[32,64]{1,0:T(8,128)S(1)}, u32[]{:S(2)}, u32[]{:S(2)}) %collective-permute-start.2) | collective-permute-done | bytes 8224 | tf_op jit(solution)/shard_map/ppermute | solution.py:612
  17.0 5.6 %collective-permute-start.3 = (f32[32,64]{1,0:T(8,128)S(1)}, f32[32,64]{1,0:T(8,128)S(1)}, u32[]{:S(2)}, u32[]{:S(2)}) collective-permute-start(f32[32,64]{1,0:T(8,128)S(1)} %pad_maximum_fusion.1), channel_id=1, source_target_pairs={{10,0},{11,1},{8,2},{9,3},{14,4},{15,5},{12,6},{13,7},{2,8},{3,9},... | collective-permute-start | bytes 24584 | tf_op jit(solution)/shard_map/ppermute | solution.py:623
  22.7 3.1 %collective-permute-start.5 = (f32[32,64]{1,0:T(8,128)S(1)}, f32[32,64]{1,0:T(8,128)S(1)}, u32[]{:S(2)}, u32[]{:S(2)}) collective-permute-start(f32[32,64]{1,0:T(8,128)S(1)} %pad_maximum_fusion.1), channel_id=1, source_target_pairs={{14,0},{15,1},{4,2},{5,3},{2,4},{3,5},{8,6},{9,7},{6,8},{7,9},{12,... | collective-permute-start | bytes 24584 | tf_op jit(solution)/shard_map/ppermute | solution.py:623
  27.1 1.4 %copy-done.3 = bf16[2112,384]{1,0:T(8,128)(2,1)S(1)} copy-done((bf16[2112,384]{1,0:T(8,128)(2,1)S(1)}, bf16[2112,384]{1,0:T(8,128)(2,1)}, u32[]{:S(2)}) %copy-start.3) | copy-done | bytes 1622040
  28.5 3.3 %base.1 = (f32[1024,256]{1,0:T(8,128)S(1)}, f32[384,384]{1,0:T(8,128)S(1)}, bf16[1024,128]{1,0:T(8,128)(2,1)S(1)}) custom-call(bf16[64,256,128]{2,1,0:T(8,128)(2,1)S(1)} %copy-done, f32[704,384]{1,0:T(8,128)S(1)} %copy-done.1, bf16[256,384]{1,0:T(8,128)(2,1)S(1)} %copy-done.8, bf16[64,384]{1,0:T(8,128)(2,1)S(1)} %copy-done.16, ...), custom_call_target="tpu_custom_call" | custom-call | flops 805306368 | bytes 8388608 | tf_op jit(solution)/shard_map/base/pallas_call | solution.py:27
  31.9 1.6 %attend.1 = (f32[1024,256]{1,0:T(8,128)S(1)}, f32[64,384]{1,0:T(8,128)}) custom-call(f32[1024,256]{1,0:T(8,128)S(1)} %copy-done.6, f32[1024,256]{1,0:T(8,128)S(1)} %get-tuple-element.40.base_ref, f32[384,384]{1,0:T(8,128)S(1)} %get-tuple-element.41.vals_ref, s32[1,256]{1,0:T(1,128)S(1)} %bitcast.31, f32[32,64]{1,0:T(8,128)S(1)} %pad_maximum_fusion.2.stats_ref), custom_call_target="tpu_custom_call" | custom-call | tf_op jit(solution)/shard_map/attend/pallas_call | solution.py:27
  34.8 2.4 %collective-permute-start.8 = (f32[64,384]{1,0:T(8,128)}, f32[64,384]{1,0:T(8,128)}, u32[]{:S(2)}, u32[]{:S(2)}) collective-permute-start(f32[64,384]{1,0:T(8,128)} %get-tuple-element.44), channel_id=1, source_target_pairs={{0,3},{1,2},{2,1},{3,0},{4,7},{5,6},{6,5},{7,4},{8,11},{9,10},{10,... | collective-permute-start | bytes 294920 | tf_op jit(solution)/shard_map/ppermute | solution.py:612
  38.5 2.0 %collective-permute-done.8 = f32[64,384]{1,0:T(8,128)} collective-permute-done((f32[64,384]{1,0:T(8,128)}, f32[64,384]{1,0:T(8,128)}, u32[]{:S(2)}, u32[]{:S(2)}) %collective-permute-start.8) | collective-permute-done | bytes 98336 | tf_op jit(solution)/shard_map/ppermute | solution.py:612
  42.0 1.9 %collective-permute-start.11 = (f32[64,384]{1,0:T(8,128)S(1)}, f32[64,384]{1,0:T(8,128)S(1)}, u32[]{:S(2)}, u32[]{:S(2)}) collective-permute-start(f32[64,384]{1,0:T(8,128)S(1)} %add_add_fusion.1), channel_id=1, source_target_pairs={{10,0},{11,1},{8,2},{9,3},{14,4},{15,5},{12,6},{13,7},{2,8},{3,9},... | collective-permute-start | bytes 294920 | tf_op jit(solution)/shard_map/ppermute | solution.py:623
  43.9 2.7 %collective-permute-start.9 = (f32[64,384]{1,0:T(8,128)S(1)}, f32[64,384]{1,0:T(8,128)S(1)}, u32[]{:S(2)}, u32[]{:S(2)}) collective-permute-start(f32[64,384]{1,0:T(8,128)S(1)} %add_add_fusion.1), channel_id=1, source_target_pairs={{14,0},{15,1},{4,2},{5,3},{2,4},{3,5},{8,6},{9,7},{6,8},{7,9},{12,... | collective-permute-start | bytes 294920 | tf_op jit(solution)/shard_map/ppermute | solution.py:623
  46.7 1.9 %collective-permute-done.11 = f32[64,384]{1,0:T(8,128)S(1)} collective-permute-done((f32[64,384]{1,0:T(8,128)S(1)}, f32[64,384]{1,0:T(8,128)S(1)}, u32[]{:S(2)}, u32[]{:S(2)}) %collective-permute-start.11) | collective-permute-done | bytes 98336 | tf_op jit(solution)/shard_map/ppermute | solution.py:623
  48.6 2.1 %collective-permute-done.9 = f32[64,384]{1,0:T(8,128)S(1)} collective-permute-done((f32[64,384]{1,0:T(8,128)S(1)}, f32[64,384]{1,0:T(8,128)S(1)}, u32[]{:S(2)}, u32[]{:S(2)}) %collective-permute-start.9) | collective-permute-done | bytes 98336 | tf_op jit(solution)/shard_map/ppermute | solution.py:623
  52.0 4.9 %query_grads.1 = (f32[72,384]{1,0:T(8,128)S(1)}, bf16[64,32,256]{2,1,0:T(8,128)(2,1)S(1)}, bf16[1024,256]{1,0:T(8,128)(2,1)S(1)}, bf16[1024,256]{1,0:T(8,128)(2,1)S(1)}, f32[64,384]{1,0:T(8,128)S(1)}) custom-call(s32[3]{0:T(128)S(1)} %pad_add_fusion.place_ref, f32[1024,256]{1,0:T(8,128)S(1)} %copy-done.5, f32[1024,256]{1,0:T(8,128)S(1)} %get-tuple-element.40.base_ref, ...), custom_call_target="tpu_custom_call" | custom-call | tf_op jit(solution)/shard_map/query_grads/pallas_call | solution.py:27
  57.8 4.3 %key_grads.1 = (f32[160,384]{1,0:T(8,128)S(1)}, f32[160,384]{1,0:T(8,128)S(1)}) custom-call(s32[3]{0:T(128)S(1)} %pad_add_fusion.place_ref, bf16[64,32,256]{2,1,0:T(8,128)(2,1)S(1)} %get-tuple-element.60.both_ref, bf16[1024,256]{1,0:T(8,128)(2,1)S(1)} %get-tuple-element.47.dlo_ref, bf16[1024,256]{1,0:T(8,128)(2,1)S(1)} %get-tuple-element.48.alo_ref, ...), custom_call_target="tpu_custom_call" | custom-call | flops 2415919104 | bytes 1048576 | tf_op jit(solution)/shard_map/key_grads/pallas_call | solution.py:27
  62.1 5.8 %collective-permute-start.13 = (f32[160,384]{1,0:T(8,128)S(1)}, f32[160,384]{1,0:T(8,128)S(1)}, u32[]{:S(2)}, u32[]{:S(2)}) collective-permute-start(f32[160,384]{1,0:T(8,128)S(1)} %get-tuple-element.53), channel_id=1, source_target_pairs={{0,16},{16,0},{32,48},{48,32},{64,80},{80,64},{96,112},{112,96},{1... | collective-permute-start | bytes 737288 | tf_op jit(solution)/shard_map/ppermute | solution.py:612
  69.1 1.4 %collective-permute-start.14 = (f32[40,384]{1,0:T(8,128)S(1)}, f32[40,384]{1,0:T(8,128)S(1)}, u32[]{:S(2)}, u32[]{:S(2)}) collective-permute-start(f32[40,384]{1,0:T(8,128)S(1)} %get-tuple-element.77), channel_id=1, source_target_pairs={{0,64},{16,80},{32,96},{48,112},{64,0},{80,16},{96,32},{112,48},{1... | collective-permute-start | bytes 184328 | tf_op jit(solution)/shard_map/ppermute | solution.py:612
  70.5 2.6 %collective-permute-start.15 = (f32[40,384]{1,0:T(8,128)S(1)}, f32[40,384]{1,0:T(8,128)S(1)}, u32[]{:S(2)}, u32[]{:S(2)}) collective-permute-start(f32[40,384]{1,0:T(8,128)S(1)} %get-tuple-element.75), channel_id=1, source_target_pairs={{0,128},{16,144},{32,160},{48,176},{64,192},{80,208},{96,224},{112... | collective-permute-start | bytes 184328 | tf_op jit(solution)/shard_map/ppermute | solution.py:612
  73.2 1.9 %collective-permute-start.17 = (f32[72,384]{1,0:T(8,128)S(1)}, f32[72,384]{1,0:T(8,128)S(1)}, u32[]{:S(2)}, u32[]{:S(2)}) collective-permute-start(f32[72,384]{1,0:T(8,128)S(1)} %add.82), channel_id=1, source_target_pairs={{0,2},{1,3},{2,0},{3,1},{4,6},{5,7},{6,4},{7,5},{8,10},{9,11},{10,... | collective-permute-start | bytes 331784 | tf_op jit(solution)/shard_map/ppermute | solution.py:612
  75.1 2.1 %pair_grad.2.refs_0_ = bf16[64,256,128]{2,1,0:T(8,128)(2,1)} custom-call(bf16[64,32,256]{2,1,0:T(8,128)(2,1)S(1)} %get-tuple-element.60.both_ref, bf16[1024,128]{1,0:T(8,128)(2,1)S(1)} %get-tuple-element.56.doz_ref, bf16[12,128]{1,0:T(8,128)(2,1)S(1)} %bitcast.28), custom_call_target="tpu_custom_call" | custom-call | flops 100663296 | bytes 2097152 | tf_op jit(solution)/shard_map/pair_grad/pallas_call | solution.py:593
  77.5 2.7 %collective-permute-start.19 = (f32[72,384]{1,0:T(8,128)S(1)}, f32[72,384]{1,0:T(8,128)S(1)}, u32[]{:S(2)}, u32[]{:S(2)}) collective-permute-start(f32[72,384]{1,0:T(8,128)S(1)} %add.83), channel_id=1, source_target_pairs={{14,0},{15,1},{4,2},{5,3},{2,4},{3,5},{8,6},{9,7},{6,8},{7,9},{12,... | collective-permute-start | bytes 331784 | tf_op jit(solution)/shard_map/ppermute | solution.py:623
  80.2 2.0 %collective-permute-start.18 = (f32[40,384]{1,0:T(8,128)S(1)}, f32[40,384]{1,0:T(8,128)S(1)}, u32[]{:S(2)}, u32[]{:S(2)}) collective-permute-start(f32[40,384]{1,0:T(8,128)S(1)} %add_add_fusion.2), channel_id=1, source_target_pairs={{0,32},{16,48},{32,0},{48,16},{64,96},{80,112},{96,64},{112,80},{1... | collective-permute-start | bytes 184328 | tf_op jit(solution)/shard_map/ppermute | solution.py:612
  82.2 2.1 %pair_grad.3 = bf16[64,256,128]{2,1,0:T(8,128)(2,1)} custom-call(bf16[64,32,256]{2,1,0:T(8,128)(2,1)S(1)} %get-tuple-element.60.both_ref, bf16[1024,128]{1,0:T(8,128)(2,1)S(1)} %get-tuple-element.56.doz_ref, bf16[12,128]{1,0:T(8,128)(2,1)S(1)} %bitcast.29, bf16[64,256,128]{2,1,0:T(8,128)(2,1)} %pair_grad.2.refs_0_), custom_call_target="tpu_custom_call", output_to_operand_aliasing={{}: (3, {})} | custom-call | flops 100663296 | bytes 2097152 | tf_op jit(solution)/shard_map/pair_grad/pallas_call | solution.py:593
  84.9 3.4 %collective-permute-start.21 = (f32[40,384]{1,0:T(8,128)S(1)}, f32[40,384]{1,0:T(8,128)S(1)}, u32[]{:S(2)}, u32[]{:S(2)}) collective-permute-start(f32[40,384]{1,0:T(8,128)S(1)} %add.85), channel_id=1, source_target_pairs={{0,128},{16,144},{32,160},{48,176},{64,192},{80,208},{96,224},{112... | collective-permute-start | bytes 184328 | tf_op jit(solution)/shard_map/ppermute | solution.py:612
  88.8 1.7 %collective-permute-start.23 = (f32[72,384]{1,0:T(8,128)S(1)}, f32[72,384]{1,0:T(8,128)S(1)}, u32[]{:S(2)}, u32[]{:S(2)}) collective-permute-start(f32[72,384]{1,0:T(8,128)S(1)} %add.84.q0_ref), channel_id=1, source_target_pairs={{6,0},{7,1},{12,2},{13,3},{10,4},{11,5},{0,6},{1,7},{14,8},{15,9},... | collective-permute-start | bytes 331784 | tf_op jit(solution)/shard_map/ppermute | solution.py:623
  90.6 2.0 %collective-permute-done.22 = f32[40,384]{1,0:T(8,128)S(1)} collective-permute-done((f32[40,384]{1,0:T(8,128)S(1)}, f32[40,384]{1,0:T(8,128)S(1)}, u32[]{:S(2)}, u32[]{:S(2)}) %collective-permute-start.22) | collective-permute-done | bytes 61472 | tf_op jit(solution)/shard_map/ppermute | solution.py:612
  92.7 2.3 %collective-permute-done.23.q1_ref = f32[72,384]{1,0:T(8,128)S(1)} collective-permute-done((f32[72,384]{1,0:T(8,128)S(1)}, f32[72,384]{1,0:T(8,128)S(1)}, u32[]{:S(2)}, u32[]{:S(2)}) %collective-permute-start.23) | collective-permute-done | bytes 110624 | tf_op jit(solution)/shard_map/ppermute | solution.py:623
  94.9 5.0 %collective-permute-start.24 = (f32[160,384]{1,0:T(8,128)S(1)}, f32[160,384]{1,0:T(8,128)S(1)}, u32[]{:S(2)}, u32[]{:S(2)}) collective-permute-start(f32[160,384]{1,0:T(8,128)S(1)} %pad_maximum_fusion.mine_ref), channel_id=1, source_target_pairs={{0,16},{16,0},{32,48},{48,32},{64,80},{80,64},{96,112},{112,96},{1... | collective-permute-start | bytes 737288 | tf_op jit(solution)/shard_map/ppermute | solution.py:612
  101.0 1.3 %finish.1 = (bf16[64,384]{1,0:T(8,128)(2,1)}, f32[3,64]{1,0:T(4,128)}, bf16[256,384]{1,0:T(8,128)(2,1)}, f32[3,256]{1,0:T(4,128)}) custom-call(s32[3]{0:T(128)S(1)} %pad_add_fusion.place_ref, f32[72,384]{1,0:T(8,128)S(1)} %add.84.q0_ref, f32[72,384]{1,0:T(8,128)S(1)} %collective-permute-done.23.q1_ref, f32[160,384]{1,0:T(8,128)S(1)} %pad_maximum_fusion.mine_ref, ...), custom_call_target="tpu_custom_call" | custom-call | tf_op jit(solution)/shard_map/finish/pallas_call | solution.py:27
  (79 shorter events, 12.3 us)
Async XLA Ops:
  0.6 25.2 %copy-start = (bf16[64,256,128]{2,1,0:T(8,128)(2,1)S(1)}, bf16[64,256,128]{2,1,0:T(8,128)(2,1)}, u32[]{:S(2)}) copy-start(bf16[64,256,128]{2,1,0:T(8,128)(2,1)} %pair_hbm.3) | copy-start | bytes 12582916
  0.6 25.2 %copy-start.8 = (bf16[256,384]{1,0:T(8,128)(2,1)S(1)}, bf16[256,384]{1,0:T(8,128)(2,1)}, u32[]{:S(2)}) copy-start(bf16[256,384]{1,0:T(8,128)(2,1)} %sk_ref.3) | copy-start | bytes 589828
  0.7 25.2 %copy-start.14 = (bf16[384,192]{0,1:T(8,128)(2,1)S(1)}, bf16[384,192]{0,1:T(8,128)(2,1)}, u32[]{:S(2)}) copy-start(bf16[384,192]{0,1:T(8,128)(2,1)} %param.26) | copy-start | bytes 442372
  0.7 25.1 %copy-start.10 = (bf16[384,288]{0,1:T(8,128)(2,1)S(1)}, bf16[384,288]{0,1:T(8,128)(2,1)}, u32[]{:S(2)}) copy-start(bf16[384,288]{0,1:T(8,128)(2,1)} %param.29) | copy-start | bytes 663556
  0.7 25.1 %copy-start.16 = (bf16[64,384]{1,0:T(8,128)(2,1)S(1)}, bf16[64,384]{1,0:T(8,128)(2,1)}, u32[]{:S(2)}) copy-start(bf16[64,384]{1,0:T(8,128)(2,1)} %cot_ref.1) | copy-start | bytes 147460
  8.8 23.1 %copy-start.18 = (s32[256]{0:T(256)S(1)}, s32[256]{0:T(256)}, u32[]{:S(2)}) copy-start(s32[256]{0:T(256)} %param.40) | copy-start | bytes 3076
  8.8 3.8 %collective-permute-start = (f32[32,64]{1,0:T(8,128)}, f32[32,64]{1,0:T(8,128)S(1)}, u32[]{:S(2)}, u32[]{:S(2)}) collective-permute-start(f32[32,64]{1,0:T(8,128)} %get-tuple-element.42), channel_id=1, source_target_pairs={{0,1},{1,0},{2,3},{3,2},{4,5},{5,4},{6,7},{7,6},{8,9},{9,8},{10,11... | collective-permute-start | bytes 24584 | tf_op jit(solution)/shard_map/ppermute | solution.py:612
  10.9 3.0 %collective-permute-start.1 = (f32[32,64]{1,0:T(8,128)}, f32[32,64]{1,0:T(8,128)S(1)}, u32[]{:S(2)}, u32[]{:S(2)}) collective-permute-start(f32[32,64]{1,0:T(8,128)} %get-tuple-element.42), channel_id=1, source_target_pairs={{0,2},{1,3},{2,0},{3,1},{4,6},{5,7},{6,4},{7,5},{8,10},{9,11},{10,... | collective-permute-start | bytes 24584 | tf_op jit(solution)/shard_map/ppermute | solution.py:612
  12.6 3.7 %collective-permute-start.2 = (f32[32,64]{1,0:T(8,128)}, f32[32,64]{1,0:T(8,128)S(1)}, u32[]{:S(2)}, u32[]{:S(2)}) collective-permute-start(f32[32,64]{1,0:T(8,128)} %get-tuple-element.42), channel_id=1, source_target_pairs={{0,3},{1,2},{2,1},{3,0},{4,7},{5,6},{6,5},{7,4},{8,11},{9,10},{10,... | collective-permute-start | bytes 24584 | tf_op jit(solution)/shard_map/ppermute | solution.py:612
  17.0 14.8 %collective-permute-start.3 = (f32[32,64]{1,0:T(8,128)S(1)}, f32[32,64]{1,0:T(8,128)S(1)}, u32[]{:S(2)}, u32[]{:S(2)}) collective-permute-start(f32[32,64]{1,0:T(8,128)S(1)} %pad_maximum_fusion.1), channel_id=1, source_target_pairs={{10,0},{11,1},{8,2},{9,3},{14,4},{15,5},{12,6},{13,7},{2,8},{3,9},... | collective-permute-start | bytes 24584 | tf_op jit(solution)/shard_map/ppermute | solution.py:623
  22.7 9.2 %collective-permute-start.4 = (f32[32,64]{1,0:T(8,128)S(1)}, f32[32,64]{1,0:T(8,128)S(1)}, u32[]{:S(2)}, u32[]{:S(2)}) collective-permute-start(f32[32,64]{1,0:T(8,128)S(1)} %pad_maximum_fusion.1), channel_id=1, source_target_pairs={{4,0},{5,1},{14,2},{15,3},{8,4},{9,5},{2,6},{3,7},{12,8},{13,9},{6... | collective-permute-start | bytes 24584 | tf_op jit(solution)/shard_map/ppermute | solution.py:623
  22.7 9.2 %collective-permute-start.5 = (f32[32,64]{1,0:T(8,128)S(1)}, f32[32,64]{1,0:T(8,128)S(1)}, u32[]{:S(2)}, u32[]{:S(2)}) collective-permute-start(f32[32,64]{1,0:T(8,128)S(1)} %pad_maximum_fusion.1), channel_id=1, source_target_pairs={{14,0},{15,1},{4,2},{5,3},{2,4},{3,5},{8,6},{9,7},{6,8},{7,9},{12,... | collective-permute-start | bytes 24584 | tf_op jit(solution)/shard_map/ppermute | solution.py:623
  31.8 26.0 %copy-start.13 = (bf16[384,192]{0,1:T(8,128)(2,1)S(1)}, bf16[384,192]{0,1:T(8,128)(2,1)}, u32[]{:S(2)}) copy-start(bf16[384,192]{0,1:T(8,128)(2,1)} %param.25) | copy-start | bytes 442372
  34.5 3.8 %collective-permute-start.6 = (f32[64,384]{1,0:T(8,128)}, f32[64,384]{1,0:T(8,128)}, u32[]{:S(2)}, u32[]{:S(2)}) collective-permute-start(f32[64,384]{1,0:T(8,128)} %get-tuple-element.44), channel_id=1, source_target_pairs={{0,1},{1,0},{2,3},{3,2},{4,5},{5,4},{6,7},{7,6},{8,9},{9,8},{10,11... | collective-permute-start | bytes 294920 | tf_op jit(solution)/shard_map/ppermute | solution.py:612
  34.8 3.8 %collective-permute-start.7 = (f32[64,384]{1,0:T(8,128)}, f32[64,384]{1,0:T(8,128)}, u32[]{:S(2)}, u32[]{:S(2)}) collective-permute-start(f32[64,384]{1,0:T(8,128)} %get-tuple-element.44), channel_id=1, source_target_pairs={{0,2},{1,3},{2,0},{3,1},{4,6},{5,7},{6,4},{7,5},{8,10},{9,11},{10,... | collective-permute-start | bytes 294920 | tf_op jit(solution)/shard_map/ppermute | solution.py:612
  34.8 5.8 %collective-permute-start.8 = (f32[64,384]{1,0:T(8,128)}, f32[64,384]{1,0:T(8,128)}, u32[]{:S(2)}, u32[]{:S(2)}) collective-permute-start(f32[64,384]{1,0:T(8,128)} %get-tuple-element.44), channel_id=1, source_target_pairs={{0,3},{1,2},{2,1},{3,0},{4,7},{5,6},{6,5},{7,4},{8,11},{9,10},{10,... | collective-permute-start | bytes 294920 | tf_op jit(solution)/shard_map/ppermute | solution.py:612
  41.6 5.1 %collective-permute-start.10 = (f32[64,384]{1,0:T(8,128)S(1)}, f32[64,384]{1,0:T(8,128)S(1)}, u32[]{:S(2)}, u32[]{:S(2)}) collective-permute-start(f32[64,384]{1,0:T(8,128)S(1)} %add_add_fusion.1), channel_id=1, source_target_pairs={{4,0},{5,1},{14,2},{15,3},{8,4},{9,5},{2,6},{3,7},{12,8},{13,9},{6... | collective-permute-start | bytes 294920 | tf_op jit(solution)/shard_map/ppermute | solution.py:623
  42.0 6.6 %collective-permute-start.11 = (f32[64,384]{1,0:T(8,128)S(1)}, f32[64,384]{1,0:T(8,128)S(1)}, u32[]{:S(2)}, u32[]{:S(2)}) collective-permute-start(f32[64,384]{1,0:T(8,128)S(1)} %add_add_fusion.1), channel_id=1, source_target_pairs={{10,0},{11,1},{8,2},{9,3},{14,4},{15,5},{12,6},{13,7},{2,8},{3,9},... | collective-permute-start | bytes 294920 | tf_op jit(solution)/shard_map/ppermute | solution.py:623
  43.9 6.8 %collective-permute-start.9 = (f32[64,384]{1,0:T(8,128)S(1)}, f32[64,384]{1,0:T(8,128)S(1)}, u32[]{:S(2)}, u32[]{:S(2)}) collective-permute-start(f32[64,384]{1,0:T(8,128)S(1)} %add_add_fusion.1), channel_id=1, source_target_pairs={{14,0},{15,1},{4,2},{5,3},{2,4},{3,5},{8,6},{9,7},{6,8},{7,9},{12,... | collective-permute-start | bytes 294920 | tf_op jit(solution)/shard_map/ppermute | solution.py:623
  56.9 5.2 %collective-permute-start.12 = (f32[72,384]{1,0:T(8,128)S(1)}, f32[72,384]{1,0:T(8,128)S(1)}, u32[]{:S(2)}, u32[]{:S(2)}) collective-permute-start(f32[72,384]{1,0:T(8,128)S(1)} %get-tuple-element.45), channel_id=1, source_target_pairs={{0,1},{1,0},{2,3},{3,2},{4,5},{5,4},{6,7},{7,6},{8,9},{9,8},{10,11... | collective-permute-start | bytes 331784 | tf_op jit(solution)/shard_map/ppermute | solution.py:612
  62.1 7.0 %collective-permute-start.13 = (f32[160,384]{1,0:T(8,128)S(1)}, f32[160,384]{1,0:T(8,128)S(1)}, u32[]{:S(2)}, u32[]{:S(2)}) collective-permute-start(f32[160,384]{1,0:T(8,128)S(1)} %get-tuple-element.53), channel_id=1, source_target_pairs={{0,16},{16,0},{32,48},{48,32},{64,80},{80,64},{96,112},{112,96},{1... | collective-permute-start | bytes 737288 | tf_op jit(solution)/shard_map/ppermute | solution.py:612
  69.1 8.0 %collective-permute-start.14 = (f32[40,384]{1,0:T(8,128)S(1)}, f32[40,384]{1,0:T(8,128)S(1)}, u32[]{:S(2)}, u32[]{:S(2)}) collective-permute-start(f32[40,384]{1,0:T(8,128)S(1)} %get-tuple-element.77), channel_id=1, source_target_pairs={{0,64},{16,80},{32,96},{48,112},{64,0},{80,16},{96,32},{112,48},{1... | collective-permute-start | bytes 184328 | tf_op jit(solution)/shard_map/ppermute | solution.py:612
  70.5 6.6 %collective-permute-start.15 = (f32[40,384]{1,0:T(8,128)S(1)}, f32[40,384]{1,0:T(8,128)S(1)}, u32[]{:S(2)}, u32[]{:S(2)}) collective-permute-start(f32[40,384]{1,0:T(8,128)S(1)} %get-tuple-element.75), channel_id=1, source_target_pairs={{0,128},{16,144},{32,160},{48,176},{64,192},{80,208},{96,224},{112... | collective-permute-start | bytes 184328 | tf_op jit(solution)/shard_map/ppermute | solution.py:612
  73.1 4.3 %collective-permute-start.16 = (f32[40,384]{1,0:T(8,128)S(1)}, f32[40,384]{1,0:T(8,128)S(1)}, u32[]{:S(2)}, u32[]{:S(2)}) collective-permute-start(f32[40,384]{1,0:T(8,128)S(1)} %get-tuple-element.76), channel_id=1, source_target_pairs={{0,192},{16,208},{32,224},{48,240},{64,128},{80,144},{96,160},{112... | collective-permute-start | bytes 184328 | tf_op jit(solution)/shard_map/ppermute | solution.py:612
  73.2 4.3 %collective-permute-start.17 = (f32[72,384]{1,0:T(8,128)S(1)}, f32[72,384]{1,0:T(8,128)S(1)}, u32[]{:S(2)}, u32[]{:S(2)}) collective-permute-start(f32[72,384]{1,0:T(8,128)S(1)} %add.82), channel_id=1, source_target_pairs={{0,2},{1,3},{2,0},{3,1},{4,6},{5,7},{6,4},{7,5},{8,10},{9,11},{10,... | collective-permute-start | bytes 331784 | tf_op jit(solution)/shard_map/ppermute | solution.py:612
  77.5 7.3 %collective-permute-start.19 = (f32[72,384]{1,0:T(8,128)S(1)}, f32[72,384]{1,0:T(8,128)S(1)}, u32[]{:S(2)}, u32[]{:S(2)}) collective-permute-start(f32[72,384]{1,0:T(8,128)S(1)} %add.83), channel_id=1, source_target_pairs={{14,0},{15,1},{4,2},{5,3},{2,4},{3,5},{8,6},{9,7},{6,8},{7,9},{12,... | collective-permute-start | bytes 331784 | tf_op jit(solution)/shard_map/ppermute | solution.py:623
  80.2 4.6 %collective-permute-start.18 = (f32[40,384]{1,0:T(8,128)S(1)}, f32[40,384]{1,0:T(8,128)S(1)}, u32[]{:S(2)}, u32[]{:S(2)}) collective-permute-start(f32[40,384]{1,0:T(8,128)S(1)} %add_add_fusion.2), channel_id=1, source_target_pairs={{0,32},{16,48},{32,0},{48,16},{64,96},{80,112},{96,64},{112,80},{1... | collective-permute-start | bytes 184328 | tf_op jit(solution)/shard_map/ppermute | solution.py:612
  84.8 5.7 %collective-permute-start.20 = (f32[40,384]{1,0:T(8,128)S(1)}, f32[40,384]{1,0:T(8,128)S(1)}, u32[]{:S(2)}, u32[]{:S(2)}) collective-permute-start(f32[40,384]{1,0:T(8,128)S(1)} %add.85), channel_id=1, source_target_pairs={{0,64},{16,80},{32,96},{48,112},{64,0},{80,16},{96,32},{112,48},{1... | collective-permute-start | bytes 184328 | tf_op jit(solution)/shard_map/ppermute | solution.py:612
  84.9 5.7 %collective-permute-start.21 = (f32[40,384]{1,0:T(8,128)S(1)}, f32[40,384]{1,0:T(8,128)S(1)}, u32[]{:S(2)}, u32[]{:S(2)}) collective-permute-start(f32[40,384]{1,0:T(8,128)S(1)} %add.85), channel_id=1, source_target_pairs={{0,128},{16,144},{32,160},{48,176},{64,192},{80,208},{96,224},{112... | collective-permute-start | bytes 184328 | tf_op jit(solution)/shard_map/ppermute | solution.py:612
  88.4 4.3 %collective-permute-start.22 = (f32[40,384]{1,0:T(8,128)S(1)}, f32[40,384]{1,0:T(8,128)S(1)}, u32[]{:S(2)}, u32[]{:S(2)}) collective-permute-start(f32[40,384]{1,0:T(8,128)S(1)} %add.85), channel_id=1, source_target_pairs={{0,192},{16,208},{32,224},{48,240},{64,128},{80,144},{96,160},{112... | collective-permute-start | bytes 184328 | tf_op jit(solution)/shard_map/ppermute | solution.py:612
  88.8 6.2 %collective-permute-start.23 = (f32[72,384]{1,0:T(8,128)S(1)}, f32[72,384]{1,0:T(8,128)S(1)}, u32[]{:S(2)}, u32[]{:S(2)}) collective-permute-start(f32[72,384]{1,0:T(8,128)S(1)} %add.84.q0_ref), channel_id=1, source_target_pairs={{6,0},{7,1},{12,2},{13,3},{10,4},{11,5},{0,6},{1,7},{14,8},{15,9},... | collective-permute-start | bytes 331784 | tf_op jit(solution)/shard_map/ppermute | solution.py:623
  94.9 6.1 %collective-permute-start.24 = (f32[160,384]{1,0:T(8,128)S(1)}, f32[160,384]{1,0:T(8,128)S(1)}, u32[]{:S(2)}, u32[]{:S(2)}) collective-permute-start(f32[160,384]{1,0:T(8,128)S(1)} %pad_maximum_fusion.mine_ref), channel_id=1, source_target_pairs={{0,16},{16,0},{32,48},{48,32},{64,80},{80,64},{96,112},{112,96},{1... | collective-permute-start | bytes 737288 | tf_op jit(solution)/shard_map/ppermute | solution.py:612
  (12 other events, 154.5 us)

commit v6 on v5

--- a/solution.py
+++ b/solution.py
@@ -265,7 +265,7 @@
     heads,
     channels,
     npoint,
-    pair_hbm,
+    pair_ref,
     pack_ref,
     sk_ref,
     cot_ref,
@@ -275,13 +275,10 @@
     base_ref,
     vals_ref,
     doz_ref,
-    pair_ref,
     lhs_ref,
-    sems,
 ):
-    rows, keys, depth = pair_hbm.shape
+    rows, keys, depth = pair_ref.shape
     hp = heads * npoint
-    copies, step = load_pair(pair_hbm, pair_ref, sems)
     sk = sk_ref[...]
     cot = cot_ref[...]
     value = nt(sk, wv_ref[...]).astype(BF)
@@ -302,28 +299,16 @@
     doz_ref[...] = lhs_ref[...].astype(BF)
     dosm = spread(dos.astype(F32), channel_mask(heads, channels)).astype(BF)
     base_ref[...] = nt(dosm, value)
-    for c, copy in enumerate(copies):
-        copy.wait()
-
-        def one(i, carry):
-            r = pl.multiple_of(i * HP, HP)
-            base_ref[pl.ds(r, HP), :] += nt(doz_ref[pl.ds(r, HP), :], pair_ref[i])
-            return carry
-
-        lax.fori_loop(c * step, (c + 1) * step, one, 0, unroll=16)
-
-
-def attend_kernel(
-    heads,
-    npoint,
-    masked_ref,
-    base_ref,
-    vals_ref,
-    km_ref,
-    stats_ref,
-    attn_ref,
-    out_ref,
-):
+
+    def one(i, carry):
+        r = pl.multiple_of(i * HP, HP)
+        base_ref[pl.ds(r, HP), :] += nt(doz_ref[pl.ds(r, HP), :], pair_ref[i])
+        return carry
+
+    lax.fori_loop(0, rows, one, 0, unroll=16)
+
+
+def softmax_rows(masked_ref, km_ref, stats_ref):
     rows = stats_ref.shape[1]
     stats = jnp.concatenate(
         [stats_ref[...], jnp.zeros((LANE - stats_ref.shape[0], rows), F32)], axis=0
@@ -331,14 +316,15 @@
     top = to_col(stats)
     total = to_col(stats, HP)
     valid = km_ref[...] == 1
-    attn = jnp.where(valid, jnp.exp(masked_ref[...] - top), 0.0) / total
-    attn_ref[...] = attn
-    attn_b = attn.astype(BF)
-    attn_f = attn_b.astype(F32)
+    return jnp.where(valid, jnp.exp(masked_ref[...] - top), 0.0) / total
+
+
+def attend_kernel(heads, npoint, masked_ref, base_ref, vals_ref, km_ref, stats_ref, out_ref):
+    attn_b = softmax_rows(masked_ref, km_ref, stats_ref).astype(BF)
     ghi, glo = split(vals_ref[0 : masked_ref.shape[1], :])
     opt = nn(attn_b, ghi) + nn(attn_b, glo)
     pmask = head_mask(heads, npoint, 3 * LANE)
-    delta = jnp.sum(attn_f * base_ref[...], axis=1, keepdims=True)
+    delta = jnp.sum(attn_b.astype(F32) * base_ref[...], axis=1, keepdims=True)
     out_ref[...] = gather_heads(opt, pmask)
     out_ref[:, 0:LANE] += to_lanes(delta, heads * npoint)
 
@@ -371,7 +357,9 @@
     channels,
     npoint,
     place_ref,
-    attn_ref,
+    masked_ref,
+    km_ref,
+    stats_ref,
     base_ref,
     pack_ref,
     vals_ref,
@@ -414,7 +402,7 @@
     delta = delta0 + jnp.sum(spread(opt_row * dglob, pmask), axis=1, keepdims=True)
     gvhi, gvlo = split(vals_ref[vplace.gv])
     dattn = base_ref[...] + nt(dghi, gvhi) + (nt(dghi, gvlo) + nt(dglo, gvhi))
-    attn = attn_ref[...]
+    attn = softmax_rows(masked_ref, km_ref, stats_ref)
     dlogit = attn * (dattn - delta)
     dhi, dlo = split(dlogit)
     ahi, alo = split(attn)
@@ -699,13 +687,9 @@
             sds((n, depth), BF),
         ],
         [],
-        [pair],
-        [pack, single_k, cotangent, w_value, w_vpoint, w_out],
-        [
-            pltpu.VMEM((rows, keys, depth), BF),
-            pltpu.VMEM((n, depth), F32),
-            pltpu.SemaphoreType.DMA((1,)),
-        ],
+        [],
+        [pair, pack, single_k, cotangent, w_value, w_vpoint, w_out],
+        [pltpu.VMEM((n, depth), F32)],
         pl.CostEstimate(
             flops=8 * n * keys * wide, bytes_accessed=4 * rows * keys * depth, transcendentals=0
         ),
@@ -713,14 +697,14 @@
     stats = merged(first)
     stats = merged([stats] + [around(stats, f) for f in (3, -2, 1)])
 
-    attn, points = call(
+    points = call(
         functools.partial(attend_kernel, heads, npoint),
         "attend",
-        [sds((n, keys), F32), sds((rows, wide), F32)],
+        [sds((rows, wide), F32)],
         [],
         [],
         [masked, base, vals, km, stats],
-    )
+    )[0]
     points = points + sum(permuted(points, "col", f) for f in (1, 2, 3))
     points = points + sum(around(points, f) for f in (1, -2, 3))
 
@@ -738,7 +722,7 @@
         ],
         [place],
         [],
-        [attn, base, pack, vals, points, w_query, w_qpoint],
+        [masked, km, stats, base, pack, vals, points, w_query, w_qpoint],
     )
 
     moved = permuted(qpart, "col", 1)
@@ -767,13 +751,13 @@
     held, both, pair_grad, moved = lax.optimization_barrier((held, both, pair_grad, moved))
     qpart = qpart + moved
     received = permuted(held, "row", 2)
-    moved = around(qpart, 1)
+    moved = around(qpart, 3)
     pair_grad = pair_part(1, 2, both, doz, w_bias, pair_grad, params)
     received, moved, pair_grad = lax.optimization_barrier((received, moved, pair_grad))
     held = held + received
     qpart = qpart + moved
     mine = jnp.concatenate([held] + [permuted(held, "row", 4 * f) for f in (1, 2, 3)], axis=0)
-    moved = around(qpart, -3)
+    moved = around(qpart, 1)
     mine, moved = lax.optimization_barrier((mine, moved))
     other = permuted(mine, "row", 1)
     grad_q, shift_q, grad_k, shift_k = call(

time: 103 us -> 103 us (level)
  local copies, waits for them, and re-layouts: 4.96 us -> 7.13 us
  waiting for transfers between devices: 18.6 us -> 17 us
  starting transfers between devices: 48.2 us -> 49.3 us
    unnamed x38 -> x42, local copies, waits for them, and re-layouts: 4.94 us -> 7.11 us
    ppermute x8, waiting for transfers between devices: 6.35 us -> 5 us  [around(): return lax.ppermute(x, 'col', moves)]
    pallas_call x6, Pallas kernels: 23.5 us -> 22.4 us  [call(): pl.pallas_call(kernel, out_shape=outs, in_specs=[SMEM] * len(smem) + [ANY...]
  transfers between devices with their start and end apart: 25 -> 25, of which waited for: 14 -> 13; matrix products, arithmetic and copies ran while one was open for 0% -> 0% of each run, Pallas kernels for 11% -> 11%
where the time goes in v6:
time: 103 us
  starting transfers between devices  49.3 us (48%)
  Pallas kernels  26.6 us (26%)
  waiting for transfers between devices  17 us (17%)
  local copies, waits for them, and re-layouts  7.13 us (7%)
  other arithmetic  1.99 us (2%)
    ppermute x17, starting transfers between devices, permuted(): return lax.ppermute(x, axis, [(i, i ^ flip) for i in range(size)])  30.6 us
    pallas_call x6, Pallas kernels, call(): pl.pallas_call(kernel, out_shape=outs, in_specs=[SMEM] * len(smem) + [ANY...  22.4 us
    ppermute x8, starting transfers between devices, around(): return lax.ppermute(x, 'col', moves)  18.8 us
    ppermute x17, waiting for transfers between devices, permuted(): return lax.ppermute(x, axis, [(i, i ^ flip) for i in range(size)])  12 us
    unnamed x42, local copies, waits for them, and re-layouts  7.11 us
    ppermute x8, waiting for transfers between devices, around(): return lax.ppermute(x, 'col', moves)  5 us
    pallas_call x2, Pallas kernels, pair_part(): pl.pallas_call(pair_kernel, grid=(1,), out_shape=jax.ShapeDtypeStruct((ro...  4.16 us
  transfers between devices with their start and end apart: 25, of which 13 were waited for; matrix products, arithmetic and copies ran while one was open for 0% of the time, Pallas kernels for 11%

profile of v6, /device:TPU:1, one launch (start us, length us, event | category | flops | bytes accessed | tf_op | source)
XLA Modules:
  0.0 103.0 jit_solution(1896736598927206097)
XLA Ops:
  0.7 8.1 %logits.1 = (f32[1024,256]{1,0:T(8,128)}, f32[32,64]{1,0:T(8,128)}, f32[704,384]{1,0:T(8,128)}) custom-call(bf16[64,256,128]{2,1,0:T(8,128)(2,1)} %pair_ref.1, bf16[64,384]{1,0:T(8,128)(2,1)} %sq_ref.1, bf16[256,384]{1,0:T(8,128)(2,1)} %sk_ref.3, bf16[192,384]{1,0:T(8,128)(2,1)} %bitcast.17, bf16[192,384]{1,0:T(8,128)(2,1)} %bitcast.23, ...), custom_call_target="tpu_custom_call" | custom-call | tf_op jit(solution)/shard_map/logits/pallas_call | solution.py:27
  8.8 2.1 %collective-permute-start = (f32[32,64]{1,0:T(8,128)}, f32[32,64]{1,0:T(8,128)S(1)}, u32[]{:S(2)}, u32[]{:S(2)}) collective-permute-start(f32[32,64]{1,0:T(8,128)} %get-tuple-element.37), channel_id=1, source_target_pairs={{0,1},{1,0},{2,3},{3,2},{4,5},{5,4},{6,7},{7,6},{8,9},{9,8},{10,11... | collective-permute-start | bytes 24584 | tf_op jit(solution)/shard_map/ppermute | solution.py:600
  10.9 1.6 %collective-permute-start.1 = (f32[32,64]{1,0:T(8,128)}, f32[32,64]{1,0:T(8,128)S(1)}, u32[]{:S(2)}, u32[]{:S(2)}) collective-permute-start(f32[32,64]{1,0:T(8,128)} %get-tuple-element.37), channel_id=1, source_target_pairs={{0,2},{1,3},{2,0},{3,1},{4,6},{5,7},{6,4},{7,5},{8,10},{9,11},{10,... | collective-permute-start | bytes 24584 | tf_op jit(solution)/shard_map/ppermute | solution.py:600
  12.6 1.4 %collective-permute-done.1 = f32[32,64]{1,0:T(8,128)S(1)} collective-permute-done((f32[32,64]{1,0:T(8,128)}, f32[32,64]{1,0:T(8,128)S(1)}, u32[]{:S(2)}, u32[]{:S(2)}) %collective-permute-start.1) | collective-permute-done | bytes 8224 | tf_op jit(solution)/shard_map/ppermute | solution.py:600
  13.9 2.3 %collective-permute-done.2 = f32[32,64]{1,0:T(8,128)S(1)} collective-permute-done((f32[32,64]{1,0:T(8,128)}, f32[32,64]{1,0:T(8,128)S(1)}, u32[]{:S(2)}, u32[]{:S(2)}) %collective-permute-start.2) | collective-permute-done | bytes 8224 | tf_op jit(solution)/shard_map/ppermute | solution.py:600
  17.0 5.6 %collective-permute-start.3 = (f32[32,64]{1,0:T(8,128)S(1)}, f32[32,64]{1,0:T(8,128)S(1)}, u32[]{:S(2)}, u32[]{:S(2)}) collective-permute-start(f32[32,64]{1,0:T(8,128)S(1)} %pad_maximum_fusion.1), channel_id=1, source_target_pairs={{10,0},{11,1},{8,2},{9,3},{14,4},{15,5},{12,6},{13,7},{2,8},{3,9},... | collective-permute-start | bytes 24584 | tf_op jit(solution)/shard_map/ppermute | solution.py:611
  22.7 3.1 %collective-permute-start.5 = (f32[32,64]{1,0:T(8,128)S(1)}, f32[32,64]{1,0:T(8,128)S(1)}, u32[]{:S(2)}, u32[]{:S(2)}) collective-permute-start(f32[32,64]{1,0:T(8,128)S(1)} %pad_maximum_fusion.1), channel_id=1, source_target_pairs={{14,0},{15,1},{4,2},{5,3},{2,4},{3,5},{8,6},{9,7},{6,8},{7,9},{12,... | collective-permute-start | bytes 24584 | tf_op jit(solution)/shard_map/ppermute | solution.py:611
  25.8 1.2 %copy-done.1 = f32[704,384]{1,0:T(8,128)S(1)} copy-done((f32[704,384]{1,0:T(8,128)S(1)}, f32[704,384]{1,0:T(8,128)}, u32[]{:S(2)}) %copy-start.1) | copy-done | bytes 1081368
  27.1 1.4 %copy-done.7 = bf16[2112,384]{1,0:T(8,128)(2,1)S(1)} copy-done((bf16[2112,384]{1,0:T(8,128)(2,1)S(1)}, bf16[2112,384]{1,0:T(8,128)(2,1)}, u32[]{:S(2)}) %copy-start.7) | copy-done | bytes 1622040
  28.5 3.0 %base.1 = (f32[1024,256]{1,0:T(8,128)S(1)}, f32[384,384]{1,0:T(8,128)S(1)}, bf16[1024,128]{1,0:T(8,128)(2,1)S(1)}) custom-call(bf16[64,256,128]{2,1,0:T(8,128)(2,1)S(1)} %copy-done, f32[704,384]{1,0:T(8,128)S(1)} %copy-done.1, bf16[256,384]{1,0:T(8,128)(2,1)S(1)} %copy-done.9, bf16[64,384]{1,0:T(8,128)(2,1)S(1)} %copy-done.17, ...), custom_call_target="tpu_custom_call" | custom-call | flops 805306368 | bytes 8388608 | tf_op jit(solution)/shard_map/base/pallas_call | solution.py:27
  33.5 2.4 %collective-permute-start.8 = (f32[64,384]{1,0:T(8,128)S(1)}, f32[64,384]{1,0:T(8,128)}, u32[]{:S(2)}, u32[]{:S(2)}) collective-permute-start(f32[64,384]{1,0:T(8,128)S(1)} %attend.1), channel_id=1, source_target_pairs={{0,3},{1,2},{2,1},{3,0},{4,7},{5,6},{6,5},{7,4},{8,11},{9,10},{10,... | collective-permute-start | bytes 294920 | tf_op jit(solution)/shard_map/ppermute | solution.py:600
  37.1 2.0 %collective-permute-done.8 = f32[64,384]{1,0:T(8,128)} collective-permute-done((f32[64,384]{1,0:T(8,128)S(1)}, f32[64,384]{1,0:T(8,128)}, u32[]{:S(2)}, u32[]{:S(2)}) %collective-permute-start.8) | collective-permute-done | bytes 98336 | tf_op jit(solution)/shard_map/ppermute | solution.py:600
  40.5 1.9 %collective-permute-start.11 = (f32[64,384]{1,0:T(8,128)S(1)}, f32[64,384]{1,0:T(8,128)S(1)}, u32[]{:S(2)}, u32[]{:S(2)}) collective-permute-start(f32[64,384]{1,0:T(8,128)S(1)} %add_add_fusion.1), channel_id=1, source_target_pairs={{10,0},{11,1},{8,2},{9,3},{14,4},{15,5},{12,6},{13,7},{2,8},{3,9},... | collective-permute-start | bytes 294920 | tf_op jit(solution)/shard_map/ppermute | solution.py:611
  42.4 2.7 %collective-permute-start.9 = (f32[64,384]{1,0:T(8,128)S(1)}, f32[64,384]{1,0:T(8,128)S(1)}, u32[]{:S(2)}, u32[]{:S(2)}) collective-permute-start(f32[64,384]{1,0:T(8,128)S(1)} %add_add_fusion.1), channel_id=1, source_target_pairs={{14,0},{15,1},{4,2},{5,3},{2,4},{3,5},{8,6},{9,7},{6,8},{7,9},{12,... | collective-permute-start | bytes 294920 | tf_op jit(solution)/shard_map/ppermute | solution.py:611
  45.2 1.9 %collective-permute-done.11 = f32[64,384]{1,0:T(8,128)S(1)} collective-permute-done((f32[64,384]{1,0:T(8,128)S(1)}, f32[64,384]{1,0:T(8,128)S(1)}, u32[]{:S(2)}, u32[]{:S(2)}) %collective-permute-start.11) | collective-permute-done | bytes 98336 | tf_op jit(solution)/shard_map/ppermute | solution.py:611
  47.1 2.1 %collective-permute-done.9 = f32[64,384]{1,0:T(8,128)S(1)} collective-permute-done((f32[64,384]{1,0:T(8,128)S(1)}, f32[64,384]{1,0:T(8,128)S(1)}, u32[]{:S(2)}, u32[]{:S(2)}) %collective-permute-start.9) | collective-permute-done | bytes 98336 | tf_op jit(solution)/shard_map/ppermute | solution.py:611
  52.9 4.9 %query_grads.1 = (f32[72,384]{1,0:T(8,128)S(1)}, bf16[64,32,256]{2,1,0:T(8,128)(2,1)S(1)}, bf16[1024,256]{1,0:T(8,128)(2,1)S(1)}, bf16[1024,256]{1,0:T(8,128)(2,1)S(1)}, f32[64,384]{1,0:T(8,128)S(1)}) custom-call(s32[3]{0:T(128)S(1)} %pad_add_fusion.place_ref, f32[1024,256]{1,0:T(8,128)S(1)} %copy-done.3, s32[1,256]{1,0:T(1,128)S(1)} %bitcast.32, ...), custom_call_target="tpu_custom_call" | custom-call | tf_op jit(solution)/shard_map/query_grads/pallas_call | solution.py:27
  58.6 4.3 %key_grads.1 = (f32[160,384]{1,0:T(8,128)S(1)}, f32[160,384]{1,0:T(8,128)S(1)}) custom-call(s32[3]{0:T(128)S(1)} %pad_add_fusion.place_ref, bf16[64,32,256]{2,1,0:T(8,128)(2,1)S(1)} %get-tuple-element.56.both_ref, bf16[1024,256]{1,0:T(8,128)(2,1)S(1)} %get-tuple-element.43.dlo_ref, bf16[1024,256]{1,0:T(8,128)(2,1)S(1)} %get-tuple-element.44.alo_ref, ...), custom_call_target="tpu_custom_call" | custom-call | flops 2415919104 | bytes 1048576 | tf_op jit(solution)/shard_map/key_grads/pallas_call | solution.py:27
  62.9 5.9 %collective-permute-start.13 = (f32[160,384]{1,0:T(8,128)S(1)}, f32[160,384]{1,0:T(8,128)S(1)}, u32[]{:S(2)}, u32[]{:S(2)}) collective-permute-start(f32[160,384]{1,0:T(8,128)S(1)} %get-tuple-element.49), channel_id=1, source_target_pairs={{0,16},{16,0},{32,48},{48,32},{64,80},{80,64},{96,112},{112,96},{1... | collective-permute-start | bytes 737288 | tf_op jit(solution)/shard_map/ppermute | solution.py:600
  68.8 1.1 %collective-permute-done.13 = f32[160,384]{1,0:T(8,128)S(1)} collective-permute-done((f32[160,384]{1,0:T(8,128)S(1)}, f32[160,384]{1,0:T(8,128)S(1)}, u32[]{:S(2)}, u32[]{:S(2)}) %collective-permute-start.13) | collective-permute-done | bytes 245792 | tf_op jit(solution)/shard_map/ppermute | solution.py:600
  70.0 1.4 %collective-permute-start.14 = (f32[40,384]{1,0:T(8,128)S(1)}, f32[40,384]{1,0:T(8,128)S(1)}, u32[]{:S(2)}, u32[]{:S(2)}) collective-permute-start(f32[40,384]{1,0:T(8,128)S(1)} %get-tuple-element.73), channel_id=1, source_target_pairs={{0,64},{16,80},{32,96},{48,112},{64,0},{80,16},{96,32},{112,48},{1... | collective-permute-start | bytes 184328 | tf_op jit(solution)/shard_map/ppermute | solution.py:600
  71.4 2.6 %collective-permute-start.15 = (f32[40,384]{1,0:T(8,128)S(1)}, f32[40,384]{1,0:T(8,128)S(1)}, u32[]{:S(2)}, u32[]{:S(2)}) collective-permute-start(f32[40,384]{1,0:T(8,128)S(1)} %get-tuple-element.71), channel_id=1, source_target_pairs={{0,128},{16,144},{32,160},{48,176},{64,192},{80,208},{96,224},{112... | collective-permute-start | bytes 184328 | tf_op jit(solution)/shard_map/ppermute | solution.py:600
  74.0 1.9 %collective-permute-start.17 = (f32[72,384]{1,0:T(8,128)S(1)}, f32[72,384]{1,0:T(8,128)S(1)}, u32[]{:S(2)}, u32[]{:S(2)}) collective-permute-start(f32[72,384]{1,0:T(8,128)S(1)} %add.82), channel_id=1, source_target_pairs={{0,2},{1,3},{2,0},{3,1},{4,6},{5,7},{6,4},{7,5},{8,10},{9,11},{10,... | collective-permute-start | bytes 331784 | tf_op jit(solution)/shard_map/ppermute | solution.py:600
  75.9 2.1 %pair_grad.2.refs_0_ = bf16[64,256,128]{2,1,0:T(8,128)(2,1)} custom-call(bf16[64,32,256]{2,1,0:T(8,128)(2,1)S(1)} %get-tuple-element.56.both_ref, bf16[1024,128]{1,0:T(8,128)(2,1)S(1)} %get-tuple-element.52.doz_ref, bf16[12,128]{1,0:T(8,128)(2,1)S(1)} %bitcast.28), custom_call_target="tpu_custom_call" | custom-call | flops 100663296 | bytes 2097152 | tf_op jit(solution)/shard_map/pair_grad/pallas_call | solution.py:581
  78.3 2.8 %collective-permute-start.19 = (f32[72,384]{1,0:T(8,128)S(1)}, f32[72,384]{1,0:T(8,128)S(1)}, u32[]{:S(2)}, u32[]{:S(2)}) collective-permute-start(f32[72,384]{1,0:T(8,128)S(1)} %add.83), channel_id=1, source_target_pairs={{10,0},{11,1},{8,2},{9,3},{14,4},{15,5},{12,6},{13,7},{2,8},{3,9},... | collective-permute-start | bytes 331784 | tf_op jit(solution)/shard_map/ppermute | solution.py:611
  81.2 1.7 %collective-permute-start.18 = (f32[40,384]{1,0:T(8,128)S(1)}, f32[40,384]{1,0:T(8,128)S(1)}, u32[]{:S(2)}, u32[]{:S(2)}) collective-permute-start(f32[40,384]{1,0:T(8,128)S(1)} %add_add_fusion.2), channel_id=1, source_target_pairs={{0,32},{16,48},{32,0},{48,16},{64,96},{80,112},{96,64},{112,80},{1... | collective-permute-start | bytes 184328 | tf_op jit(solution)/shard_map/ppermute | solution.py:600
  82.9 2.1 %pair_grad.3 = bf16[64,256,128]{2,1,0:T(8,128)(2,1)} custom-call(bf16[64,32,256]{2,1,0:T(8,128)(2,1)S(1)} %get-tuple-element.56.both_ref, bf16[1024,128]{1,0:T(8,128)(2,1)S(1)} %get-tuple-element.52.doz_ref, bf16[12,128]{1,0:T(8,128)(2,1)S(1)} %bitcast.29, bf16[64,256,128]{2,1,0:T(8,128)(2,1)} %pair_grad.2.refs_0_), custom_call_target="tpu_custom_call", output_to_operand_aliasing={{}: (3, {})} | custom-call | flops 100663296 | bytes 2097152 | tf_op jit(solution)/shard_map/pair_grad/pallas_call | solution.py:581
  85.9 3.5 %collective-permute-start.21 = (f32[40,384]{1,0:T(8,128)S(1)}, f32[40,384]{1,0:T(8,128)S(1)}, u32[]{:S(2)}, u32[]{:S(2)}) collective-permute-start(f32[40,384]{1,0:T(8,128)S(1)} %add.85), channel_id=1, source_target_pairs={{0,128},{16,144},{32,160},{48,176},{64,192},{80,208},{96,224},{112... | collective-permute-start | bytes 184328 | tf_op jit(solution)/shard_map/ppermute | solution.py:600
  89.7 2.2 %collective-permute-start.23 = (f32[72,384]{1,0:T(8,128)S(1)}, f32[72,384]{1,0:T(8,128)S(1)}, u32[]{:S(2)}, u32[]{:S(2)}) collective-permute-start(f32[72,384]{1,0:T(8,128)S(1)} %add.84.q0_ref), channel_id=1, source_target_pairs={{14,0},{15,1},{4,2},{5,3},{2,4},{3,5},{8,6},{9,7},{6,8},{7,9},{12,... | collective-permute-start | bytes 331784 | tf_op jit(solution)/shard_map/ppermute | solution.py:611
  91.9 1.8 %collective-permute-done.22 = f32[40,384]{1,0:T(8,128)S(1)} collective-permute-done((f32[40,384]{1,0:T(8,128)S(1)}, f32[40,384]{1,0:T(8,128)S(1)}, u32[]{:S(2)}, u32[]{:S(2)}) %collective-permute-start.22) | collective-permute-done | bytes 61472 | tf_op jit(solution)/shard_map/ppermute | solution.py:600
  94.6 5.9 %collective-permute-start.24 = (f32[160,384]{1,0:T(8,128)S(1)}, f32[160,384]{1,0:T(8,128)S(1)}, u32[]{:S(2)}, u32[]{:S(2)}) collective-permute-start(f32[160,384]{1,0:T(8,128)S(1)} %pad_maximum_fusion.mine_ref), channel_id=1, source_target_pairs={{0,16},{16,0},{32,48},{48,32},{64,80},{80,64},{96,112},{112,96},{1... | collective-permute-start | bytes 737288 | tf_op jit(solution)/shard_map/ppermute | solution.py:600
  101.6 1.3 %finish.1 = (bf16[64,384]{1,0:T(8,128)(2,1)}, f32[3,64]{1,0:T(4,128)}, bf16[256,384]{1,0:T(8,128)(2,1)}, f32[3,256]{1,0:T(4,128)}) custom-call(s32[3]{0:T(128)S(1)} %pad_add_fusion.place_ref, f32[72,384]{1,0:T(8,128)S(1)} %add.84.q0_ref, f32[72,384]{1,0:T(8,128)S(1)} %collective-permute-done.23.q1_ref, f32[160,384]{1,0:T(8,128)S(1)} %pad_maximum_fusion.mine_ref, ...), custom_call_target="tpu_custom_call" | custom-call | tf_op jit(solution)/shard_map/finish/pallas_call | solution.py:27
  (83 shorter events, 13.6 us)
Async XLA Ops:
  0.6 25.2 %copy-start = (bf16[64,256,128]{2,1,0:T(8,128)(2,1)S(1)}, bf16[64,256,128]{2,1,0:T(8,128)(2,1)}, u32[]{:S(2)}) copy-start(bf16[64,256,128]{2,1,0:T(8,128)(2,1)} %pair_ref.1) | copy-start | bytes 12582916
  0.6 25.2 %copy-start.9 = (bf16[256,384]{1,0:T(8,128)(2,1)S(1)}, bf16[256,384]{1,0:T(8,128)(2,1)}, u32[]{:S(2)}) copy-start(bf16[256,384]{1,0:T(8,128)(2,1)} %sk_ref.3) | copy-start | bytes 589828
  0.7 25.2 %copy-start.15 = (bf16[384,192]{0,1:T(8,128)(2,1)S(1)}, bf16[384,192]{0,1:T(8,128)(2,1)}, u32[]{:S(2)}) copy-start(bf16[384,192]{0,1:T(8,128)(2,1)} %param.26) | copy-start | bytes 442372
  0.7 25.1 %copy-start.11 = (bf16[384,288]{0,1:T(8,128)(2,1)S(1)}, bf16[384,288]{0,1:T(8,128)(2,1)}, u32[]{:S(2)}) copy-start(bf16[384,288]{0,1:T(8,128)(2,1)} %param.29) | copy-start | bytes 663556
  0.7 25.1 %copy-start.17 = (bf16[64,384]{1,0:T(8,128)(2,1)S(1)}, bf16[64,384]{1,0:T(8,128)(2,1)}, u32[]{:S(2)}) copy-start(bf16[64,384]{1,0:T(8,128)(2,1)} %cot_ref.1) | copy-start | bytes 147460
  8.8 22.7 %copy-start.19 = (s32[256]{0:T(256)S(1)}, s32[256]{0:T(256)}, u32[]{:S(2)}) copy-start(s32[256]{0:T(256)} %param.40) | copy-start | bytes 3076
  8.8 3.8 %collective-permute-start = (f32[32,64]{1,0:T(8,128)}, f32[32,64]{1,0:T(8,128)S(1)}, u32[]{:S(2)}, u32[]{:S(2)}) collective-permute-start(f32[32,64]{1,0:T(8,128)} %get-tuple-element.37), channel_id=1, source_target_pairs={{0,1},{1,0},{2,3},{3,2},{4,5},{5,4},{6,7},{7,6},{8,9},{9,8},{10,11... | collective-permute-start | bytes 24584 | tf_op jit(solution)/shard_map/ppermute | solution.py:600
  10.9 3.0 %collective-permute-start.1 = (f32[32,64]{1,0:T(8,128)}, f32[32,64]{1,0:T(8,128)S(1)}, u32[]{:S(2)}, u32[]{:S(2)}) collective-permute-start(f32[32,64]{1,0:T(8,128)} %get-tuple-element.37), channel_id=1, source_target_pairs={{0,2},{1,3},{2,0},{3,1},{4,6},{5,7},{6,4},{7,5},{8,10},{9,11},{10,... | collective-permute-start | bytes 24584 | tf_op jit(solution)/shard_map/ppermute | solution.py:600
  12.6 3.7 %collective-permute-start.2 = (f32[32,64]{1,0:T(8,128)}, f32[32,64]{1,0:T(8,128)S(1)}, u32[]{:S(2)}, u32[]{:S(2)}) collective-permute-start(f32[32,64]{1,0:T(8,128)} %get-tuple-element.37), channel_id=1, source_target_pairs={{0,3},{1,2},{2,1},{3,0},{4,7},{5,6},{6,5},{7,4},{8,11},{9,10},{10,... | collective-permute-start | bytes 24584 | tf_op jit(solution)/shard_map/ppermute | solution.py:600
  17.0 14.4 %collective-permute-start.3 = (f32[32,64]{1,0:T(8,128)S(1)}, f32[32,64]{1,0:T(8,128)S(1)}, u32[]{:S(2)}, u32[]{:S(2)}) collective-permute-start(f32[32,64]{1,0:T(8,128)S(1)} %pad_maximum_fusion.1), channel_id=1, source_target_pairs={{10,0},{11,1},{8,2},{9,3},{14,4},{15,5},{12,6},{13,7},{2,8},{3,9},... | collective-permute-start | bytes 24584 | tf_op jit(solution)/shard_map/ppermute | solution.py:611
  22.7 8.8 %collective-permute-start.4 = (f32[32,64]{1,0:T(8,128)S(1)}, f32[32,64]{1,0:T(8,128)S(1)}, u32[]{:S(2)}, u32[]{:S(2)}) collective-permute-start(f32[32,64]{1,0:T(8,128)S(1)} %pad_maximum_fusion.1), channel_id=1, source_target_pairs={{4,0},{5,1},{14,2},{15,3},{8,4},{9,5},{2,6},{3,7},{12,8},{13,9},{6... | collective-permute-start | bytes 24584 | tf_op jit(solution)/shard_map/ppermute | solution.py:611
  22.7 8.8 %collective-permute-start.5 = (f32[32,64]{1,0:T(8,128)S(1)}, f32[32,64]{1,0:T(8,128)S(1)}, u32[]{:S(2)}, u32[]{:S(2)}) collective-permute-start(f32[32,64]{1,0:T(8,128)S(1)} %pad_maximum_fusion.1), channel_id=1, source_target_pairs={{14,0},{15,1},{4,2},{5,3},{2,4},{3,5},{8,6},{9,7},{6,8},{7,9},{12,... | collective-permute-start | bytes 24584 | tf_op jit(solution)/shard_map/ppermute | solution.py:611
  33.3 3.6 %collective-permute-start.6 = (f32[64,384]{1,0:T(8,128)S(1)}, f32[64,384]{1,0:T(8,128)}, u32[]{:S(2)}, u32[]{:S(2)}) collective-permute-start(f32[64,384]{1,0:T(8,128)S(1)} %attend.1), channel_id=1, source_target_pairs={{0,1},{1,0},{2,3},{3,2},{4,5},{5,4},{6,7},{7,6},{8,9},{9,8},{10,11... | collective-permute-start | bytes 294920 | tf_op jit(solution)/shard_map/ppermute | solution.py:600
  33.5 3.6 %collective-permute-start.7 = (f32[64,384]{1,0:T(8,128)S(1)}, f32[64,384]{1,0:T(8,128)}, u32[]{:S(2)}, u32[]{:S(2)}) collective-permute-start(f32[64,384]{1,0:T(8,128)S(1)} %attend.1), channel_id=1, source_target_pairs={{0,2},{1,3},{2,0},{3,1},{4,6},{5,7},{6,4},{7,5},{8,10},{9,11},{10,... | collective-permute-start | bytes 294920 | tf_op jit(solution)/shard_map/ppermute | solution.py:600
  33.5 5.5 %collective-permute-start.8 = (f32[64,384]{1,0:T(8,128)S(1)}, f32[64,384]{1,0:T(8,128)}, u32[]{:S(2)}, u32[]{:S(2)}) collective-permute-start(f32[64,384]{1,0:T(8,128)S(1)} %attend.1), channel_id=1, source_target_pairs={{0,3},{1,2},{2,1},{3,0},{4,7},{5,6},{6,5},{7,4},{8,11},{9,10},{10,... | collective-permute-start | bytes 294920 | tf_op jit(solution)/shard_map/ppermute | solution.py:600
  35.9 22.7 %copy-start.14 = (bf16[384,192]{0,1:T(8,128)(2,1)S(1)}, bf16[384,192]{0,1:T(8,128)(2,1)}, u32[]{:S(2)}) copy-start(bf16[384,192]{0,1:T(8,128)(2,1)} %param.25) | copy-start | bytes 442372
  40.1 5.1 %collective-permute-start.10 = (f32[64,384]{1,0:T(8,128)S(1)}, f32[64,384]{1,0:T(8,128)S(1)}, u32[]{:S(2)}, u32[]{:S(2)}) collective-permute-start(f32[64,384]{1,0:T(8,128)S(1)} %add_add_fusion.1), channel_id=1, source_target_pairs={{4,0},{5,1},{14,2},{15,3},{8,4},{9,5},{2,6},{3,7},{12,8},{13,9},{6... | collective-permute-start | bytes 294920 | tf_op jit(solution)/shard_map/ppermute | solution.py:611
  40.5 6.6 %collective-permute-start.11 = (f32[64,384]{1,0:T(8,128)S(1)}, f32[64,384]{1,0:T(8,128)S(1)}, u32[]{:S(2)}, u32[]{:S(2)}) collective-permute-start(f32[64,384]{1,0:T(8,128)S(1)} %add_add_fusion.1), channel_id=1, source_target_pairs={{10,0},{11,1},{8,2},{9,3},{14,4},{15,5},{12,6},{13,7},{2,8},{3,9},... | collective-permute-start | bytes 294920 | tf_op jit(solution)/shard_map/ppermute | solution.py:611
  42.4 6.8 %collective-permute-start.9 = (f32[64,384]{1,0:T(8,128)S(1)}, f32[64,384]{1,0:T(8,128)S(1)}, u32[]{:S(2)}, u32[]{:S(2)}) collective-permute-start(f32[64,384]{1,0:T(8,128)S(1)} %add_add_fusion.1), channel_id=1, source_target_pairs={{14,0},{15,1},{4,2},{5,3},{2,4},{3,5},{8,6},{9,7},{6,8},{7,9},{12,... | collective-permute-start | bytes 294920 | tf_op jit(solution)/shard_map/ppermute | solution.py:611
  57.8 5.1 %collective-permute-start.12 = (f32[72,384]{1,0:T(8,128)S(1)}, f32[72,384]{1,0:T(8,128)S(1)}, u32[]{:S(2)}, u32[]{:S(2)}) collective-permute-start(f32[72,384]{1,0:T(8,128)S(1)} %get-tuple-element.41), channel_id=1, source_target_pairs={{0,1},{1,0},{2,3},{3,2},{4,5},{5,4},{6,7},{7,6},{8,9},{9,8},{10,11... | collective-permute-start | bytes 331784 | tf_op jit(solution)/shard_map/ppermute | solution.py:600
  62.9 7.0 %collective-permute-start.13 = (f32[160,384]{1,0:T(8,128)S(1)}, f32[160,384]{1,0:T(8,128)S(1)}, u32[]{:S(2)}, u32[]{:S(2)}) collective-permute-start(f32[160,384]{1,0:T(8,128)S(1)} %get-tuple-element.49), channel_id=1, source_target_pairs={{0,16},{16,0},{32,48},{48,32},{64,80},{80,64},{96,112},{112,96},{1... | collective-permute-start | bytes 737288 | tf_op jit(solution)/shard_map/ppermute | solution.py:600
  70.0 8.0 %collective-permute-start.14 = (f32[40,384]{1,0:T(8,128)S(1)}, f32[40,384]{1,0:T(8,128)S(1)}, u32[]{:S(2)}, u32[]{:S(2)}) collective-permute-start(f32[40,384]{1,0:T(8,128)S(1)} %get-tuple-element.73), channel_id=1, source_target_pairs={{0,64},{16,80},{32,96},{48,112},{64,0},{80,16},{96,32},{112,48},{1... | collective-permute-start | bytes 184328 | tf_op jit(solution)/shard_map/ppermute | solution.py:600
  71.4 6.6 %collective-permute-start.15 = (f32[40,384]{1,0:T(8,128)S(1)}, f32[40,384]{1,0:T(8,128)S(1)}, u32[]{:S(2)}, u32[]{:S(2)}) collective-permute-start(f32[40,384]{1,0:T(8,128)S(1)} %get-tuple-element.71), channel_id=1, source_target_pairs={{0,128},{16,144},{32,160},{48,176},{64,192},{80,208},{96,224},{112... | collective-permute-start | bytes 184328 | tf_op jit(solution)/shard_map/ppermute | solution.py:600
  74.0 4.3 %collective-permute-start.16 = (f32[40,384]{1,0:T(8,128)S(1)}, f32[40,384]{1,0:T(8,128)S(1)}, u32[]{:S(2)}, u32[]{:S(2)}) collective-permute-start(f32[40,384]{1,0:T(8,128)S(1)} %get-tuple-element.72), channel_id=1, source_target_pairs={{0,192},{16,208},{32,224},{48,240},{64,128},{80,144},{96,160},{112... | collective-permute-start | bytes 184328 | tf_op jit(solution)/shard_map/ppermute | solution.py:600
  74.0 4.3 %collective-permute-start.17 = (f32[72,384]{1,0:T(8,128)S(1)}, f32[72,384]{1,0:T(8,128)S(1)}, u32[]{:S(2)}, u32[]{:S(2)}) collective-permute-start(f32[72,384]{1,0:T(8,128)S(1)} %add.82), channel_id=1, source_target_pairs={{0,2},{1,3},{2,0},{3,1},{4,6},{5,7},{6,4},{7,5},{8,10},{9,11},{10,... | collective-permute-start | bytes 331784 | tf_op jit(solution)/shard_map/ppermute | solution.py:600
  78.3 7.4 %collective-permute-start.19 = (f32[72,384]{1,0:T(8,128)S(1)}, f32[72,384]{1,0:T(8,128)S(1)}, u32[]{:S(2)}, u32[]{:S(2)}) collective-permute-start(f32[72,384]{1,0:T(8,128)S(1)} %add.83), channel_id=1, source_target_pairs={{10,0},{11,1},{8,2},{9,3},{14,4},{15,5},{12,6},{13,7},{2,8},{3,9},... | collective-permute-start | bytes 331784 | tf_op jit(solution)/shard_map/ppermute | solution.py:611
  81.2 4.6 %collective-permute-start.18 = (f32[40,384]{1,0:T(8,128)S(1)}, f32[40,384]{1,0:T(8,128)S(1)}, u32[]{:S(2)}, u32[]{:S(2)}) collective-permute-start(f32[40,384]{1,0:T(8,128)S(1)} %add_add_fusion.2), channel_id=1, source_target_pairs={{0,32},{16,48},{32,0},{48,16},{64,96},{80,112},{96,64},{112,80},{1... | collective-permute-start | bytes 184328 | tf_op jit(solution)/shard_map/ppermute | solution.py:600
  85.8 6.1 %collective-permute-start.20 = (f32[40,384]{1,0:T(8,128)S(1)}, f32[40,384]{1,0:T(8,128)S(1)}, u32[]{:S(2)}, u32[]{:S(2)}) collective-permute-start(f32[40,384]{1,0:T(8,128)S(1)} %add.85), channel_id=1, source_target_pairs={{0,64},{16,80},{32,96},{48,112},{64,0},{80,16},{96,32},{112,48},{1... | collective-permute-start | bytes 184328 | tf_op jit(solution)/shard_map/ppermute | solution.py:600
  85.9 6.0 %collective-permute-start.21 = (f32[40,384]{1,0:T(8,128)S(1)}, f32[40,384]{1,0:T(8,128)S(1)}, u32[]{:S(2)}, u32[]{:S(2)}) collective-permute-start(f32[40,384]{1,0:T(8,128)S(1)} %add.85), channel_id=1, source_target_pairs={{0,128},{16,144},{32,160},{48,176},{64,192},{80,208},{96,224},{112... | collective-permute-start | bytes 184328 | tf_op jit(solution)/shard_map/ppermute | solution.py:600
  89.4 4.3 %collective-permute-start.22 = (f32[40,384]{1,0:T(8,128)S(1)}, f32[40,384]{1,0:T(8,128)S(1)}, u32[]{:S(2)}, u32[]{:S(2)}) collective-permute-start(f32[40,384]{1,0:T(8,128)S(1)} %add.85), channel_id=1, source_target_pairs={{0,192},{16,208},{32,224},{48,240},{64,128},{80,144},{96,160},{112... | collective-permute-start | bytes 184328 | tf_op jit(solution)/shard_map/ppermute | solution.py:600
  89.7 4.9 %collective-permute-start.23 = (f32[72,384]{1,0:T(8,128)S(1)}, f32[72,384]{1,0:T(8,128)S(1)}, u32[]{:S(2)}, u32[]{:S(2)}) collective-permute-start(f32[72,384]{1,0:T(8,128)S(1)} %add.84.q0_ref), channel_id=1, source_target_pairs={{14,0},{15,1},{4,2},{5,3},{2,4},{3,5},{8,6},{9,7},{6,8},{7,9},{12,... | collective-permute-start | bytes 331784 | tf_op jit(solution)/shard_map/ppermute | solution.py:611
  94.6 7.0 %collective-permute-start.24 = (f32[160,384]{1,0:T(8,128)S(1)}, f32[160,384]{1,0:T(8,128)S(1)}, u32[]{:S(2)}, u32[]{:S(2)}) collective-permute-start(f32[160,384]{1,0:T(8,128)S(1)} %pad_maximum_fusion.mine_ref), channel_id=1, source_target_pairs={{0,16},{16,0},{32,48},{48,32},{64,80},{80,64},{96,112},{112,96},{1... | collective-permute-start | bytes 737288 | tf_op jit(solution)/shard_map/ppermute | solution.py:600
  (14 other events, 105.1 us)

commit v7 on v5

--- a/solution.py
+++ b/solution.py
@@ -102,6 +102,8 @@
 
 def pad_lanes(x, width=LANE):
     n, w = x.shape
+    if w == width:
+        return x
     return jnp.concatenate([x, jnp.zeros((n, width - w), x.dtype)], axis=1)
 
 
@@ -265,7 +267,7 @@
     heads,
     channels,
     npoint,
-    pair_hbm,
+    pair_ref,
     pack_ref,
     sk_ref,
     cot_ref,
@@ -275,13 +277,10 @@
     base_ref,
     vals_ref,
     doz_ref,
-    pair_ref,
     lhs_ref,
-    sems,
 ):
-    rows, keys, depth = pair_hbm.shape
+    rows, keys, depth = pair_ref.shape
     hp = heads * npoint
-    copies, step = load_pair(pair_hbm, pair_ref, sems)
     sk = sk_ref[...]
     cot = cot_ref[...]
     value = nt(sk, wv_ref[...]).astype(BF)
@@ -302,15 +301,32 @@
     doz_ref[...] = lhs_ref[...].astype(BF)
     dosm = spread(dos.astype(F32), channel_mask(heads, channels)).astype(BF)
     base_ref[...] = nt(dosm, value)
-    for c, copy in enumerate(copies):
-        copy.wait()
-
-        def one(i, carry):
-            r = pl.multiple_of(i * HP, HP)
-            base_ref[pl.ds(r, HP), :] += nt(doz_ref[pl.ds(r, HP), :], pair_ref[i])
-            return carry
-
-        lax.fori_loop(c * step, (c + 1) * step, one, 0, unroll=16)
+
+    def one(i, carry):
+        r = pl.multiple_of(i * HP, HP)
+        base_ref[pl.ds(r, HP), :] += nt(doz_ref[pl.ds(r, HP), :], pair_ref[i])
+        return carry
+
+    lax.fori_loop(0, rows, one, 0, unroll=16)
+
+
+def folded(x, used):
+    n, spare, half = x.shape[0], LANE - used, LANE // 2
+    third = x[:, 2 * LANE :]
+    second = jnp.concatenate([x[:, LANE : LANE + used], third[:, :spare]], axis=1)
+    rest = pad_lanes(third[:, spare:used], half)
+    quarter = n // 4
+    rest = jnp.concatenate([rest[q * quarter : (q + 1) * quarter] for q in range(4)], axis=1)
+    return jnp.concatenate([jnp.concatenate([x[:, :LANE], second], axis=1), rest], axis=0)
+
+
+def unfolded(y, used):
+    quarter = y.shape[0] // 5
+    n, spare, half = 4 * quarter, LANE - used, LANE // 2
+    rest = jnp.concatenate([y[n:, q * half : (q + 1) * half] for q in range(4)], axis=0)
+    second = y[:n, LANE:]
+    third = jnp.concatenate([second[:, used:], rest[:, : used - spare]], axis=1)
+    return jnp.concatenate([y[:n, :LANE], pad_lanes(second[:, :used]), pad_lanes(third)], axis=1)
 
 
 def attend_kernel(
@@ -339,8 +355,9 @@
     opt = nn(attn_b, ghi) + nn(attn_b, glo)
     pmask = head_mask(heads, npoint, 3 * LANE)
     delta = jnp.sum(attn_f * base_ref[...], axis=1, keepdims=True)
-    out_ref[...] = gather_heads(opt, pmask)
-    out_ref[:, 0:LANE] += to_lanes(delta, heads * npoint)
+    points = gather_heads(opt, pmask)
+    stat = pad_lanes(to_lanes(delta, heads * npoint), 3 * LANE)
+    out_ref[...] = folded(points + stat, heads * npoint)
 
 
 def frames_of(heads, npoint, qall, rows):
@@ -384,7 +401,7 @@
     alo_ref,
     dglob_ref,
 ):
-    rows, keys = psum_ref.shape[0], base_ref.shape[1]
+    rows, keys = dglob_ref.shape[0], base_ref.shape[1]
     place = packing(rows, keys, heads * channels)
     vplace = value_packing(rows, keys, heads * channels)
     hp = heads * npoint
@@ -393,7 +410,7 @@
     pmask, qcols, coef_lane = frames_of(heads, npoint, pack_ref[place.qcol], rows)
     inside = iota((1, LANE), 1) < hp
 
-    psum = psum_ref[...]
+    psum = unfolded(psum_ref[...], hp)
     delta0 = to_col(psum[:, :LANE], hp)
     opt = [jnp.where(inside, psum[:, a * LANE : (a + 1) * LANE], 0.0) for a in range(3)]
     moved = [jnp.where(inside, opt[a] - qcols[:, 9 + a : 10 + a], 0.0) for a in range(3)]
@@ -699,13 +716,9 @@
             sds((n, depth), BF),
         ],
         [],
-        [pair],
-        [pack, single_k, cotangent, w_value, w_vpoint, w_out],
-        [
-            pltpu.VMEM((rows, keys, depth), BF),
-            pltpu.VMEM((n, depth), F32),
-            pltpu.SemaphoreType.DMA((1,)),
-        ],
+        [],
+        [pair, pack, single_k, cotangent, w_value, w_vpoint, w_out],
+        [pltpu.VMEM((n, depth), F32)],
         pl.CostEstimate(
             flops=8 * n * keys * wide, bytes_accessed=4 * rows * keys * depth, transcendentals=0
         ),
@@ -716,7 +729,7 @@
     attn, points = call(
         functools.partial(attend_kernel, heads, npoint),
         "attend",
-        [sds((n, keys), F32), sds((rows, wide), F32)],
+        [sds((n, keys), F32), sds((rows + rows // 4, 2 * LANE), F32)],
         [],
         [],
         [masked, base, vals, km, stats],

time: 103 us -> 102 us (level)
  waiting for transfers between devices: 18.6 us -> 17.3 us
  transfers between devices with their start and end apart: 25 -> 25, of which waited for: 14 -> 13; matrix products, arithmetic and copies ran while one was open for 0% -> 0% of each run, Pallas kernels for 11% -> 11%
where the time goes in v7:
time: 102 us
  starting transfers between devices  49 us (48%)
  Pallas kernels  27.4 us (27%)
  waiting for transfers between devices  17.3 us (17%)
  local copies, waits for them, and re-layouts  4.96 us (5%)
  other arithmetic  2.02 us (2%)
    ppermute x17, starting transfers between devices, permuted(): return lax.ppermute(x, axis, [(i, i ^ flip) for i in range(size)])  30.6 us
    pallas_call x6, Pallas kernels, call(): pl.pallas_call(kernel, out_shape=outs, in_specs=[SMEM] * len(smem) + [ANY...  23.2 us
    ppermute x8, starting transfers between devices, around(): return lax.ppermute(x, 'col', moves)  18.4 us
    ppermute x17, waiting for transfers between devices, permuted(): return lax.ppermute(x, axis, [(i, i ^ flip) for i in range(size)])  11.4 us
    ppermute x8, waiting for transfers between devices, around(): return lax.ppermute(x, 'col', moves)  5.87 us
    unnamed x38, local copies, waits for them, and re-layouts  4.94 us
    pallas_call x2, Pallas kernels, pair_part(): pl.pallas_call(pair_kernel, grid=(1,), out_shape=jax.ShapeDtypeStruct((ro...  4.16 us
  transfers between devices with their start and end apart: 25, of which 13 were waited for; matrix products, arithmetic and copies ran while one was open for 0% of the time, Pallas kernels for 11%

profile of v7, /device:TPU:1, one launch (start us, length us, event | category | flops | bytes accessed | tf_op | source)
XLA Modules:
  0.0 101.6 jit_solution(40287582699192546)
XLA Ops:
  0.7 8.1 %logits.1 = (f32[1024,256]{1,0:T(8,128)}, f32[32,64]{1,0:T(8,128)}, f32[704,384]{1,0:T(8,128)}) custom-call(bf16[64,256,128]{2,1,0:T(8,128)(2,1)} %pair_ref.1, bf16[64,384]{1,0:T(8,128)(2,1)} %sq_ref.1, bf16[256,384]{1,0:T(8,128)(2,1)} %sk_ref.3, bf16[192,384]{1,0:T(8,128)(2,1)} %bitcast.17, bf16[192,384]{1,0:T(8,128)(2,1)} %bitcast.23, ...), custom_call_target="tpu_custom_call" | custom-call | tf_op jit(solution)/shard_map/logits/pallas_call | solution.py:27
  8.8 2.1 %collective-permute-start = (f32[32,64]{1,0:T(8,128)}, f32[32,64]{1,0:T(8,128)S(1)}, u32[]{:S(2)}, u32[]{:S(2)}) collective-permute-start(f32[32,64]{1,0:T(8,128)} %get-tuple-element.42), channel_id=1, source_target_pairs={{0,1},{1,0},{2,3},{3,2},{4,5},{5,4},{6,7},{7,6},{8,9},{9,8},{10,11... | collective-permute-start | bytes 24584 | tf_op jit(solution)/shard_map/ppermute | solution.py:629
  10.9 1.6 %collective-permute-start.1 = (f32[32,64]{1,0:T(8,128)}, f32[32,64]{1,0:T(8,128)S(1)}, u32[]{:S(2)}, u32[]{:S(2)}) collective-permute-start(f32[32,64]{1,0:T(8,128)} %get-tuple-element.42), channel_id=1, source_target_pairs={{0,2},{1,3},{2,0},{3,1},{4,6},{5,7},{6,4},{7,5},{8,10},{9,11},{10,... | collective-permute-start | bytes 24584 | tf_op jit(solution)/shard_map/ppermute | solution.py:629
  12.6 1.4 %collective-permute-done.1 = f32[32,64]{1,0:T(8,128)S(1)} collective-permute-done((f32[32,64]{1,0:T(8,128)}, f32[32,64]{1,0:T(8,128)S(1)}, u32[]{:S(2)}, u32[]{:S(2)}) %collective-permute-start.1) | collective-permute-done | bytes 8224 | tf_op jit(solution)/shard_map/ppermute | solution.py:629
  13.9 2.3 %collective-permute-done.2 = f32[32,64]{1,0:T(8,128)S(1)} collective-permute-done((f32[32,64]{1,0:T(8,128)}, f32[32,64]{1,0:T(8,128)S(1)}, u32[]{:S(2)}, u32[]{:S(2)}) %collective-permute-start.2) | collective-permute-done | bytes 8224 | tf_op jit(solution)/shard_map/ppermute | solution.py:629
  17.0 5.6 %collective-permute-start.3 = (f32[32,64]{1,0:T(8,128)S(1)}, f32[32,64]{1,0:T(8,128)S(1)}, u32[]{:S(2)}, u32[]{:S(2)}) collective-permute-start(f32[32,64]{1,0:T(8,128)S(1)} %pad_maximum_fusion.1), channel_id=1, source_target_pairs={{10,0},{11,1},{8,2},{9,3},{14,4},{15,5},{12,6},{13,7},{2,8},{3,9},... | collective-permute-start | bytes 24584 | tf_op jit(solution)/shard_map/ppermute | solution.py:640
  22.7 3.1 %collective-permute-start.5 = (f32[32,64]{1,0:T(8,128)S(1)}, f32[32,64]{1,0:T(8,128)S(1)}, u32[]{:S(2)}, u32[]{:S(2)}) collective-permute-start(f32[32,64]{1,0:T(8,128)S(1)} %pad_maximum_fusion.1), channel_id=1, source_target_pairs={{14,0},{15,1},{4,2},{5,3},{2,4},{3,5},{8,6},{9,7},{6,8},{7,9},{12,... | collective-permute-start | bytes 24584 | tf_op jit(solution)/shard_map/ppermute | solution.py:640
  27.1 1.4 %copy-done.3 = bf16[2112,384]{1,0:T(8,128)(2,1)S(1)} copy-done((bf16[2112,384]{1,0:T(8,128)(2,1)S(1)}, bf16[2112,384]{1,0:T(8,128)(2,1)}, u32[]{:S(2)}) %copy-start.3) | copy-done | bytes 1622040
  28.5 3.0 %base.1 = (f32[1024,256]{1,0:T(8,128)S(1)}, f32[384,384]{1,0:T(8,128)S(1)}, bf16[1024,128]{1,0:T(8,128)(2,1)S(1)}) custom-call(bf16[64,256,128]{2,1,0:T(8,128)(2,1)S(1)} %copy-done, f32[704,384]{1,0:T(8,128)S(1)} %copy-done.1, bf16[256,384]{1,0:T(8,128)(2,1)S(1)} %copy-done.8, bf16[64,384]{1,0:T(8,128)(2,1)S(1)} %copy-done.16, ...), custom_call_target="tpu_custom_call" | custom-call | flops 805306368 | bytes 8388608 | tf_op jit(solution)/shard_map/base/pallas_call | solution.py:27
  31.6 1.6 %attend.1 = (f32[1024,256]{1,0:T(8,128)S(1)}, f32[80,256]{1,0:T(8,128)}) custom-call(f32[1024,256]{1,0:T(8,128)S(1)} %copy-done.6, f32[1024,256]{1,0:T(8,128)S(1)} %get-tuple-element.40.base_ref, f32[384,384]{1,0:T(8,128)S(1)} %get-tuple-element.41.vals_ref, s32[1,256]{1,0:T(1,128)S(1)} %bitcast.31, f32[32,64]{1,0:T(8,128)S(1)} %pad_maximum_fusion.2.stats_ref), custom_call_target="tpu_custom_call" | custom-call | tf_op jit(solution)/shard_map/attend/pallas_call | solution.py:27
  34.5 2.4 %collective-permute-start.8 = (f32[80,256]{1,0:T(8,128)}, f32[80,256]{1,0:T(8,128)}, u32[]{:S(2)}, u32[]{:S(2)}) collective-permute-start(f32[80,256]{1,0:T(8,128)} %get-tuple-element.44), channel_id=1, source_target_pairs={{0,3},{1,2},{2,1},{3,0},{4,7},{5,6},{6,5},{7,4},{8,11},{9,10},{10,... | collective-permute-start | bytes 245768 | tf_op jit(solution)/shard_map/ppermute | solution.py:629
  38.1 1.8 %collective-permute-done.8 = f32[80,256]{1,0:T(8,128)} collective-permute-done((f32[80,256]{1,0:T(8,128)}, f32[80,256]{1,0:T(8,128)}, u32[]{:S(2)}, u32[]{:S(2)}) %collective-permute-start.8) | collective-permute-done | bytes 81952 | tf_op jit(solution)/shard_map/ppermute | solution.py:629
  41.5 1.7 %collective-permute-start.11 = (f32[80,256]{1,0:T(8,128)S(1)}, f32[80,256]{1,0:T(8,128)S(1)}, u32[]{:S(2)}, u32[]{:S(2)}) collective-permute-start(f32[80,256]{1,0:T(8,128)S(1)} %add_add_fusion.1), channel_id=1, source_target_pairs={{10,0},{11,1},{8,2},{9,3},{14,4},{15,5},{12,6},{13,7},{2,8},{3,9},... | collective-permute-start | bytes 245768 | tf_op jit(solution)/shard_map/ppermute | solution.py:640
  43.3 2.7 %collective-permute-start.9 = (f32[80,256]{1,0:T(8,128)S(1)}, f32[80,256]{1,0:T(8,128)S(1)}, u32[]{:S(2)}, u32[]{:S(2)}) collective-permute-start(f32[80,256]{1,0:T(8,128)S(1)} %add_add_fusion.1), channel_id=1, source_target_pairs={{14,0},{15,1},{4,2},{5,3},{2,4},{3,5},{8,6},{9,7},{6,8},{7,9},{12,... | collective-permute-start | bytes 245768 | tf_op jit(solution)/shard_map/ppermute | solution.py:640
  46.0 1.9 %collective-permute-done.11 = f32[80,256]{1,0:T(8,128)S(1)} collective-permute-done((f32[80,256]{1,0:T(8,128)S(1)}, f32[80,256]{1,0:T(8,128)S(1)}, u32[]{:S(2)}, u32[]{:S(2)}) %collective-permute-start.11) | collective-permute-done | bytes 81952 | tf_op jit(solution)/shard_map/ppermute | solution.py:640
  47.9 1.6 %collective-permute-done.9 = f32[80,256]{1,0:T(8,128)S(1)} collective-permute-done((f32[80,256]{1,0:T(8,128)S(1)}, f32[80,256]{1,0:T(8,128)S(1)}, u32[]{:S(2)}, u32[]{:S(2)}) %collective-permute-start.9) | collective-permute-done | bytes 81952 | tf_op jit(solution)/shard_map/ppermute | solution.py:640
  50.8 4.9 %query_grads.1 = (f32[72,384]{1,0:T(8,128)S(1)}, bf16[64,32,256]{2,1,0:T(8,128)(2,1)S(1)}, bf16[1024,256]{1,0:T(8,128)(2,1)S(1)}, bf16[1024,256]{1,0:T(8,128)(2,1)S(1)}, f32[64,384]{1,0:T(8,128)S(1)}) custom-call(s32[3]{0:T(128)S(1)} %pad_add_fusion.place_ref, f32[1024,256]{1,0:T(8,128)S(1)} %copy-done.5, f32[1024,256]{1,0:T(8,128)S(1)} %get-tuple-element.40.base_ref, ...), custom_call_target="tpu_custom_call" | custom-call | tf_op jit(solution)/shard_map/query_grads/pallas_call | solution.py:27
  56.9 4.3 %key_grads.1 = (f32[160,384]{1,0:T(8,128)S(1)}, f32[160,384]{1,0:T(8,128)S(1)}) custom-call(s32[3]{0:T(128)S(1)} %pad_add_fusion.place_ref, bf16[64,32,256]{2,1,0:T(8,128)(2,1)S(1)} %get-tuple-element.60.both_ref, bf16[1024,256]{1,0:T(8,128)(2,1)S(1)} %get-tuple-element.47.dlo_ref, bf16[1024,256]{1,0:T(8,128)(2,1)S(1)} %get-tuple-element.48.alo_ref, ...), custom_call_target="tpu_custom_call" | custom-call | flops 2415919104 | bytes 1048576 | tf_op jit(solution)/shard_map/key_grads/pallas_call | solution.py:27
  61.2 5.7 %collective-permute-start.13 = (f32[160,384]{1,0:T(8,128)S(1)}, f32[160,384]{1,0:T(8,128)S(1)}, u32[]{:S(2)}, u32[]{:S(2)}) collective-permute-start(f32[160,384]{1,0:T(8,128)S(1)} %get-tuple-element.53), channel_id=1, source_target_pairs={{0,16},{16,0},{32,48},{48,32},{64,80},{80,64},{96,112},{112,96},{1... | collective-permute-start | bytes 737288 | tf_op jit(solution)/shard_map/ppermute | solution.py:629
  68.0 1.4 %collective-permute-start.14 = (f32[40,384]{1,0:T(8,128)S(1)}, f32[40,384]{1,0:T(8,128)S(1)}, u32[]{:S(2)}, u32[]{:S(2)}) collective-permute-start(f32[40,384]{1,0:T(8,128)S(1)} %get-tuple-element.77), channel_id=1, source_target_pairs={{0,64},{16,80},{32,96},{48,112},{64,0},{80,16},{96,32},{112,48},{1... | collective-permute-start | bytes 184328 | tf_op jit(solution)/shard_map/ppermute | solution.py:629
  69.4 2.6 %collective-permute-start.15 = (f32[40,384]{1,0:T(8,128)S(1)}, f32[40,384]{1,0:T(8,128)S(1)}, u32[]{:S(2)}, u32[]{:S(2)}) collective-permute-start(f32[40,384]{1,0:T(8,128)S(1)} %get-tuple-element.75), channel_id=1, source_target_pairs={{0,128},{16,144},{32,160},{48,176},{64,192},{80,208},{96,224},{112... | collective-permute-start | bytes 184328 | tf_op jit(solution)/shard_map/ppermute | solution.py:629
  72.1 1.9 %collective-permute-start.17 = (f32[72,384]{1,0:T(8,128)S(1)}, f32[72,384]{1,0:T(8,128)S(1)}, u32[]{:S(2)}, u32[]{:S(2)}) collective-permute-start(f32[72,384]{1,0:T(8,128)S(1)} %add.82), channel_id=1, source_target_pairs={{0,2},{1,3},{2,0},{3,1},{4,6},{5,7},{6,4},{7,5},{8,10},{9,11},{10,... | collective-permute-start | bytes 331784 | tf_op jit(solution)/shard_map/ppermute | solution.py:629
  74.0 2.1 %pair_grad.2.refs_0_ = bf16[64,256,128]{2,1,0:T(8,128)(2,1)} custom-call(bf16[64,32,256]{2,1,0:T(8,128)(2,1)S(1)} %get-tuple-element.60.both_ref, bf16[1024,128]{1,0:T(8,128)(2,1)S(1)} %get-tuple-element.56.doz_ref, bf16[12,128]{1,0:T(8,128)(2,1)S(1)} %bitcast.28), custom_call_target="tpu_custom_call" | custom-call | flops 100663296 | bytes 2097152 | tf_op jit(solution)/shard_map/pair_grad/pallas_call | solution.py:610
  76.4 2.9 %collective-permute-start.19 = (f32[72,384]{1,0:T(8,128)S(1)}, f32[72,384]{1,0:T(8,128)S(1)}, u32[]{:S(2)}, u32[]{:S(2)}) collective-permute-start(f32[72,384]{1,0:T(8,128)S(1)} %add.83), channel_id=1, source_target_pairs={{14,0},{15,1},{4,2},{5,3},{2,4},{3,5},{8,6},{9,7},{6,8},{7,9},{12,... | collective-permute-start | bytes 331784 | tf_op jit(solution)/shard_map/ppermute | solution.py:640
  79.3 2.6 %collective-permute-start.18 = (f32[40,384]{1,0:T(8,128)S(1)}, f32[40,384]{1,0:T(8,128)S(1)}, u32[]{:S(2)}, u32[]{:S(2)}) collective-permute-start(f32[40,384]{1,0:T(8,128)S(1)} %add_add_fusion.2), channel_id=1, source_target_pairs={{0,32},{16,48},{32,0},{48,16},{64,96},{80,112},{96,64},{112,80},{1... | collective-permute-start | bytes 184328 | tf_op jit(solution)/shard_map/ppermute | solution.py:629
  81.8 2.1 %pair_grad.3 = bf16[64,256,128]{2,1,0:T(8,128)(2,1)} custom-call(bf16[64,32,256]{2,1,0:T(8,128)(2,1)S(1)} %get-tuple-element.60.both_ref, bf16[1024,128]{1,0:T(8,128)(2,1)S(1)} %get-tuple-element.56.doz_ref, bf16[12,128]{1,0:T(8,128)(2,1)S(1)} %bitcast.29, bf16[64,256,128]{2,1,0:T(8,128)(2,1)} %pair_grad.2.refs_0_), custom_call_target="tpu_custom_call", output_to_operand_aliasing={{}: (3, {})} | custom-call | flops 100663296 | bytes 2097152 | tf_op jit(solution)/shard_map/pair_grad/pallas_call | solution.py:610
  84.0 3.4 %collective-permute-start.21 = (f32[40,384]{1,0:T(8,128)S(1)}, f32[40,384]{1,0:T(8,128)S(1)}, u32[]{:S(2)}, u32[]{:S(2)}) collective-permute-start(f32[40,384]{1,0:T(8,128)S(1)} %add.85), channel_id=1, source_target_pairs={{0,128},{16,144},{32,160},{48,176},{64,192},{80,208},{96,224},{112... | collective-permute-start | bytes 184328 | tf_op jit(solution)/shard_map/ppermute | solution.py:629
  87.9 1.7 %collective-permute-start.23 = (f32[72,384]{1,0:T(8,128)S(1)}, f32[72,384]{1,0:T(8,128)S(1)}, u32[]{:S(2)}, u32[]{:S(2)}) collective-permute-start(f32[72,384]{1,0:T(8,128)S(1)} %add.84.q0_ref), channel_id=1, source_target_pairs={{6,0},{7,1},{12,2},{13,3},{10,4},{11,5},{0,6},{1,7},{14,8},{15,9},... | collective-permute-start | bytes 331784 | tf_op jit(solution)/shard_map/ppermute | solution.py:640
  89.8 2.0 %collective-permute-done.22 = f32[40,384]{1,0:T(8,128)S(1)} collective-permute-done((f32[40,384]{1,0:T(8,128)S(1)}, f32[40,384]{1,0:T(8,128)S(1)}, u32[]{:S(2)}, u32[]{:S(2)}) %collective-permute-start.22) | collective-permute-done | bytes 61472 | tf_op jit(solution)/shard_map/ppermute | solution.py:629
  91.8 2.3 %collective-permute-done.23.q1_ref = f32[72,384]{1,0:T(8,128)S(1)} collective-permute-done((f32[72,384]{1,0:T(8,128)S(1)}, f32[72,384]{1,0:T(8,128)S(1)}, u32[]{:S(2)}, u32[]{:S(2)}) %collective-permute-start.23) | collective-permute-done | bytes 110624 | tf_op jit(solution)/shard_map/ppermute | solution.py:640
  94.2 4.9 %collective-permute-start.24 = (f32[160,384]{1,0:T(8,128)S(1)}, f32[160,384]{1,0:T(8,128)S(1)}, u32[]{:S(2)}, u32[]{:S(2)}) collective-permute-start(f32[160,384]{1,0:T(8,128)S(1)} %pad_maximum_fusion.mine_ref), channel_id=1, source_target_pairs={{0,16},{16,0},{32,48},{48,32},{64,80},{80,64},{96,112},{112,96},{1... | collective-permute-start | bytes 737288 | tf_op jit(solution)/shard_map/ppermute | solution.py:629
  100.2 1.3 %finish.1 = (bf16[64,384]{1,0:T(8,128)(2,1)}, f32[3,64]{1,0:T(4,128)}, bf16[256,384]{1,0:T(8,128)(2,1)}, f32[3,256]{1,0:T(4,128)}) custom-call(s32[3]{0:T(128)S(1)} %pad_add_fusion.place_ref, f32[72,384]{1,0:T(8,128)S(1)} %add.84.q0_ref, f32[72,384]{1,0:T(8,128)S(1)} %collective-permute-done.23.q1_ref, f32[160,384]{1,0:T(8,128)S(1)} %pad_maximum_fusion.mine_ref, ...), custom_call_target="tpu_custom_call" | custom-call | tf_op jit(solution)/shard_map/finish/pallas_call | solution.py:27
  (79 shorter events, 12.0 us)
Async XLA Ops:
  0.6 25.2 %copy-start = (bf16[64,256,128]{2,1,0:T(8,128)(2,1)S(1)}, bf16[64,256,128]{2,1,0:T(8,128)(2,1)}, u32[]{:S(2)}) copy-start(bf16[64,256,128]{2,1,0:T(8,128)(2,1)} %pair_ref.1) | copy-start | bytes 12582916
  0.6 25.2 %copy-start.8 = (bf16[256,384]{1,0:T(8,128)(2,1)S(1)}, bf16[256,384]{1,0:T(8,128)(2,1)}, u32[]{:S(2)}) copy-start(bf16[256,384]{1,0:T(8,128)(2,1)} %sk_ref.3) | copy-start | bytes 589828
  0.7 25.2 %copy-start.14 = (bf16[384,192]{0,1:T(8,128)(2,1)S(1)}, bf16[384,192]{0,1:T(8,128)(2,1)}, u32[]{:S(2)}) copy-start(bf16[384,192]{0,1:T(8,128)(2,1)} %param.26) | copy-start | bytes 442372
  0.7 25.1 %copy-start.10 = (bf16[384,288]{0,1:T(8,128)(2,1)S(1)}, bf16[384,288]{0,1:T(8,128)(2,1)}, u32[]{:S(2)}) copy-start(bf16[384,288]{0,1:T(8,128)(2,1)} %param.29) | copy-start | bytes 663556
  0.7 25.1 %copy-start.16 = (bf16[64,384]{1,0:T(8,128)(2,1)S(1)}, bf16[64,384]{1,0:T(8,128)(2,1)}, u32[]{:S(2)}) copy-start(bf16[64,384]{1,0:T(8,128)(2,1)} %cot_ref.1) | copy-start | bytes 147460
  8.8 22.8 %copy-start.18 = (s32[256]{0:T(256)S(1)}, s32[256]{0:T(256)}, u32[]{:S(2)}) copy-start(s32[256]{0:T(256)} %param.40) | copy-start | bytes 3076
  8.8 3.8 %collective-permute-start = (f32[32,64]{1,0:T(8,128)}, f32[32,64]{1,0:T(8,128)S(1)}, u32[]{:S(2)}, u32[]{:S(2)}) collective-permute-start(f32[32,64]{1,0:T(8,128)} %get-tuple-element.42), channel_id=1, source_target_pairs={{0,1},{1,0},{2,3},{3,2},{4,5},{5,4},{6,7},{7,6},{8,9},{9,8},{10,11... | collective-permute-start | bytes 24584 | tf_op jit(solution)/shard_map/ppermute | solution.py:629
  10.9 3.0 %collective-permute-start.1 = (f32[32,64]{1,0:T(8,128)}, f32[32,64]{1,0:T(8,128)S(1)}, u32[]{:S(2)}, u32[]{:S(2)}) collective-permute-start(f32[32,64]{1,0:T(8,128)} %get-tuple-element.42), channel_id=1, source_target_pairs={{0,2},{1,3},{2,0},{3,1},{4,6},{5,7},{6,4},{7,5},{8,10},{9,11},{10,... | collective-permute-start | bytes 24584 | tf_op jit(solution)/shard_map/ppermute | solution.py:629
  12.6 3.7 %collective-permute-start.2 = (f32[32,64]{1,0:T(8,128)}, f32[32,64]{1,0:T(8,128)S(1)}, u32[]{:S(2)}, u32[]{:S(2)}) collective-permute-start(f32[32,64]{1,0:T(8,128)} %get-tuple-element.42), channel_id=1, source_target_pairs={{0,3},{1,2},{2,1},{3,0},{4,7},{5,6},{6,5},{7,4},{8,11},{9,10},{10,... | collective-permute-start | bytes 24584 | tf_op jit(solution)/shard_map/ppermute | solution.py:629
  17.0 14.5 %collective-permute-start.3 = (f32[32,64]{1,0:T(8,128)S(1)}, f32[32,64]{1,0:T(8,128)S(1)}, u32[]{:S(2)}, u32[]{:S(2)}) collective-permute-start(f32[32,64]{1,0:T(8,128)S(1)} %pad_maximum_fusion.1), channel_id=1, source_target_pairs={{10,0},{11,1},{8,2},{9,3},{14,4},{15,5},{12,6},{13,7},{2,8},{3,9},... | collective-permute-start | bytes 24584 | tf_op jit(solution)/shard_map/ppermute | solution.py:640
  22.7 8.9 %collective-permute-start.4 = (f32[32,64]{1,0:T(8,128)S(1)}, f32[32,64]{1,0:T(8,128)S(1)}, u32[]{:S(2)}, u32[]{:S(2)}) collective-permute-start(f32[32,64]{1,0:T(8,128)S(1)} %pad_maximum_fusion.1), channel_id=1, source_target_pairs={{4,0},{5,1},{14,2},{15,3},{8,4},{9,5},{2,6},{3,7},{12,8},{13,9},{6... | collective-permute-start | bytes 24584 | tf_op jit(solution)/shard_map/ppermute | solution.py:640
  22.7 8.9 %collective-permute-start.5 = (f32[32,64]{1,0:T(8,128)S(1)}, f32[32,64]{1,0:T(8,128)S(1)}, u32[]{:S(2)}, u32[]{:S(2)}) collective-permute-start(f32[32,64]{1,0:T(8,128)S(1)} %pad_maximum_fusion.1), channel_id=1, source_target_pairs={{14,0},{15,1},{4,2},{5,3},{2,4},{3,5},{8,6},{9,7},{6,8},{7,9},{12,... | collective-permute-start | bytes 24584 | tf_op jit(solution)/shard_map/ppermute | solution.py:640
  31.5 25.4 %copy-start.13 = (bf16[384,192]{0,1:T(8,128)(2,1)S(1)}, bf16[384,192]{0,1:T(8,128)(2,1)}, u32[]{:S(2)}) copy-start(bf16[384,192]{0,1:T(8,128)(2,1)} %param.25) | copy-start | bytes 442372
  34.2 3.6 %collective-permute-start.6 = (f32[80,256]{1,0:T(8,128)}, f32[80,256]{1,0:T(8,128)}, u32[]{:S(2)}, u32[]{:S(2)}) collective-permute-start(f32[80,256]{1,0:T(8,128)} %get-tuple-element.44), channel_id=1, source_target_pairs={{0,1},{1,0},{2,3},{3,2},{4,5},{5,4},{6,7},{7,6},{8,9},{9,8},{10,11... | collective-permute-start | bytes 245768 | tf_op jit(solution)/shard_map/ppermute | solution.py:629
  34.5 3.6 %collective-permute-start.7 = (f32[80,256]{1,0:T(8,128)}, f32[80,256]{1,0:T(8,128)}, u32[]{:S(2)}, u32[]{:S(2)}) collective-permute-start(f32[80,256]{1,0:T(8,128)} %get-tuple-element.44), channel_id=1, source_target_pairs={{0,2},{1,3},{2,0},{3,1},{4,6},{5,7},{6,4},{7,5},{8,10},{9,11},{10,... | collective-permute-start | bytes 245768 | tf_op jit(solution)/shard_map/ppermute | solution.py:629
  34.5 5.4 %collective-permute-start.8 = (f32[80,256]{1,0:T(8,128)}, f32[80,256]{1,0:T(8,128)}, u32[]{:S(2)}, u32[]{:S(2)}) collective-permute-start(f32[80,256]{1,0:T(8,128)} %get-tuple-element.44), channel_id=1, source_target_pairs={{0,3},{1,2},{2,1},{3,0},{4,7},{5,6},{6,5},{7,4},{8,11},{9,10},{10,... | collective-permute-start | bytes 245768 | tf_op jit(solution)/shard_map/ppermute | solution.py:629
  40.9 5.1 %collective-permute-start.10 = (f32[80,256]{1,0:T(8,128)S(1)}, f32[80,256]{1,0:T(8,128)S(1)}, u32[]{:S(2)}, u32[]{:S(2)}) collective-permute-start(f32[80,256]{1,0:T(8,128)S(1)} %add_add_fusion.1), channel_id=1, source_target_pairs={{4,0},{5,1},{14,2},{15,3},{8,4},{9,5},{2,6},{3,7},{12,8},{13,9},{6... | collective-permute-start | bytes 245768 | tf_op jit(solution)/shard_map/ppermute | solution.py:640
  41.5 6.4 %collective-permute-start.11 = (f32[80,256]{1,0:T(8,128)S(1)}, f32[80,256]{1,0:T(8,128)S(1)}, u32[]{:S(2)}, u32[]{:S(2)}) collective-permute-start(f32[80,256]{1,0:T(8,128)S(1)} %add_add_fusion.1), channel_id=1, source_target_pairs={{10,0},{11,1},{8,2},{9,3},{14,4},{15,5},{12,6},{13,7},{2,8},{3,9},... | collective-permute-start | bytes 245768 | tf_op jit(solution)/shard_map/ppermute | solution.py:640
  43.3 6.2 %collective-permute-start.9 = (f32[80,256]{1,0:T(8,128)S(1)}, f32[80,256]{1,0:T(8,128)S(1)}, u32[]{:S(2)}, u32[]{:S(2)}) collective-permute-start(f32[80,256]{1,0:T(8,128)S(1)} %add_add_fusion.1), channel_id=1, source_target_pairs={{14,0},{15,1},{4,2},{5,3},{2,4},{3,5},{8,6},{9,7},{6,8},{7,9},{12,... | collective-permute-start | bytes 245768 | tf_op jit(solution)/shard_map/ppermute | solution.py:640
  55.7 5.4 %collective-permute-start.12 = (f32[72,384]{1,0:T(8,128)S(1)}, f32[72,384]{1,0:T(8,128)S(1)}, u32[]{:S(2)}, u32[]{:S(2)}) collective-permute-start(f32[72,384]{1,0:T(8,128)S(1)} %get-tuple-element.45), channel_id=1, source_target_pairs={{0,1},{1,0},{2,3},{3,2},{4,5},{5,4},{6,7},{7,6},{8,9},{9,8},{10,11... | collective-permute-start | bytes 331784 | tf_op jit(solution)/shard_map/ppermute | solution.py:629
  61.2 6.8 %collective-permute-start.13 = (f32[160,384]{1,0:T(8,128)S(1)}, f32[160,384]{1,0:T(8,128)S(1)}, u32[]{:S(2)}, u32[]{:S(2)}) collective-permute-start(f32[160,384]{1,0:T(8,128)S(1)} %get-tuple-element.53), channel_id=1, source_target_pairs={{0,16},{16,0},{32,48},{48,32},{64,80},{80,64},{96,112},{112,96},{1... | collective-permute-start | bytes 737288 | tf_op jit(solution)/shard_map/ppermute | solution.py:629
  68.0 8.0 %collective-permute-start.14 = (f32[40,384]{1,0:T(8,128)S(1)}, f32[40,384]{1,0:T(8,128)S(1)}, u32[]{:S(2)}, u32[]{:S(2)}) collective-permute-start(f32[40,384]{1,0:T(8,128)S(1)} %get-tuple-element.77), channel_id=1, source_target_pairs={{0,64},{16,80},{32,96},{48,112},{64,0},{80,16},{96,32},{112,48},{1... | collective-permute-start | bytes 184328 | tf_op jit(solution)/shard_map/ppermute | solution.py:629
  69.4 6.6 %collective-permute-start.15 = (f32[40,384]{1,0:T(8,128)S(1)}, f32[40,384]{1,0:T(8,128)S(1)}, u32[]{:S(2)}, u32[]{:S(2)}) collective-permute-start(f32[40,384]{1,0:T(8,128)S(1)} %get-tuple-element.75), channel_id=1, source_target_pairs={{0,128},{16,144},{32,160},{48,176},{64,192},{80,208},{96,224},{112... | collective-permute-start | bytes 184328 | tf_op jit(solution)/shard_map/ppermute | solution.py:629
  72.0 4.3 %collective-permute-start.16 = (f32[40,384]{1,0:T(8,128)S(1)}, f32[40,384]{1,0:T(8,128)S(1)}, u32[]{:S(2)}, u32[]{:S(2)}) collective-permute-start(f32[40,384]{1,0:T(8,128)S(1)} %get-tuple-element.76), channel_id=1, source_target_pairs={{0,192},{16,208},{32,224},{48,240},{64,128},{80,144},{96,160},{112... | collective-permute-start | bytes 184328 | tf_op jit(solution)/shard_map/ppermute | solution.py:629
  72.1 4.3 %collective-permute-start.17 = (f32[72,384]{1,0:T(8,128)S(1)}, f32[72,384]{1,0:T(8,128)S(1)}, u32[]{:S(2)}, u32[]{:S(2)}) collective-permute-start(f32[72,384]{1,0:T(8,128)S(1)} %add.82), channel_id=1, source_target_pairs={{0,2},{1,3},{2,0},{3,1},{4,6},{5,7},{6,4},{7,5},{8,10},{9,11},{10,... | collective-permute-start | bytes 331784 | tf_op jit(solution)/shard_map/ppermute | solution.py:629
  76.4 7.6 %collective-permute-start.19 = (f32[72,384]{1,0:T(8,128)S(1)}, f32[72,384]{1,0:T(8,128)S(1)}, u32[]{:S(2)}, u32[]{:S(2)}) collective-permute-start(f32[72,384]{1,0:T(8,128)S(1)} %add.83), channel_id=1, source_target_pairs={{14,0},{15,1},{4,2},{5,3},{2,4},{3,5},{8,6},{9,7},{6,8},{7,9},{12,... | collective-permute-start | bytes 331784 | tf_op jit(solution)/shard_map/ppermute | solution.py:640
  79.3 4.6 %collective-permute-start.18 = (f32[40,384]{1,0:T(8,128)S(1)}, f32[40,384]{1,0:T(8,128)S(1)}, u32[]{:S(2)}, u32[]{:S(2)}) collective-permute-start(f32[40,384]{1,0:T(8,128)S(1)} %add_add_fusion.2), channel_id=1, source_target_pairs={{0,32},{16,48},{32,0},{48,16},{64,96},{80,112},{96,64},{112,80},{1... | collective-permute-start | bytes 184328 | tf_op jit(solution)/shard_map/ppermute | solution.py:629
  83.9 5.7 %collective-permute-start.20 = (f32[40,384]{1,0:T(8,128)S(1)}, f32[40,384]{1,0:T(8,128)S(1)}, u32[]{:S(2)}, u32[]{:S(2)}) collective-permute-start(f32[40,384]{1,0:T(8,128)S(1)} %add.85), channel_id=1, source_target_pairs={{0,64},{16,80},{32,96},{48,112},{64,0},{80,16},{96,32},{112,48},{1... | collective-permute-start | bytes 184328 | tf_op jit(solution)/shard_map/ppermute | solution.py:629
  84.0 5.7 %collective-permute-start.21 = (f32[40,384]{1,0:T(8,128)S(1)}, f32[40,384]{1,0:T(8,128)S(1)}, u32[]{:S(2)}, u32[]{:S(2)}) collective-permute-start(f32[40,384]{1,0:T(8,128)S(1)} %add.85), channel_id=1, source_target_pairs={{0,128},{16,144},{32,160},{48,176},{64,192},{80,208},{96,224},{112... | collective-permute-start | bytes 184328 | tf_op jit(solution)/shard_map/ppermute | solution.py:629
  87.5 4.3 %collective-permute-start.22 = (f32[40,384]{1,0:T(8,128)S(1)}, f32[40,384]{1,0:T(8,128)S(1)}, u32[]{:S(2)}, u32[]{:S(2)}) collective-permute-start(f32[40,384]{1,0:T(8,128)S(1)} %add.85), channel_id=1, source_target_pairs={{0,192},{16,208},{32,224},{48,240},{64,128},{80,144},{96,160},{112... | collective-permute-start | bytes 184328 | tf_op jit(solution)/shard_map/ppermute | solution.py:629
  87.9 6.2 %collective-permute-start.23 = (f32[72,384]{1,0:T(8,128)S(1)}, f32[72,384]{1,0:T(8,128)S(1)}, u32[]{:S(2)}, u32[]{:S(2)}) collective-permute-start(f32[72,384]{1,0:T(8,128)S(1)} %add.84.q0_ref), channel_id=1, source_target_pairs={{6,0},{7,1},{12,2},{13,3},{10,4},{11,5},{0,6},{1,7},{14,8},{15,9},... | collective-permute-start | bytes 331784 | tf_op jit(solution)/shard_map/ppermute | solution.py:640
  94.2 6.1 %collective-permute-start.24 = (f32[160,384]{1,0:T(8,128)S(1)}, f32[160,384]{1,0:T(8,128)S(1)}, u32[]{:S(2)}, u32[]{:S(2)}) collective-permute-start(f32[160,384]{1,0:T(8,128)S(1)} %pad_maximum_fusion.mine_ref), channel_id=1, source_target_pairs={{0,16},{16,0},{32,48},{48,32},{64,80},{80,64},{96,112},{112,96},{1... | collective-permute-start | bytes 737288 | tf_op jit(solution)/shard_map/ppermute | solution.py:629
  (12 other events, 148.2 us)
